TPU v7x, 32 devices: a whole 2x2x4 slice. The times are simulated.
32 devices in a mesh: spec: 2 (over x), tm: 16 (over z, y, core).
Axes of the slice: x: 2, y: 2, z: 4, core: 2. Of those that a mesh axis runs over, the one named last changes fastest.
Arguments:
- series: bfloat16 [64, 32768], P(None, ('spec', 'tm')), parts along dimension 1, may hold values from -8 to 8
- loadings: bfloat16 [32768, 256], P('spec'), parts along dimension 0, may hold values from -0.046875 to 0.046875
- precision: float32 [32768], P('spec'), parts along dimension 0, may hold values from 0.5 to 4
- start_day: int32 [32768], P('spec'), parts along dimension 0, may hold values from 0 to 15
- stop_day: int32 [32768], P('spec'), parts along dimension 0, may hold values from 49 to 64
- off_day: int32 [32768], P('spec'), parts along dimension 0, may hold values from 0 to 6
- decay: float32 [256], replicated, may hold values from 0 to 1
- gain: bfloat16 [256, 256], replicated, may hold values from -1 to 1
- smoother: float32 [256, 256], replicated, may hold values from -1 to 1
Outputs:
- smoothed: float32 [64, 512], P('tm', 'spec'), parts along dimension 1
- scores: bfloat16 [64, 32768], P(None, ('spec', 'tm')), parts along dimension 1
There are 2 independent parts, one for each index of `spec`. A program takes and returns all parts, laid end to end along the dimension named above; an argument that names none is the same for every part. Nothing has to cross between parts.
All inputs are finite; a program needn't handle non-finite values.
Results may differ from a plain program's by a relative error of at most 0.002.
The roundings to bfloat16 on the way count: a program that leaves them out, or rounds other values in their place, can miss the bound.
Values may be sent and summed in bfloat16 or wider, within the bound.
No kernel may reach another device: no remote copies, remote signals or barrier semaphores. Data moves between devices by JAX's collectives and lax.ppermute only.
A program may use at most 192 MiB of HBM per device.

v0:
```python
import jax
import jax.numpy as jnp
from jax import lax
from jax.sharding import PartitionSpec as P


def prefix(part, axis, combine, identity, reverse):
    count = lax.axis_size(axis)
    place = lax.axis_index(axis)
    ahead = count - 1 - place if reverse else place
    gathered = jax.tree.map(lambda a: lax.all_gather(a, axis), part)
    state = jax.tree.map(lambda a, e: jnp.zeros_like(a) + jnp.asarray(e, a.dtype), part, identity)

    def one(turn, state):
        source = count - 1 - turn if reverse else turn
        return combine(
            state, jax.tree.map(lambda a: lax.dynamic_index_in_dim(a, source, 0, False), gathered)
        )

    return lax.fori_loop(0, ahead, one, state)


def activity(day_ids, start_day, stop_day, off_day):
    return (
        (day_ids[:, None] >= start_day[None, :])
        & (day_ids[:, None] < stop_day[None, :])
        & (day_ids[:, None] % 7 != off_day[None, :])
    ).astype(jnp.float32)


def compose(earlier, later):
    high = lax.Precision.HIGHEST
    return (
        jnp.dot(later[0], earlier[0], precision=high),
        jnp.dot(later[0], earlier[1], precision=high) + later[1],
    )


def local(series, loadings, precision, start_day, stop_day, off_day, decay, gain, smoother):
    high = lax.Precision.HIGHEST
    blocks = lax.axis_size("tm")
    block_index = lax.axis_index("tm")
    factor_count = loadings.shape[1]
    gathered = lax.all_to_all(series, "tm", split_axis=0, concat_axis=1, tiled=True)
    day_count = gathered.shape[0]
    day_ids = block_index * day_count + jnp.arange(day_count, dtype=jnp.int32)
    active = activity(day_ids, start_day, stop_day, off_day)
    weights = active * precision[None, :]

    def information_of(weight_row):
        scaled = (weight_row[:, None] * loadings).astype(jnp.bfloat16)
        return lax.dot_general(
            loadings, scaled, (((0,), (0,)), ((), ())), preferred_element_type=jnp.float32
        )

    information = lax.map(information_of, weights)
    weighted = (weights * gathered.astype(jnp.float32)).astype(jnp.bfloat16)
    drive_terms = jnp.dot(weighted, loadings, preferred_element_type=jnp.float32)
    damped = (information * decay[None, None, :]).astype(jnp.bfloat16)
    transitions = jnp.diag(decay)[None, :, :] - jnp.einsum(
        "ij,djk->dik", gain, damped, preferred_element_type=jnp.float32
    )
    offsets = jnp.dot(drive_terms, gain.astype(jnp.float32).T, precision=high)
    identity_matrix = jnp.eye(factor_count, dtype=jnp.float32)
    zero_vector = jnp.zeros((factor_count,), jnp.float32)

    def fold_day(carried, day_item):
        step_matrix, step_offset = day_item
        return (compose(carried, (step_matrix, step_offset)), None)

    block_element = lax.scan(fold_day, (identity_matrix, zero_vector), (transitions, offsets))[0]
    entering = prefix(block_element, "tm", compose, (identity_matrix, zero_vector), False)[1]

    def advance(carried, day_item):
        step_matrix, step_offset = day_item
        updated = jnp.dot(step_matrix, carried, precision=high) + step_offset
        return (updated, updated)

    filtered = lax.scan(advance, entering, (transitions, offsets))[1]
    pulled = jnp.dot(filtered * decay[None, :], smoother.T, precision=high)
    final_day = (day_ids == blocks * day_count - 1)[:, None]
    back_term = jnp.where(final_day, filtered, filtered - pulled)

    def retreat(carried, term_row):
        updated = jnp.dot(smoother, carried, precision=high) + term_row
        return (updated, updated)

    local_tail = lax.scan(retreat, zero_vector, back_term, reverse=True)[1][0]

    def raise_once(turn, product):
        return jnp.dot(smoother, product, precision=high)

    step_power = lax.fori_loop(0, day_count, raise_once, identity_matrix)
    beyond = prefix((step_power, local_tail), "tm", compose, (identity_matrix, zero_vector), True)[
        1
    ]
    smoothed = lax.scan(retreat, beyond, back_term, reverse=True)[1]
    rounded = smoothed.astype(jnp.bfloat16)
    fitted = lax.dot_general(
        rounded, loadings, (((1,), (1,)), ((), ())), preferred_element_type=jnp.float32
    )
    local_scores = (
        active * (gathered.astype(jnp.float32) - fitted) * jnp.sqrt(precision)[None, :]
    ).astype(jnp.bfloat16)
    scores = lax.all_to_all(local_scores, "tm", split_axis=1, concat_axis=0, tiled=True)
    return (smoothed, scores)


def solution(mesh):
    in_specs = (
        P(None, ("spec", "tm")),
        P("spec", None),
        P("spec"),
        P("spec"),
        P("spec"),
        P("spec"),
        P(),
        P(),
        P(),
    )
    out_specs = (P("tm", "spec"), P(None, ("spec", "tm")))
    return jax.shard_map(local, mesh=mesh, in_specs=in_specs, out_specs=out_specs, check_vma=False)
```

profile of v0, /device:TPU:0, one launch (start us, length us, event | category | flops | bytes accessed | tf_op | source)
XLA Modules:
  0.0 229.0 jit_solution(11653354949137619354)
XLA Ops:
  7.2 1.7 all_to_all.24
  8.8 7.4 %all-to-all-start = ((bf16[16,4,1024]{2,1,0:T(4,128)(2,1)}), bf16[16,4,1024]{2,1,0:T(4,128)(2,1)S(1)}, u32[]{:S(2)}, u32[]{:S(2)}) async-start(bf16[16,4,1024]{2,1,0:T(4,128)(2,1)} %all_to_all.24), calls=%async_computation | async-start | bytes 262144 | tf_op jit(solution)/shard_map/all_to_all | solution.py:44
  16.3 1.2 broadcast_select_fusion.2
  17.5 52.9 %while.105 = (s32[]{:T(128)}, f32[4,256,256]{1,2,0:T(8,128)S(1)}, f32[4,16384]{1,0:T(4,128)S(1)}, bf16[16384,256]{1,0:T(8,128)(2,1)}, s32[]{:T(128)}) while((s32[]{:T(128)}, f32[4,256,256]{1,2,0:T(8,128)S(1)}, f32[4,16384]{1,0:T(4,128)S(1)}, bf16[16384,256]{1,0:T(8,128)(2,1)}, s32[]{:T(128)}) %tuple.176), condition=%wide.region_3.4_spmd, body=%wide.region_2.3_spmd.sunk | while | flops 2160066560 | bytes 17236544 | solution.py:56
  17.6 13.1 %fusion.89 = f32[4,256,256]{1,2,0:T(8,128)S(1)} fusion(f32[4,256,256]{1,2,0:T(8,128)S(1)} %get-tuple-element.823, s32[]{:T(128)} %get-tuple-element.822, bf16[16384,256]{1,0:T(8,128)(2,1)} %get-tuple-element.830, f32[16384]{0:T(1024)S(1)} %bitcast.164), kind=kOutput, calls=%fused_computation.4.clone.1 | convolution fusion | flops 2160066560 | bytes 17105408 | tf_op jit(solution)/shard_map/while/body/eval_jaxpr/dot_general | solution.py:52
  30.8 13.1 %fusion.89 = f32[4,256,256]{1,2,0:T(8,128)S(1)} fusion(f32[4,256,256]{1,2,0:T(8,128)S(1)} %get-tuple-element.823, s32[]{:T(128)} %get-tuple-element.822, bf16[16384,256]{1,0:T(8,128)(2,1)} %get-tuple-element.830, f32[16384]{0:T(1024)S(1)} %bitcast.164), kind=kOutput, calls=%fused_computation.4.clone.1 | convolution fusion | flops 2160066560 | bytes 17105408 | tf_op jit(solution)/shard_map/while/body/eval_jaxpr/dot_general | solution.py:52
  44.0 13.1 %fusion.89 = f32[4,256,256]{1,2,0:T(8,128)S(1)} fusion(f32[4,256,256]{1,2,0:T(8,128)S(1)} %get-tuple-element.823, s32[]{:T(128)} %get-tuple-element.822, bf16[16384,256]{1,0:T(8,128)(2,1)} %get-tuple-element.830, f32[16384]{0:T(1024)S(1)} %bitcast.164), kind=kOutput, calls=%fused_computation.4.clone.1 | convolution fusion | flops 2160066560 | bytes 17105408 | tf_op jit(solution)/shard_map/while/body/eval_jaxpr/dot_general | solution.py:52
  57.2 13.1 %fusion.89 = f32[4,256,256]{1,2,0:T(8,128)S(1)} fusion(f32[4,256,256]{1,2,0:T(8,128)S(1)} %get-tuple-element.823, s32[]{:T(128)} %get-tuple-element.822, bf16[16384,256]{1,0:T(8,128)(2,1)} %get-tuple-element.830, f32[16384]{0:T(1024)S(1)} %bitcast.164), kind=kOutput, calls=%fused_computation.4.clone.1 | convolution fusion | flops 2160066560 | bytes 17105408 | tf_op jit(solution)/shard_map/while/body/eval_jaxpr/dot_general | solution.py:52
  70.6 0.3 fusion.27
  71.4 4.6 %fusion.32 = f32[4,256]{1,0:T(4,128)S(1)} fusion(bf16[16384,256]{1,0:T(8,128)(2,1)} %get-tuple-element.977, f32[4,16384]{1,0:T(4,128)S(1)} %bitcast.162, pred[4,16384]{1,0:T(4,128)(4,1)S(1)} %get-tuple-element.570, f32[16384]{0:T(1024)S(1)} %copy-done.4), kind=kOutput, calls=%fused_computation.49 | convolution fusion | flops 33751040 | bytes 8785920 | tf_op jit(solution)/shard_map/dot_general | solution.py:58
  76.2 3.3 %while.110 = (s32[]{:T(128)}, f32[256,256]{1,0:T(8,128)S(1)}, f32[256]{0:T(256)S(1)}, f32[4,256,256]{2,1,0:T(8,128)S(1)}, f32[4,256]{1,0:T(4,128)S(1)}, /*index=5*/s32[]{:T(128)}, s32[]{:T(128)}) while((s32[]{:T(128)}, f32[256,256]{1,0:T(8,128)S(1)}, f32[256]{0:T(256)S(1)}, f32[4,256,256]{2,1,0:T(8,128)S(1)}, ...), condition=%wide.region_5.6_spmd.clone, body=%wide.region_4.5_spmd.clone.sunk | while | flops 202113536 | bytes 1582179 | solution.py:71
  76.7 0.4 fusion.106
  77.5 0.4 fusion.106
  78.3 0.4 fusion.106
  79.1 0.4 fusion.106
  79.5 0.7 copy-done.3
  80.3 1.7 while.104
  80.4 0.4 fusion.87
  80.8 0.4 fusion.87
  81.2 0.4 fusion.87
  81.7 0.4 fusion.87
  82.1 0.7 copy-done.2
  82.8 21.7 %all-gather.3 = f32[16,1,256]{2,1,0:T(1,128)S(1)} all-gather(f32[1,1,256]{2,1,0:T(1,128)S(1)} %bitcast.190), channel_id=4, replica_groups=mesh['spec'=2,'tm'=16] {'tm'}, dimensions={0}, use_global_device_ids=true | all-gather | bytes 17408 | tf_op jit(solution)/shard_map/all_gather | solution.py:11
  104.6 27.8 %all-gather.10.cloned.1.call-done = f32[4096,256]{1,0:T(8,128)} async-done(((f32[256,256]{1,0:T(8,128)}), f32[4096,256]{1,0:T(8,128)}) %all-gather.10.cloned.1.call-update) | async-done | bytes 4194320 | tf_op jit(solution)/shard_map/all_gather | solution.py:11
  132.3 1.6 while.107
  134.3 1.6 while.111
  135.9 37.6 %all-gather.4 = f32[16,1,256]{2,1,0:T(1,128)S(1)} all-gather(f32[1,1,256]{2,1,0:T(1,128)S(1)} %slice_bitcast_fusion), channel_id=1, replica_groups=mesh['spec'=2,'tm'=16] {'tm'}, dimensions={0}, use_global_device_ids=true | all-gather | bytes 17408 | tf_op jit(solution)/shard_map/all_gather | solution.py:11
  173.5 10.3 %all-gather.8.cloned.1.call-done = f32[4096,256]{1,0:T(8,128)} async-done(((f32[256,256]{1,0:T(8,128)}), f32[4096,256]{1,0:T(8,128)}) %all-gather.8.cloned.1.call-update) | async-done | bytes 4194320 | tf_op jit(solution)/shard_map/all_gather | solution.py:11
  183.8 19.9 %while.108 = (s32[]{:T(128)}, f32[256]{0:T(256)S(1)}, s32[]{:T(128)}, f32[16,256,256]{2,1,0:T(8,128)}, f32[16,256]{1,0:T(8,128)S(1)}, /*index=5*/s32[]{:T(128)}, s32[]{:T(128)}, s32[]{:T(128)}, s32[]{:T(128)}) while((s32[]{:T(128)}, f32[256]{0:T(256)S(1)}, s32[]{:T(128)}, f32[16,256,256]{2,1,0:T(8,128)}, f32[16,256]{1,0:T(8,128)S(1)}, ...), condition=%wide.region_13.14_spmd, body=%wide.region_12.13_spmd.sunk | while | flops 786694 | bytes 269459 | solution.py:20
  183.8 1.2 fusion.98
  185.1 1.2 fusion.98
  186.4 1.2 fusion.98
  187.8 1.2 fusion.98
  189.1 1.2 fusion.98
  190.4 1.2 fusion.98
  191.8 1.2 fusion.98
  193.1 1.2 fusion.98
  194.4 1.2 fusion.98
  195.7 1.2 fusion.98
  197.1 1.2 fusion.98
  198.4 1.2 fusion.98
  199.7 1.2 fusion.98
  201.1 1.2 fusion.98
  202.4 1.2 fusion.98
  203.7 1.6 while.109
  205.3 5.7 %fusion.26 = bf16[4,16384]{1,0:T(4,128)(2,1)S(1)} fusion(pred[4,16384]{1,0:T(4,128)(4,1)S(1)} %get-tuple-element.570, f32[4,16384]{1,0:T(4,128)S(1)} %bitcast.163, bf16[16384,256]{1,0:T(8,128)(2,1)} %get-tuple-element.977, f32[16384]{0:T(1024)S(1)} %sqrt.3, f32[4,256]{1,0:T(4,128)S(1)} %get-tuple-element.428), kind=kOutput, calls=%fused_computation.37 | convolution fusion | flops 33817600 | bytes 8916992 | tf_op jit(solution)/shard_map/dot_general | solution.py:99
  210.9 10.5 %all_to_all.32 = bf16[4,16,1024]{2,0,1:T(4,128)(2,1)S(1)} all-to-all(bf16[4,16,1024]{2,0,1:T(4,128)(2,1)S(1)} %bitcast.165), channel_id=1, replica_groups=mesh['spec'=2,'tm'=16] {'tm'}, dimensions={1} | all-to-all | bytes 262144 | tf_op jit(solution)/shard_map/all_to_all | solution.py:105
  221.5 0.7 all_to_all.29
  (150 shorter events, 8.6 us)
Async XLA Ops:
  7.2 63.5 %copy-start = (bf16[256,256]{1,0:T(8,128)(2,1)S(1)}, bf16[256,256]{1,0:T(8,128)(2,1)}, u32[]{:S(2)}) copy-start(bf16[256,256]{1,0:T(8,128)(2,1)} %param.32) | copy-start | bytes 393220
  8.8 62.6 %all-to-all-start = ((bf16[16,4,1024]{2,1,0:T(4,128)(2,1)}), bf16[16,4,1024]{2,1,0:T(4,128)(2,1)S(1)}, u32[]{:S(2)}, u32[]{:S(2)}) async-start(bf16[16,4,1024]{2,1,0:T(4,128)(2,1)} %all_to_all.24), calls=%async_computation | async-start | bytes 262144 | tf_op jit(solution)/shard_map/all_to_all | solution.py:44
  16.2 116.1 %all-gather.10.cloned.1.call-start = ((), (), s32[]{:S(2)}) async-start(), calls=%async_computation.3 | async-start | bytes 4456448 | tf_op jit(solution)/shard_map/all_gather | solution.py:11
  17.5 52.9 %copy-start.6 = (f32[256]{0:T(256)S(1)}, f32[256]{0:T(256)}, u32[]{:S(2)}) copy-start(f32[256]{0:T(256)} %param.31) | copy-start | bytes 3076
  17.5 53.9 %copy-start.4 = (f32[16384]{0:T(1024)S(1)}, f32[16384]{0:T(1024)}, u32[]{:S(2)}) copy-start(f32[16384]{0:T(1024)} %param.27) | copy-start | bytes 196612
  71.4 8.9 %copy-start.1 = (f32[256,256]{1,0:T(8,128)S(1)}, f32[256,256]{1,0:T(8,128)}, u32[]{:S(2)}) copy-start(f32[256,256]{1,0:T(8,128)} %param.33) | copy-start | bytes 786436
  79.5 0.7 copy-start.3
  80.3 103.5 %all-gather.8.cloned.1.call-start = ((), (), s32[]{:S(2)}) async-start(), calls=%async_computation.2 | async-start | bytes 4456448 | tf_op jit(solution)/shard_map/all_gather | solution.py:11
  82.0 0.7 copy-start.2
  205.3 16.9 %copy-start.5 = (f32[4,256]{1,0:T(4,128)}, f32[4,256]{1,0:T(4,128)S(1)}, u32[]{:S(2)}) copy-start(f32[4,256]{1,0:T(4,128)S(1)} %get-tuple-element.428) | copy-start | bytes 12292
Sparse Core Ops, SparseCore 0:
  80.4 51.8 all-gather.9
  134.5 49.2 all-gather.7
where the time goes:
time: 230 us; the launch traced here: 229 us
  matrix products  89.4 us (39%)
  blocking collectives  69.9 us (30%)
  waiting for transfers between devices  38.1 us (17%)
  between operations  14.3 us (6%)
  starting transfers between devices  7.47 us (3%)
  local copies, waits for them, and re-layouts  7 us (3%)
    all_gather x2, blocking collectives, prefix(): gathered = jax.tree.map(lambda a: lax.all_gather(a, axis), part)  59.3 us
    dot_general x4, matrix products, information_of(): lax.dot_general(loadings, scaled, (((0,), (0,)), ((), ())), preferred_ele...  52.5 us
    all_gather x2, waiting for transfers between devices, prefix(): gathered = jax.tree.map(lambda a: lax.all_gather(a, axis), part)  38 us
    dot_general x19, matrix products, compose(): jnp.dot(later[0], earlier[1], precision=high) + later[1]  19.5 us
    all_to_all x1, blocking collectives, local(): lax.all_to_all(local_scores, 'tm', split_axis=1, concat_axis=0, tiled=True)  10.5 us
    all_to_all x1, starting transfers between devices, local(): lax.all_to_all(series, 'tm', split_axis=0, concat_axis=1, tiled=True)  7.39 us
    dot_general x1, matrix products, local(): lax.dot_general(rounded, loadings, (((1,), (1,)), ((), ())), preferred_el...  5.65 us
    dot_general x1, matrix products, local(): jnp.dot(weighted, loadings, preferred_element_type=jnp.float32)  4.61 us
  transfers between devices with their start and end apart: 3, of which 2 were waited for; matrix products, arithmetic and copies ran while one was open for 26% of the time, Pallas kernels for 0%

commit v1 on v0

v1 whole, which is shorter than its diff:
```python
import functools
import jax
import jax.numpy as jnp
from jax import lax
from jax.experimental import pallas as pl
from jax.experimental.pallas import tpu as pltpu
from jax.sharding import PartitionSpec as P

F32 = jnp.float32
BF16 = jnp.bfloat16
HIGH = lax.Precision.HIGHEST
VMEM = pltpu.MemorySpace.VMEM
SMEM = pltpu.MemorySpace.SMEM


def params(grid=True):
    semantics = {"dimension_semantics": ("arbitrary",)} if grid else {}
    return pltpu.CompilerParams(vmem_limit_bytes=48 << 20, **semantics)


def cost(flops, nbytes):
    return pl.CostEstimate(flops=flops, bytes_accessed=nbytes, transcendentals=0)


def whole(count):
    return [pl.BlockSpec(memory_space=VMEM)] * count


def exact(a, b):
    return jnp.dot(a, b, precision=HIGH, preferred_element_type=F32)


def partial_drive(index, series, loadings, precision, start, stop, off):
    days, own = series.shape
    factors = loadings.shape[1]

    def kernel(index_ref, series_ref, load_ref, prec_ref, start_ref, stop_ref, off_ref, out_ref):
        day = lax.broadcasted_iota(jnp.int32, (days, 1), 0)
        active = (
            (day >= start_ref[...]) & (day < stop_ref[...]) & (lax.rem(day, 7) != off_ref[...])
        )
        weights = jnp.where(active, prec_ref[...], 0.0)
        weighted = (weights * series_ref[...].astype(F32)).astype(BF16)
        out_ref[...] = jnp.dot(weighted, load_ref[...], preferred_element_type=F32)

    row = pl.BlockSpec((1, own), lambda i, s: (0, s[0]))
    return pl.pallas_call(
        kernel,
        grid_spec=pltpu.PrefetchScalarGridSpec(
            num_scalar_prefetch=1,
            grid=(1,),
            in_specs=[
                pl.BlockSpec((days, own), lambda i, s: (0, 0)),
                pl.BlockSpec((own, factors), lambda i, s: (s[0], 0)),
                row,
                row,
                row,
                row,
            ],
            out_specs=pl.BlockSpec((days, factors), lambda i, s: (0, 0)),
        ),
        out_shape=jax.ShapeDtypeStruct((days, factors), F32),
        compiler_params=params(),
        cost_estimate=cost(2 * days * own * factors, 1 << 20),
        name="partial_drive",
    )(index, series, loadings, precision, start, stop, off)


def transitions_of(first_day, day_count, loadings, precision, start, stop, off, decay, gain):
    providers, factors = loadings.shape
    chunk = min(4096, providers)
    steps = providers // chunk

    def kernel(
        day_ref, load_ref, prec_ref, start_ref, stop_ref, off_ref, row_ref, col_ref, gain_ref,
        step_ref, run_ref, acc,
    ):
        step = pl.program_id(0)

        @pl.when(step == 0)
        def _():
            acc[...] = jnp.zeros_like(acc)

        block = load_ref[...]
        scaled = (block.T.astype(F32) * prec_ref[...]).astype(BF16)
        for d in range(day_count):
            day = day_ref[0] + d
            active = (
                (start_ref[...] <= day) & (stop_ref[...] > day) & (off_ref[...] != lax.rem(day, 7))
            )
            mask = active.astype(F32).astype(BF16)
            acc[d] += jnp.dot(scaled * mask, block, preferred_element_type=F32)

        @pl.when(step == steps - 1)
        def _():
            shape = (factors, factors)
            diagonal = jnp.where(
                lax.broadcasted_iota(jnp.int32, shape, 0) == lax.broadcasted_iota(jnp.int32, shape, 1),
                row_ref[...],
                0.0,
            )
            for d in range(day_count):
                damped = (acc[d] * col_ref[...]).astype(BF16)
                pulled = lax.dot_general(
                    damped, gain_ref[...], (((1,), (1,)), ((), ())), preferred_element_type=F32
                )
                step_ref[d] = diagonal - pulled
            run_ref[0] = step_ref[0]
            for d in range(1, day_count):
                run_ref[d] = exact(run_ref[d - 1], step_ref[d])

    row = pl.BlockSpec((1, chunk), lambda i: (0, i))
    cube = pl.BlockSpec((day_count, factors, factors), lambda i: (0, 0, 0))
    shape = jax.ShapeDtypeStruct((day_count, factors, factors), F32)
    return pl.pallas_call(
        kernel,
        grid=(steps,),
        in_specs=[
            pl.BlockSpec(memory_space=SMEM),
            pl.BlockSpec((chunk, factors), lambda i: (i, 0)),
            row,
            row,
            row,
            row,
            pl.BlockSpec((1, factors), lambda i: (0, 0)),
            pl.BlockSpec((factors, 1), lambda i: (0, 0)),
            pl.BlockSpec((factors, factors), lambda i: (0, 0)),
        ],
        out_specs=[cube, cube],
        out_shape=[shape, shape],
        scratch_shapes=[pltpu.VMEM((day_count, factors, factors), F32)],
        compiler_params=params(),
        cost_estimate=cost(2 * day_count * providers * factors * factors, 10 << 20),
        name="transitions",
    )(
        first_day, loadings, precision, start, stop, off,
        decay.reshape(1, factors), decay.reshape(factors, 1), gain,
    )


def own_states(terms, steps, gain):
    parts, day_count, factors = terms.shape

    def kernel(terms_ref, step_ref, gain_ref, out_ref):
        drive = terms_ref[0]
        for p in range(1, parts):
            drive = drive + terms_ref[p]
        offsets = lax.dot_general(
            drive, gain_ref[...].astype(F32), (((1,), (1,)), ((), ())), precision=HIGH,
            preferred_element_type=F32,
        )
        state = offsets[0:1]
        out_ref[0:1] = state
        for d in range(1, day_count):
            state = exact(state, step_ref[d]) + offsets[d : d + 1]
            out_ref[d : d + 1] = state

    return pl.pallas_call(
        kernel,
        in_specs=whole(3),
        out_specs=pl.BlockSpec(memory_space=VMEM),
        out_shape=jax.ShapeDtypeStruct((day_count, factors), F32),
        compiler_params=params(False),
        cost_estimate=cost(20 * factors * factors * 8, 1 << 20),
        name="own_states",
    )(terms, steps, gain)


def combined(upper, mine, my_tail, other, other_tail):
    factors = mine.shape[0]

    def kernel(upper_ref, mine_ref, my_ref, other_ref, other_tail_ref, map_ref, tail_ref):
        def write(low, low_tail, high, high_tail):
            map_ref[...] = exact(low[...], high[...])
            tail_ref[...] = exact(low_tail[...], high[...]) + high_tail[...]

        @pl.when(upper_ref[0] == 1)
        def _():
            write(other_ref, other_tail_ref, mine_ref, my_ref)

        @pl.when(upper_ref[0] == 0)
        def _():
            write(mine_ref, my_ref, other_ref, other_tail_ref)

    return pl.pallas_call(
        kernel,
        in_specs=[pl.BlockSpec(memory_space=SMEM)] + whole(4),
        out_specs=whole(2),
        out_shape=[
            jax.ShapeDtypeStruct((factors, factors), F32),
            jax.ShapeDtypeStruct((1, factors), F32),
        ],
        compiler_params=params(False),
        cost_estimate=cost(12 * factors**3, 1 << 20),
        name="combined",
    )(upper, mine, my_tail, other, other_tail)


def advanced(state, matrix, tail):
    factors = matrix.shape[0]

    def kernel(state_ref, matrix_ref, tail_ref, out_ref):
        out_ref[...] = exact(state_ref[...], matrix_ref[...]) + tail_ref[...]

    return pl.pallas_call(
        kernel,
        in_specs=whole(3),
        out_specs=pl.BlockSpec(memory_space=VMEM),
        out_shape=jax.ShapeDtypeStruct((1, factors), F32),
        compiler_params=params(False),
        cost_estimate=cost(12 * factors**2, 1 << 18),
        name="advanced",
    )(state, matrix, tail)


def filtered_of(entering, uppers, levels, running, states):
    day_count, factors = states.shape
    count = len(levels)

    def kernel(upper_ref, enter_ref, *refs):
        out_ref = refs[-1]
        states_ref, run_ref = refs[-2], refs[-3]
        state = enter_ref[...]
        for level in reversed(range(count)):
            matrix_ref, tail_ref = refs[2 * level], refs[2 * level + 1]
            moved = exact(state, matrix_ref[...]) + tail_ref[...]
            state = jnp.where(upper_ref[level] == 1, moved, state)
        for d in range(day_count):
            out_ref[d : d + 1] = exact(state, run_ref[d]) + states_ref[d : d + 1]

    flat = [a for level in levels for a in level]
    return pl.pallas_call(
        kernel,
        in_specs=[pl.BlockSpec(memory_space=SMEM)] + whole(len(flat) + 3),
        out_specs=pl.BlockSpec(memory_space=VMEM),
        out_shape=jax.ShapeDtypeStruct((day_count, factors), F32),
        compiler_params=params(False),
        cost_estimate=cost(80 * factors**2, 2 << 20),
        name="filtered",
    )(uppers, entering, *flat, running, states)


POWERS = 5


def smoother_powers(smoother):
    factors = smoother.shape[0]

    def kernel(in_ref, out_ref):
        out_ref[0] = in_ref[...].T
        for p in range(1, POWERS):
            out_ref[p] = exact(out_ref[p - 1], out_ref[p - 1])

    return pl.pallas_call(
        kernel,
        in_specs=whole(1),
        out_specs=pl.BlockSpec(memory_space=VMEM),
        out_shape=jax.ShapeDtypeStruct((POWERS, factors, factors), F32),
        compiler_params=params(False),
        cost_estimate=cost(48 * factors**3, 2 << 20),
        name="smoother_powers",
    )(smoother)


def finish(index, day_count, filtered, powers, decay, series, loadings, precision, start, stop, off):
    days, own = series.shape
    factors = loadings.shape[1]
    stride = 2 ** (POWERS - 1)

    def kernel(
        index_ref, filt_ref, pow_ref, decay_ref, series_ref, load_ref, prec_ref, start_ref,
        stop_ref, off_ref, smooth_ref, score_ref, work,
    ):
        filtered = filt_ref[...]
        day = lax.broadcasted_iota(jnp.int32, (days, 1), 0)
        pulled = exact(filtered * decay_ref[...], pow_ref[0])
        total = jnp.where(day == days - 1, filtered, filtered - pulled)
        for p in range(POWERS - 1):
            reach = 2**p
            later = jnp.concatenate([total[reach:], jnp.zeros((reach, factors), F32)], 0)
            total = total + exact(later, pow_ref[p])
        blocks = days // stride
        block = total[(blocks - 1) * stride :]
        work[(blocks - 1) * stride :, :] = block
        for b in reversed(range(blocks - 1)):
            block = total[b * stride : (b + 1) * stride] + exact(block, pow_ref[POWERS - 1])
            work[b * stride : (b + 1) * stride, :] = block
        mine = index_ref[0] * day_count
        for d in range(day_count):
            smooth_ref[d : d + 1, :] = work[pl.ds(mine + d, 1), :]
        fitted = lax.dot_general(
            work[...].astype(BF16), load_ref[...], (((1,), (1,)), ((), ())),
            preferred_element_type=F32,
        )
        active = (
            (day >= start_ref[...]) & (day < stop_ref[...]) & (lax.rem(day, 7) != off_ref[...])
        )
        residual = (series_ref[...].astype(F32) - fitted) * jnp.sqrt(prec_ref[...])
        score_ref[...] = jnp.where(active, residual, 0.0).astype(BF16)

    row = pl.BlockSpec((1, own), lambda i, s: (0, s[0]))
    return pl.pallas_call(
        kernel,
        grid_spec=pltpu.PrefetchScalarGridSpec(
            num_scalar_prefetch=1,
            grid=(1,),
            in_specs=[
                pl.BlockSpec((days, factors), lambda i, s: (0, 0)),
                pl.BlockSpec((POWERS, factors, factors), lambda i, s: (0, 0, 0)),
                pl.BlockSpec((1, factors), lambda i, s: (0, 0)),
                pl.BlockSpec((days, own), lambda i, s: (0, 0)),
                pl.BlockSpec((own, factors), lambda i, s: (s[0], 0)),
                row,
                row,
                row,
                row,
            ],
            out_specs=[
                pl.BlockSpec((day_count, factors), lambda i, s: (0, 0)),
                pl.BlockSpec((days, own), lambda i, s: (0, 0)),
            ],
            scratch_shapes=[pltpu.VMEM((days, factors), F32)],
        ),
        out_shape=[
            jax.ShapeDtypeStruct((day_count, factors), F32),
            jax.ShapeDtypeStruct((days, own), BF16),
        ],
        compiler_params=params(),
        cost_estimate=cost(2 * days * own * factors, 2 << 20),
        name="finish",
    )(index, filtered, powers, decay.reshape(1, factors), series, loadings, precision, start, stop, off)


def local(series, loadings, precision, start_day, stop_day, off_day, decay, gain, smoother):
    devices = lax.axis_size("tm")
    place = lax.axis_index("tm").astype(jnp.int32)
    index = place[None]
    days = series.shape[0]
    day_count = days // devices
    factors = loadings.shape[1]
    precision, start, stop, off = (
        a.reshape(1, -1) for a in (precision, start_day, stop_day, off_day)
    )

    partial = partial_drive(index, series, loadings, precision, start, stop, off)
    terms = lax.all_to_all(
        partial.reshape(devices, day_count, factors), "tm", 0, 0, tiled=True
    )
    steps, running = transitions_of(
        index * day_count, day_count, loadings, precision, start, stop, off, decay, gain
    )
    states = own_states(terms, steps, gain)
    powers = smoother_powers(smoother)

    group = min(4, devices)
    matrix, tail = running[day_count - 1], states[day_count - 1 :]
    levels, uppers = [], []
    reach = 1
    while reach < group:
        pairs = [(i, i ^ reach) for i in range(devices)]
        other = lax.ppermute(matrix, "tm", pairs)
        other_tail = lax.ppermute(tail, "tm", pairs)
        upper = (place // reach) % 2
        levels.append((other, other_tail))
        uppers.append(upper)
        matrix, tail = combined(upper[None], matrix, tail, other, other_tail)
        reach *= 2

    state = jnp.zeros((1, factors), F32)
    for g in range(devices // group - 1):
        moved = tail if g == 0 else advanced(state, matrix, tail)
        pairs = [(g * group + j, (g + 1) * group + j) for j in range(group)]
        state = state + lax.ppermute(moved, "tm", pairs)

    filtered = filtered_of(state, jnp.stack(uppers), levels, running, states)
    everyone = lax.all_to_all(
        jnp.broadcast_to(filtered[None], (devices, day_count, factors)), "tm", 0, 0, tiled=True
    ).reshape(days, factors)
    return tuple(
        finish(
            index, day_count, everyone, powers, decay, series, loadings, precision, start, stop, off
        )
    )


def solution(mesh):
    in_specs = (
        P(None, ("spec", "tm")),
        P("spec", None),
        P("spec"),
        P("spec"),
        P("spec"),
        P("spec"),
        P(),
        P(),
        P(),
    )
    out_specs = (P("tm", "spec"), P(None, ("spec", "tm")))
    return jax.shard_map(local, mesh=mesh, in_specs=in_specs, out_specs=out_specs, check_vma=False)
```

time: 230 us -> 77.5 us (0.34)
  matrix products: 89.4 us -> 0 us
  blocking collectives: 69.9 us -> 13.7 us
  Pallas kernels: 0 us -> 25.4 us
  waiting for transfers between devices: 38.1 us -> 13.5 us
  between operations: 14.3 us -> 0.86 us
  starting transfers between devices: 7.47 us -> 16.8 us
    dot_general x48 -> x0, matrix products: 89.4 us -> none  [the longest x4 52.5 us: information_of(): lax.dot_general(loadings, scaled, (((0,), (0,)), ((), ())), preferred_ele...]
    all_gather x2 -> x0, blocking collectives: 59.3 us -> none  [prefix(): gathered = jax.tree.map(lambda a: lax.all_gather(a, axis), part)]
    all_gather x2 -> x0, waiting for transfers between devices: 38 us -> none  [prefix(): gathered = jax.tree.map(lambda a: lax.all_gather(a, axis), part)]
    pallas_call x0 -> x10, Pallas kernels: none -> 25.4 us  [the longest x1 13.1 us: transitions_of(): pl.pallas_call(kernel, grid=(steps,), in_specs=[pl.BlockSpec(memory_space...]
    ppermute x0 -> x7, waiting for transfers between devices: none -> 8.86 us  [the longest x2 7.57 us: local(): other_tail = lax.ppermute(tail, 'tm', pairs)]
    ppermute x0 -> x7, starting transfers between devices: none -> 5.95 us  [the longest x3 3.33 us: local(): state = state + lax.ppermute(moved, 'tm', pairs)]
    all_to_all x1, waiting for transfers between devices: 0.01 us -> 4.66 us  [local(): lax.all_to_all(jnp.broadcast_to(filtered[None], (devices, day_count, fact...]
    all_to_all x1, starting transfers between devices: 7.39 us -> 10.9 us  [local(): lax.all_to_all(jnp.broadcast_to(filtered[None], (devices, day_count, fact...]
  transfers between devices with their start and end apart: 3 -> 8, of which waited for: 2 -> 4; matrix products, arithmetic and copies ran while one was open for 26% -> 0% of each run, Pallas kernels for 0% -> 6%
where the time goes in v1:
time: 77.5 us; the launch traced here: 76.9 us
  Pallas kernels  25.4 us (33%)
  starting transfers between devices  16.8 us (22%)
  blocking collectives  13.7 us (18%)
  waiting for transfers between devices  13.5 us (17%)
  local copies, waits for them, and re-layouts  6.5 us (8%)
  between operations  0.86 us (1%)
    all_to_all x1, blocking collectives, local(): lax.all_to_all(partial.reshape(devices, day_count, factors), 'tm', 0, 0,...  13.7 us
    pallas_call x1, Pallas kernels, transitions_of(): pl.pallas_call(kernel, grid=(steps,), in_specs=[pl.BlockSpec(memory_space...  13.1 us
    all_to_all x1, starting transfers between devices, local(): lax.all_to_all(jnp.broadcast_to(filtered[None], (devices, day_count, fact...  10.9 us
    ppermute x2, waiting for transfers between devices, local(): other_tail = lax.ppermute(tail, 'tm', pairs)  7.57 us
    unnamed x28, local copies, waits for them, and re-layouts  4.97 us
    all_to_all x1, waiting for transfers between devices, local(): lax.all_to_all(jnp.broadcast_to(filtered[None], (devices, day_count, fact...  4.66 us
    pallas_call x1, Pallas kernels, finish(): pl.pallas_call(kernel, grid_spec=pltpu.PrefetchScalarGridSpec(num_scalar_...  4.42 us
    ppermute x3, starting transfers between devices, local(): state = state + lax.ppermute(moved, 'tm', pairs)  3.33 us
  transfers between devices with their start and end apart: 8, of which 4 were waited for; matrix products, arithmetic and copies ran while one was open for 0% of the time, Pallas kernels for 6%

profile of v1, /device:TPU:0, one launch (start us, length us, event | category | flops | bytes accessed | tf_op | source)
XLA Modules:
  0.0 76.9 jit_solution(6357050328697940155)
XLA Ops:
  0.6 0.8 %copy.11.col_ref = f32[256,1]{1,0:T(8,128)S(1)} copy(f32[256,1]{0,1:T(1,128)} %bitcast.23) | data formatting | bytes 2048 | tf_op jit(solution)/shard_map/reshape | solution.py:137
  1.5 0.0 copy-start.1
  1.5 0.8 %copy-done.1 = f32[16384]{0:T(1024)S(1)} copy-done((f32[16384]{0:T(1024)S(1)}, f32[16384]{0:T(1024)}, u32[]{:S(2)}) %copy-start.1) | copy-done | bytes 65560
  2.3 0.8 %copy-done.3 = s32[16384]{0:T(1024)S(1)} copy-done((s32[16384]{0:T(1024)S(1)}, s32[16384]{0:T(1024)}, u32[]{:S(2)}) %copy-start.3) | copy-done | bytes 65560
  3.1 0.8 %copy-done.5 = s32[16384]{0:T(1024)S(1)} copy-done((s32[16384]{0:T(1024)S(1)}, s32[16384]{0:T(1024)}, u32[]{:S(2)}) %copy-start.5) | copy-done | bytes 65560
  4.0 0.8 %copy-done.7 = s32[16384]{0:T(1024)S(1)} copy-done((s32[16384]{0:T(1024)S(1)}, s32[16384]{0:T(1024)}, u32[]{:S(2)}) %copy-start.7) | copy-done | bytes 65560
  4.8 0.9 %copy-done.9 = bf16[256,256]{1,0:T(8,128)(2,1)S(1)} copy-done((bf16[256,256]{1,0:T(8,128)(2,1)S(1)}, bf16[256,256]{1,0:T(8,128)(2,1)}, u32[]{:S(2)}) %copy-start.9) | copy-done | bytes 131096
  5.7 0.7 copy-done.11
  6.4 0.0 copy-start.8
  6.4 13.1 %transitions.1 = (f32[4,256,256]{2,1,0:T(8,128)S(1)}, f32[4,256,256]{2,1,0:T(8,128)S(1)}) custom-call(s32[1]{0:T(128)S(6)} %mul.3.day_ref, bf16[16384,256]{1,0:T(8,128)(2,1)} %load_ref.5, f32[1,16384]{1,0:T(1,128)S(1)} %bitcast.11, s32[1,16384]{1,0:T(1,128)S(1)} %bitcast.14, s32[1,16384]{1,0:T(1,128)S(1)} %bitcast.17, s32[1,16384]{1,0:T(1,128)S(1)} %bitcast.20, ...), custom_call_target="tpu_custom_call" | custom-call | flops 8589934592 | bytes 10485760 | tf_op jit(solution)/shard_map/transitions/pallas_call | solution.py:115
  19.5 0.0 copy-start.10
  19.5 0.0 copy-start.13
  19.6 0.0 copy-start.12
  19.6 0.5 collective-permute-start
  20.1 0.0 copy-done
  20.1 0.0 copy-done.2
  20.1 0.0 copy-done.4
  20.1 0.0 copy-done.6
  20.1 0.0 copy-done.8
  20.1 1.3 %partial_drive.1 = f32[64,256]{1,0:T(8,128)S(1)} custom-call(s32[1]{0:T(128)} %bitcast.index_ref, bf16[64,1024]{1,0:T(8,128)(2,1)S(1)} %copy-done, bf16[16384,256]{1,0:T(8,128)(2,1)} %load_ref.5, f32[1,16384]{1,0:T(1,128)S(1)} %bitcast.12, s32[1,16384]{1,0:T(1,128)S(1)} %bitcast.15, s32[1,16384]{1,0:T(1,128)S(1)} %bitcast.18, s32[1,16384]{1,0:T(1,128)S(1)} %bitcast.21), custom_call_target="tpu_custom_call" | custom-call | flops 33554432 | bytes 1048576 | tf_op jit(solution)/shard_map/partial_drive/pallas_call | solution.py:47
  21.4 13.7 %all_to_all.10.terms_ref = f32[16,4,256]{2,1,0:T(4,128)S(1)} all-to-all(f32[16,4,256]{2,1,0:T(4,128)S(1)} %reshape.36), channel_id=1, replica_groups=mesh['spec'=2,'tm'=16] {'tm'}, dimensions={0} | all-to-all | bytes 131072 | tf_op jit(solution)/shard_map/all_to_all | solution.py:346
  35.2 0.0 copy-done.10
  35.2 1.3 %own_states.1.refs_5_ = f32[4,256]{1,0:T(4,128)S(1)} custom-call(f32[16,4,256]{2,1,0:T(4,128)S(1)} %all_to_all.10.terms_ref, f32[4,256,256]{2,1,0:T(8,128)S(1)} %get-tuple-element.9.step_ref, bf16[256,256]{1,0:T(8,128)(2,1)S(1)} %copy-done.10), custom_call_target="tpu_custom_call" | custom-call | flops 10485760 | bytes 1048576 | tf_op jit(solution)/shard_map/own_states/pallas_call | solution.py:158
  36.5 0.0 collective-permute-start.1
  36.5 1.1 %collective-permute-done.1.other_tail_ref.refs_1_ = f32[1,256]{1,0:T(1,128)S(1)} collective-permute-done((f32[1,256]{1,0:T(1,128)S(1)}, f32[1,256]{1,0:T(1,128)S(1)}, u32[]{:S(2)}, u32[]{:S(2)}) %collective-permute-start.1) | collective-permute-done | bytes 1056 | tf_op jit(solution)/shard_map/ppermute | solution.py:362
  37.6 0.0 collective-permute-done.other_ref.refs_0_
  37.6 0.5 combined.2
  38.1 0.2 collective-permute-start.2
  38.3 1.9 %collective-permute-start.3 = (f32[1,256]{1,0:T(1,128)S(1)}, f32[1,256]{1,0:T(1,128)S(1)}, u32[]{:S(2)}, u32[]{:S(2)}) collective-permute-start(f32[1,256]{1,0:T(1,128)S(1)} %get-tuple-element.11.my_ref), channel_id=1, source_target_pairs={{0,2},{1,3},{2,0},{3,1},{4,6},{5,7},{6,4},{7,5},{8,10},{9,11},{10,... | collective-permute-start | bytes 3080 | tf_op jit(solution)/shard_map/ppermute | solution.py:362
  40.2 6.4 %collective-permute-done.3.other_tail_ref.refs_3_ = f32[1,256]{1,0:T(1,128)S(1)} collective-permute-done((f32[1,256]{1,0:T(1,128)S(1)}, f32[1,256]{1,0:T(1,128)S(1)}, u32[]{:S(2)}, u32[]{:S(2)}) %collective-permute-start.3) | collective-permute-done | bytes 1056 | tf_op jit(solution)/shard_map/ppermute | solution.py:362
  46.7 0.0 collective-permute-done.2.other_ref.refs_2_
  46.7 0.5 combined.3
  47.2 2.0 %collective-permute-start.4 = (f32[1,256]{1,0:T(1,128)S(1)}, f32[1,256]{1,0:T(1,128)S(1)}, u32[]{:S(2)}, u32[]{:S(2)}) collective-permute-start(f32[1,256]{1,0:T(1,128)S(1)} %get-tuple-element.12.tail_ref), channel_id=1, source_target_pairs={{0,4},{1,5},{2,6},{3,7},{16,20},{17,21},{18,22},{19,23}} | collective-permute-start | bytes 3080 | tf_op jit(solution)/shard_map/ppermute | solution.py:373
  49.2 1.3 %collective-permute-done.4.state_ref = f32[1,256]{1,0:T(1,128)S(1)} collective-permute-done((f32[1,256]{1,0:T(1,128)S(1)}, f32[1,256]{1,0:T(1,128)S(1)}, u32[]{:S(2)}, u32[]{:S(2)}) %collective-permute-start.4) | collective-permute-done | bytes 1056 | tf_op jit(solution)/shard_map/ppermute | solution.py:373
  50.5 0.2 advanced.2
  50.7 0.7 collective-permute-start.5
  51.4 0.0 collective-permute-done.5
  51.4 0.2 advanced.3
  51.6 0.7 collective-permute-start.6
  52.3 0.1 pad_add_fusion.upper_ref
  52.4 0.0 collective-permute-done.6
  52.4 1.7 %filtered.1 = f32[4,256]{1,0:T(4,128)S(1)} custom-call(s32[2]{0:T(128)S(1)} %pad_add_fusion.upper_ref, f32[1,256]{1,0:T(1,128)S(1)} %add.18.enter_ref, f32[256,256]{1,0:T(8,128)S(1)} %collective-permute-done.other_ref.refs_0_, f32[1,256]{1,0:T(1,128)S(1)} %collective-permute-done.1.other_tail_ref.refs_1_, ...), custom_call_target="tpu_custom_call" | custom-call | flops 5242880 | bytes 2097152 | tf_op jit(solution)/shard_map/filtered/pallas_call | solution.py:232
  54.0 0.6 broadcast_in_dim.5
  54.7 10.9 %all-to-all-start.1 = ((f32[16,4,256]{2,1,0:T(4,128)}), f32[16,4,256]{2,1,0:T(4,128)S(1)}, u32[]{:S(2)}, u32[]{:S(2)}) async-start(f32[16,4,256]{2,1,0:T(4,128)} %broadcast_in_dim.5), calls=%async_computation.1 | async-start | bytes 131072 | tf_op jit(solution)/shard_map/all_to_all | solution.py:376
  65.6 0.0 copy-done.13
  65.6 2.2 %smoother_powers.1.pow_ref = f32[5,256,256]{2,1,0:T(8,128)S(1)} custom-call(f32[256,256]{1,0:T(8,128)S(1)} %copy-done.13), custom_call_target="tpu_custom_call" | custom-call | flops 805306368 | bytes 2097152 | tf_op jit(solution)/shard_map/smoother_powers/pallas_call | solution.py:254
  67.8 4.7 %all-to-all-done.1 = f32[16,4,256]{2,1,0:T(4,128)S(1)} async-done(((f32[16,4,256]{2,1,0:T(4,128)}), f32[16,4,256]{2,1,0:T(4,128)S(1)}, u32[]{:S(2)}, u32[]{:S(2)}) %all-to-all-start.1) | async-done | bytes 65568 | tf_op jit(solution)/shard_map/all_to_all | solution.py:376
  72.5 4.4 %finish.1 = (f32[4,256]{1,0:T(4,128)}, bf16[64,1024]{1,0:T(8,128)(2,1)}) custom-call(s32[1]{0:T(128)} %bitcast.index_ref, f32[64,256]{1,0:T(8,128)S(1)} %reshape.37.filt_ref, f32[5,256,256]{2,1,0:T(8,128)S(1)} %smoother_powers.1.pow_ref, f32[1,256]{1,0:T(1,128)S(1)} %bitcast.25, bf16[64,1024]{1,0:T(8,128)(2,1)S(1)} %copy-done, bf16[16384,256]{1,0:T(8,128)(2,1)} %load_ref.5, ...), custom_call_target="tpu_custom_call" | custom-call | flops 33554432 | bytes 2097152 | tf_op jit(solution)/shard_map/finish/pallas_call | solution.py:302
  (16 shorter events, 0.1 us)
Async XLA Ops:
  1.5 0.8 %copy-start.1 = (f32[16384]{0:T(1024)S(1)}, f32[16384]{0:T(1024)}, u32[]{:S(2)}) copy-start(f32[16384]{0:T(1024)} %param.11) | copy-start | bytes 196612
  2.3 0.8 %copy-start.3 = (s32[16384]{0:T(1024)S(1)}, s32[16384]{0:T(1024)}, u32[]{:S(2)}) copy-start(s32[16384]{0:T(1024)} %param.12) | copy-start | bytes 196612
  3.1 0.8 %copy-start.5 = (s32[16384]{0:T(1024)S(1)}, s32[16384]{0:T(1024)}, u32[]{:S(2)}) copy-start(s32[16384]{0:T(1024)} %param.13) | copy-start | bytes 196612
  4.0 0.8 %copy-start.7 = (s32[16384]{0:T(1024)S(1)}, s32[16384]{0:T(1024)}, u32[]{:S(2)}) copy-start(s32[16384]{0:T(1024)} %param.14) | copy-start | bytes 196612
  4.8 0.9 %copy-start.9 = (bf16[256,256]{1,0:T(8,128)(2,1)S(1)}, bf16[256,256]{1,0:T(8,128)(2,1)}, u32[]{:S(2)}) copy-start(bf16[256,256]{1,0:T(8,128)(2,1)} %gain_ref.3) | copy-start | bytes 393220
  5.7 0.7 copy-start.11
  6.4 13.7 %copy-start = (bf16[64,1024]{1,0:T(8,128)(2,1)S(1)}, bf16[64,1024]{1,0:T(8,128)(2,1)}, u32[]{:S(2)}) copy-start(bf16[64,1024]{1,0:T(8,128)(2,1)} %series_ref.3) | copy-start | bytes 393220
  6.4 13.7 %copy-start.2 = (f32[16384]{0:T(1024)S(1)}, f32[16384]{0:T(1024)}, u32[]{:S(2)}) copy-start(f32[16384]{0:T(1024)} %param.11) | copy-start | bytes 196612
  6.4 13.7 %copy-start.4 = (s32[16384]{0:T(1024)S(1)}, s32[16384]{0:T(1024)}, u32[]{:S(2)}) copy-start(s32[16384]{0:T(1024)} %param.12) | copy-start | bytes 196612
  6.4 13.7 %copy-start.6 = (s32[16384]{0:T(1024)S(1)}, s32[16384]{0:T(1024)}, u32[]{:S(2)}) copy-start(s32[16384]{0:T(1024)} %param.13) | copy-start | bytes 196612
  6.4 13.7 %copy-start.8 = (s32[16384]{0:T(1024)S(1)}, s32[16384]{0:T(1024)}, u32[]{:S(2)}) copy-start(s32[16384]{0:T(1024)} %param.14) | copy-start | bytes 196612
  19.5 15.7 %copy-start.10 = (bf16[256,256]{1,0:T(8,128)(2,1)S(1)}, bf16[256,256]{1,0:T(8,128)(2,1)}, u32[]{:S(2)}) copy-start(bf16[256,256]{1,0:T(8,128)(2,1)} %gain_ref.3) | copy-start | bytes 393220
  19.5 46.1 %copy-start.13 = (f32[256,256]{1,0:T(8,128)S(1)}, f32[256,256]{1,0:T(8,128)}, u32[]{:S(2)}) copy-start(f32[256,256]{1,0:T(8,128)} %in_ref.1) | copy-start | bytes 786436
  19.6 52.9 %copy-start.12 = (f32[256]{0:T(256)S(1)}, f32[256]{0:T(256)}, u32[]{:S(2)}) copy-start(f32[256]{0:T(256)} %param.15) | copy-start | bytes 3076
  19.6 18.0 %collective-permute-start = (f32[256,256]{1,0:T(8,128)S(1)}, f32[256,256]{1,0:T(8,128)S(1)}, u32[]{:S(2)}, u32[]{:S(2)}) collective-permute-start(f32[256,256]{1,0:T(8,128)S(1)} %slice_bitcast_fusion.mine_ref), channel_id=1, source_target_pairs={{0,1},{1,0},{2,3},{3,2},{4,5},{5,4},{6,7},{7,6},{8,9},{9,8},{10,11... | collective-permute-start | bytes 786440 | tf_op jit(solution)/shard_map/ppermute | solution.py:361
  36.5 1.2 %collective-permute-start.1 = (f32[1,256]{1,0:T(1,128)S(1)}, f32[1,256]{1,0:T(1,128)S(1)}, u32[]{:S(2)}, u32[]{:S(2)}) collective-permute-start(f32[1,256]{1,0:T(1,128)S(1)} %slice.8.my_ref), channel_id=1, source_target_pairs={{0,1},{1,0},{2,3},{3,2},{4,5},{5,4},{6,7},{7,6},{8,9},{9,8},{10,11... | collective-permute-start | bytes 3080 | tf_op jit(solution)/shard_map/ppermute | solution.py:362
  38.1 8.5 %collective-permute-start.2 = (f32[256,256]{1,0:T(8,128)S(1)}, f32[256,256]{1,0:T(8,128)S(1)}, u32[]{:S(2)}, u32[]{:S(2)}) collective-permute-start(f32[256,256]{1,0:T(8,128)S(1)} %get-tuple-element.10.mine_ref), channel_id=1, source_target_pairs={{0,2},{1,3},{2,0},{3,1},{4,6},{5,7},{6,4},{7,5},{8,10},{9,11},{10,... | collective-permute-start | bytes 786440 | tf_op jit(solution)/shard_map/ppermute | solution.py:361
  38.3 8.3 %collective-permute-start.3 = (f32[1,256]{1,0:T(1,128)S(1)}, f32[1,256]{1,0:T(1,128)S(1)}, u32[]{:S(2)}, u32[]{:S(2)}) collective-permute-start(f32[1,256]{1,0:T(1,128)S(1)} %get-tuple-element.11.my_ref), channel_id=1, source_target_pairs={{0,2},{1,3},{2,0},{3,1},{4,6},{5,7},{6,4},{7,5},{8,10},{9,11},{10,... | collective-permute-start | bytes 3080 | tf_op jit(solution)/shard_map/ppermute | solution.py:362
  47.2 3.3 %collective-permute-start.4 = (f32[1,256]{1,0:T(1,128)S(1)}, f32[1,256]{1,0:T(1,128)S(1)}, u32[]{:S(2)}, u32[]{:S(2)}) collective-permute-start(f32[1,256]{1,0:T(1,128)S(1)} %get-tuple-element.12.tail_ref), channel_id=1, source_target_pairs={{0,4},{1,5},{2,6},{3,7},{16,20},{17,21},{18,22},{19,23}} | collective-permute-start | bytes 3080 | tf_op jit(solution)/shard_map/ppermute | solution.py:373
  50.7 0.7 collective-permute-start.5
  51.6 0.7 collective-permute-start.6
  54.7 17.8 %all-to-all-start.1 = ((f32[16,4,256]{2,1,0:T(4,128)}), f32[16,4,256]{2,1,0:T(4,128)S(1)}, u32[]{:S(2)}, u32[]{:S(2)}) async-start(f32[16,4,256]{2,1,0:T(4,128)} %broadcast_in_dim.5), calls=%async_computation.1 | async-start | bytes 131072 | tf_op jit(solution)/shard_map/all_to_all | solution.py:376

commit v2 on v1

v2 whole, which is shorter than its diff:
```python
import jax
import jax.numpy as jnp
from jax import lax
from jax.experimental import pallas as pl
from jax.experimental.pallas import tpu as pltpu
from jax.sharding import PartitionSpec as P

F32 = jnp.float32
BF16 = jnp.bfloat16
VMEM = pltpu.MemorySpace.VMEM
SMEM = pltpu.MemorySpace.SMEM
HBM = pltpu.MemorySpace.HBM
POWERS = 5


def params(**more):
    return pltpu.CompilerParams(vmem_limit_bytes=48 << 20, **more)


def cost(flops, nbytes):
    return pl.CostEstimate(flops=flops, bytes_accessed=nbytes, transcendentals=0)


def vmem(count):
    return [pl.BlockSpec(memory_space=VMEM)] * count


def hbm(count):
    return [pl.BlockSpec(memory_space=HBM)] * count


def smem():
    return pl.BlockSpec(memory_space=SMEM)


def shape(*dims, dtype=F32):
    return jax.ShapeDtypeStruct(dims, dtype)


def mul(a, b):
    return jnp.dot(a, b, preferred_element_type=F32)


def split(a):
    high = a.astype(BF16)
    return high, (a - high.astype(F32)).astype(BF16)


def product(a, b):
    high, low = split(a)
    return mul(high, b[0]) + mul(low, b[0]) + mul(high, b[1])


def eye(factors):
    dims = (factors, factors)
    return lax.broadcasted_iota(jnp.int32, dims, 0) == lax.broadcasted_iota(jnp.int32, dims, 1)


def activity(day, start, stop, off):
    return (day >= start) & (day < stop) & (lax.rem(day, 7) != off)


def partial_drive(index, series, loadings, tables):
    days, own = series.shape
    factors = loadings.shape[1]

    def kernel(
        index_ref, series_hbm, load_hbm, prec_hbm, start_hbm, stop_hbm, off_hbm, out_ref,
        series_ref, load_ref, prec_ref, start_ref, stop_ref, off_ref, sems,
    ):
        first = pl.multiple_of(index_ref[0] * own, own)
        mine = pl.ds(first, own)
        copies = [
            pltpu.make_async_copy(source, target, sems.at[n])
            for n, (source, target) in enumerate(
                [
                    (prec_hbm.at[:, mine], prec_ref),
                    (start_hbm.at[:, mine], start_ref),
                    (stop_hbm.at[:, mine], stop_ref),
                    (off_hbm.at[:, mine], off_ref),
                    (series_hbm, series_ref),
                    (load_hbm.at[mine], load_ref),
                ]
            )
        ]
        for copy in copies:
            copy.start()
        day = lax.broadcasted_iota(jnp.int32, (days, 1), 0)
        for copy in copies[:5]:
            copy.wait()
        active = activity(day, start_ref[...], stop_ref[...], off_ref[...])
        weights = jnp.where(active, prec_ref[...], 0.0)
        weighted = (weights * series_ref[...].astype(F32)).astype(BF16)
        copies[5].wait()
        out_ref[...] = mul(weighted, load_ref[...])

    return pl.pallas_call(
        kernel,
        in_specs=[smem()] + hbm(6),
        out_specs=pl.BlockSpec(memory_space=VMEM),
        out_shape=shape(days, factors),
        scratch_shapes=[
            pltpu.VMEM((days, own), BF16),
            pltpu.VMEM((own, factors), BF16),
            pltpu.VMEM((1, own), F32),
            pltpu.VMEM((1, own), jnp.int32),
            pltpu.VMEM((1, own), jnp.int32),
            pltpu.VMEM((1, own), jnp.int32),
            pltpu.SemaphoreType.DMA((6,)),
        ],
        compiler_params=params(),
        cost_estimate=cost(2 * days * own * factors, 1 << 20),
        name="partial_drive",
    )(index, series, loadings, *tables)


def transitions_of(first_day, day_count, loadings, tables, decay, gain):
    providers, factors = loadings.shape
    chunk = min(4096, providers)
    steps = providers // chunk

    def kernel(
        day_ref, load_ref, prec_hbm, start_hbm, stop_hbm, off_hbm, decay_hbm, gain_hbm,
        step_ref, run_ref, rest_ref, diag_ref,
        acc, prec_ref, start_ref, stop_ref, off_ref, decay_ref, gain_ref, sems,
    ):
        step = pl.program_id(0)

        @pl.when(step == 0)
        def _():
            copies = [
                pltpu.make_async_copy(source, target, sems.at[n])
                for n, (source, target) in enumerate(
                    [
                        (prec_hbm, prec_ref),
                        (start_hbm, start_ref),
                        (stop_hbm, stop_ref),
                        (off_hbm, off_ref),
                        (decay_hbm, decay_ref),
                        (gain_hbm, gain_ref),
                    ]
                )
            ]
            for copy in copies:
                copy.start()
            acc[...] = jnp.zeros_like(acc)
            for copy in copies:
                copy.wait()

        place = pl.ds(pl.multiple_of(step * chunk, chunk), chunk)
        block = load_ref[...]
        scaled = (block.T.astype(F32) * prec_ref[:, place]).astype(BF16)
        for d in range(day_count):
            active = activity(
                day_ref[0] + d, start_ref[:, place], stop_ref[:, place], off_ref[:, place]
            )
            mask = active.astype(F32).astype(BF16)
            acc[d] += mul(scaled * mask, block)

        @pl.when(step == steps - 1)
        def _():
            same = eye(factors)
            diagonal = jnp.where(same, decay_ref[...], 0.0)
            column = jnp.sum(diagonal, axis=1, keepdims=True)
            for d in range(day_count):
                damped = (acc[d] * column).astype(BF16)
                pulled = lax.dot_general(
                    damped, gain_ref[...], (((1,), (1,)), ((), ())), preferred_element_type=F32
                )
                step_ref[d] = diagonal - pulled
            run_ref[0] = step_ref[0]
            for d in range(1, day_count):
                run_ref[d] = product(run_ref[d - 1], split(step_ref[d]))
            last = run_ref[day_count - 1]
            rest_ref[...] = jnp.where(same, 0.0, last).astype(BF16)
            diag_ref[...] = jnp.sum(jnp.where(same, last, 0.0), axis=0, keepdims=True)

    cube = pl.BlockSpec((day_count, factors, factors), lambda i: (0, 0, 0))
    return pl.pallas_call(
        kernel,
        grid=(steps,),
        in_specs=[smem(), pl.BlockSpec((chunk, factors), lambda i: (i, 0))] + hbm(6),
        out_specs=[
            cube,
            cube,
            pl.BlockSpec((factors, factors), lambda i: (0, 0)),
            pl.BlockSpec((1, factors), lambda i: (0, 0)),
        ],
        out_shape=[
            shape(day_count, factors, factors),
            shape(day_count, factors, factors),
            shape(factors, factors, dtype=BF16),
            shape(1, factors),
        ],
        scratch_shapes=[
            pltpu.VMEM((day_count, factors, factors), F32),
            pltpu.VMEM((1, providers), F32),
            pltpu.VMEM((1, providers), jnp.int32),
            pltpu.VMEM((1, providers), jnp.int32),
            pltpu.VMEM((1, providers), jnp.int32),
            pltpu.VMEM((1, factors), F32),
            pltpu.VMEM((factors, factors), BF16),
            pltpu.SemaphoreType.DMA((6,)),
        ],
        compiler_params=params(dimension_semantics=("arbitrary",)),
        cost_estimate=cost(2 * day_count * providers * factors * factors, 10 << 20),
        name="transitions",
    )(first_day, loadings, *tables, decay, gain)


def own_states(terms, steps, gain, diag):
    parts, day_count, factors = terms.shape

    def kernel(terms_ref, step_ref, gain_ref, diag_ref, out_ref, packet_ref):
        drive = terms_ref[0]
        for p in range(1, parts):
            drive = drive + terms_ref[p]
        high, low = split(drive)
        weights = gain_ref[...]
        dims = (((1,), (1,)), ((), ()))
        rest = (drive - high.astype(F32) - low.astype(F32)).astype(BF16)
        offsets = sum(
            lax.dot_general(part, weights, dims, preferred_element_type=F32)
            for part in (high, low, rest)
        )
        state = offsets[0:1]
        out_ref[0:1] = state
        for d in range(1, day_count):
            state = product(state, split(step_ref[d])) + offsets[d : d + 1]
            out_ref[d : d + 1] = state
        packet_ref[0:1] = state
        packet_ref[1:2] = diag_ref[...]

    return pl.pallas_call(
        kernel,
        in_specs=vmem(4),
        out_specs=vmem(2),
        out_shape=[shape(day_count, factors), shape(2, factors)],
        compiler_params=params(),
        cost_estimate=cost(20 * factors * factors * 8, 1 << 20),
        name="own_states",
    )(terms, steps, gain, diag)


def rebuilt(rest, diag, same):
    return rest.astype(F32) + jnp.where(same, diag, 0.0)


def combined(upper, matrix, packet, other_rest, other_packet):
    factors = matrix.shape[0]

    def kernel(upper_ref, mine_ref, packet_ref, rest_ref, other_ref, map_ref, part_ref, next_ref):
        same = eye(factors)
        other = rebuilt(rest_ref[...], other_ref[1:2], same)

        def write(low, low_tail, high, high_tail):
            high = split(high)
            total = product(low, high)
            map_ref[...] = total
            part_ref[...] = jnp.where(same, 0.0, total).astype(BF16)
            next_ref[0:1] = product(low_tail, high) + high_tail
            next_ref[1:2] = jnp.sum(jnp.where(same, total, 0.0), axis=0, keepdims=True)

        @pl.when(upper_ref[0] == 1)
        def _():
            write(other, other_ref[0:1], mine_ref[...], packet_ref[0:1])

        @pl.when(upper_ref[0] == 0)
        def _():
            write(mine_ref[...], packet_ref[0:1], other, other_ref[0:1])

    return pl.pallas_call(
        kernel,
        in_specs=[smem()] + vmem(4),
        out_specs=vmem(3),
        out_shape=[
            shape(factors, factors),
            shape(factors, factors, dtype=BF16),
            shape(2, factors),
        ],
        compiler_params=params(),
        cost_estimate=cost(12 * factors**3, 1 << 20),
        name="combined",
    )(upper, matrix, packet, other_rest, other_packet)


def advanced(state, matrix, packet):
    factors = matrix.shape[0]

    def kernel(state_ref, matrix_ref, packet_ref, out_ref):
        out_ref[...] = product(state_ref[...], split(matrix_ref[...])) + packet_ref[0:1]

    return pl.pallas_call(
        kernel,
        in_specs=vmem(3),
        out_specs=pl.BlockSpec(memory_space=VMEM),
        out_shape=shape(1, factors),
        compiler_params=params(),
        cost_estimate=cost(12 * factors**2, 1 << 18),
        name="advanced",
    )(state, matrix, packet)


def prefixed(uppers, levels, running, states):
    day_count, factors = states.shape
    count = len(levels)

    def kernel(*refs):
        upper_refs = refs[:count]
        parts = refs[count : 3 * count]
        run_ref, states_ref, high_ref, low_ref, add_ref, work, tail = refs[3 * count :]
        same = eye(factors)
        work[...] = jnp.where(same, 1.0, 0.0)
        tail[...] = jnp.zeros_like(tail)
        for level in reversed(range(count)):

            @pl.when(upper_refs[level][0] == 1)
            def _():
                packet = parts[2 * level + 1]
                step = split(rebuilt(parts[2 * level][...], packet[1:2], same))
                work[...] = product(work[...], step)
                tail[...] = product(tail[...], step) + packet[0:1]

        for d in range(day_count):
            step = split(run_ref[d])
            place = slice(d * factors, (d + 1) * factors)
            high, low = split(product(work[...], step))
            high_ref[:, place] = high
            low_ref[:, place] = low
            add_ref[:, place] = product(tail[...], step) + states_ref[d : d + 1]

    wide = day_count * factors
    return pl.pallas_call(
        kernel,
        in_specs=[smem()] * count + vmem(2 * count + 2),
        out_specs=vmem(3),
        out_shape=[
            shape(factors, wide, dtype=BF16),
            shape(factors, wide, dtype=BF16),
            shape(1, wide),
        ],
        scratch_shapes=[pltpu.VMEM((factors, factors), F32), pltpu.VMEM((1, factors), F32)],
        compiler_params=params(),
        cost_estimate=cost(36 * factors**3, 3 << 20),
        name="prefixed",
    )(*uppers, *[a for level in levels for a in level], running, states)


def filtered_of(state, arrived, high, low, add):
    factors, wide = high.shape
    day_count = wide // factors

    def kernel(state_ref, arrived_ref, high_ref, low_ref, add_ref, out_ref):
        entering = state_ref[...] + arrived_ref[...]
        row = product(entering, (high_ref[...], low_ref[...])) + add_ref[...]
        for d in range(day_count):
            out_ref[d : d + 1] = row[:, d * factors : (d + 1) * factors]

    return pl.pallas_call(
        kernel,
        in_specs=vmem(5),
        out_specs=pl.BlockSpec(memory_space=VMEM),
        out_shape=shape(day_count, factors),
        compiler_params=params(),
        cost_estimate=cost(6 * factors * wide, 1 << 20),
        name="filtered",
    )(state, arrived, high, low, add)


def smoother_powers(smoother):
    factors = smoother.shape[0]

    def kernel(in_ref, high_ref, low_ref):
        power = in_ref[...].T
        for p in range(POWERS):
            parts = split(power)
            high_ref[p], low_ref[p] = parts
            if p < POWERS - 1:
                power = product(power, parts)

    return pl.pallas_call(
        kernel,
        in_specs=vmem(1),
        out_specs=vmem(2),
        out_shape=[shape(POWERS, factors, factors, dtype=BF16)] * 2,
        compiler_params=params(),
        cost_estimate=cost(24 * factors**3, 2 << 20),
        name="smoother_powers",
    )(smoother)


def finish(index, day_count, pieces, powers, decay, series, loadings, tables):
    days, own = series.shape
    factors = loadings.shape[1]
    stride = 2 ** (POWERS - 1)
    blocks = days // stride
    count = len(pieces)

    def kernel(index_ref, *refs):
        piece_refs = refs[:count]
        (
            high_ref, low_ref, decay_ref, series_hbm, load_hbm, prec_hbm, start_hbm, stop_hbm,
            off_hbm, smooth_ref, score_ref, filt, work, series_ref, load_ref, prec_ref, start_ref,
            stop_ref, off_ref, sems,
        ) = refs[count:]
        me = index_ref[0]
        mine = pl.ds(pl.multiple_of(me * own, own), own)
        copies = [
            pltpu.make_async_copy(source, target, sems.at[n])
            for n, (source, target) in enumerate(
                [
                    (load_hbm.at[mine], load_ref),
                    (series_hbm, series_ref),
                    (prec_hbm.at[:, mine], prec_ref),
                    (start_hbm.at[:, mine], start_ref),
                    (stop_hbm.at[:, mine], stop_ref),
                    (off_hbm.at[:, mine], off_ref),
                ]
            )
        ]
        for copy in copies:
            copy.start()
        block = 0
        for piece in piece_refs:
            for b in range(piece.shape[0]):
                first = (me ^ block) * day_count
                for d in range(day_count):
                    filt[pl.ds(first + d, 1), :] = piece[b, d : d + 1]
                block += 1
        filtered = filt[...]
        carried = filtered * decay_ref[...]
        carried = jnp.concatenate([jnp.zeros((1, factors), F32), carried[:-1]], 0)
        total = filtered - carried
        for p in range(POWERS - 1):
            reach = 2**p
            later = jnp.concatenate([total[reach:], jnp.zeros((reach, factors), F32)], 0)
            total = total + product(later, (high_ref[p], low_ref[p]))
        far = (high_ref[POWERS - 1], low_ref[POWERS - 1])
        row = total[(blocks - 1) * stride :]
        work[(blocks - 1) * stride :, :] = row
        for b in reversed(range(blocks - 1)):
            row = total[b * stride : (b + 1) * stride] + product(row, far)
            work[b * stride : (b + 1) * stride, :] = row
        work[...] += carried
        for d in range(day_count):
            smooth_ref[d : d + 1, :] = work[pl.ds(me * day_count + d, 1), :]
        for copy in copies:
            copy.wait()
        fitted = lax.dot_general(
            work[...].astype(BF16), load_ref[...], (((1,), (1,)), ((), ())),
            preferred_element_type=F32,
        )
        day = lax.broadcasted_iota(jnp.int32, (days, 1), 0)
        active = activity(day, start_ref[...], stop_ref[...], off_ref[...])
        residual = (series_ref[...].astype(F32) - fitted) * jnp.sqrt(prec_ref[...])
        score_ref[...] = jnp.where(active, residual, 0.0).astype(BF16)

    return pl.pallas_call(
        kernel,
        in_specs=[smem()] + vmem(count + 3) + hbm(6),
        out_specs=vmem(2),
        out_shape=[shape(day_count, factors), shape(days, own, dtype=BF16)],
        scratch_shapes=[
            pltpu.VMEM((days, factors), F32),
            pltpu.VMEM((days, factors), F32),
            pltpu.VMEM((days, own), BF16),
            pltpu.VMEM((own, factors), BF16),
            pltpu.VMEM((1, own), F32),
            pltpu.VMEM((1, own), jnp.int32),
            pltpu.VMEM((1, own), jnp.int32),
            pltpu.VMEM((1, own), jnp.int32),
            pltpu.SemaphoreType.DMA((6,)),
        ],
        compiler_params=params(),
        cost_estimate=cost(2 * days * own * factors, 2 << 20),
        name="finish",
    )(index, *pieces, *powers, decay, series, loadings, *tables)


def local(series, loadings, precision, start_day, stop_day, off_day, decay, gain, smoother):
    devices = lax.axis_size("tm")
    place = lax.axis_index("tm").astype(jnp.int32)
    index = place[None]
    days = series.shape[0]
    day_count = days // devices
    factors = loadings.shape[1]
    tables = [a.reshape(1, -1) for a in (precision, start_day, stop_day, off_day)]
    decay = decay.reshape(1, factors)

    def swapped(array, distance):
        return lax.ppermute(array, "tm", [(i, i ^ distance) for i in range(devices)])

    partial = partial_drive(index, series, loadings, tables)
    partial, first_day = lax.optimization_barrier((partial, index * day_count))
    terms = lax.all_to_all(
        partial.reshape(devices, day_count, factors), "tm", 0, 0, tiled=True
    )
    steps, running, rest, diag = transitions_of(first_day, day_count, loadings, tables, decay, gain)
    states, packet = own_states(terms, steps, gain, diag)

    group = min(4, devices)
    matrix = running[day_count - 1]
    levels, uppers = [], []
    reach = 1
    while reach < group:
        other_rest = swapped(rest, reach)
        other_packet = swapped(packet, reach)
        upper = jnp.where((place & reach) != 0, 1, 0).astype(jnp.int32)[None]
        levels.append((other_rest, other_packet))
        uppers.append(upper)
        matrix, rest, packet = combined(upper, matrix, packet, other_rest, other_packet)
        reach *= 2

    ahead = prefixed(uppers, levels, running, states)
    state = jnp.zeros((1, factors), F32)
    arrived = jnp.zeros((1, factors), F32)
    for g in range(devices // group - 1):
        state = state + arrived
        moved = packet[0:1] if g == 0 else advanced(state, matrix, packet)
        pairs = [(g * group + j, (g + 1) * group + j) for j in range(group)]
        arrived = lax.ppermute(moved, "tm", pairs)

    pieces = filtered_of(state, arrived, *ahead)[None]
    reach = 1
    while reach * 4 < devices:
        pieces = jnp.concatenate([pieces, swapped(pieces, reach)], 0)
        reach *= 2
    pieces = [pieces] + [
        swapped(pieces, reach * n) for n in range(1, devices // reach)
    ]
    powers = smoother_powers(smoother)
    return tuple(finish(index, day_count, pieces, powers, decay, series, loadings, tables))


def solution(mesh):
    in_specs = (
        P(None, ("spec", "tm")),
        P("spec", None),
        P("spec"),
        P("spec"),
        P("spec"),
        P("spec"),
        P(),
        P(),
        P(),
    )
    out_specs = (P("tm", "spec"), P(None, ("spec", "tm")))
    return jax.shard_map(local, mesh=mesh, in_specs=in_specs, out_specs=out_specs, check_vma=False)
```

time: 77.5 us -> 67.8 us (0.87)
  blocking collectives: 13.7 us -> 0 us
  starting transfers between devices: 16.8 us -> 26.1 us
  Pallas kernels: 25.4 us -> 22.3 us
  local copies, waits for them, and re-layouts: 6.5 us -> 4.96 us
    all_to_all x1 -> x0, blocking collectives: 13.7 us -> none  [local(): lax.all_to_all(partial.reshape(devices, day_count, factors), 'tm', 0, 0,...]
    ppermute x7 -> x12, starting transfers between devices: 5.95 us -> 18.7 us  [the longest x9 13.7 us: swapped(): lax.ppermute(array, 'tm', [(i, i ^ distance) for i in range(devices)])]
    all_to_all x1, waiting for transfers between devices: 4.66 us -> 0.01 us  [local(): lax.all_to_all(partial.reshape(devices, day_count, factors), 'tm', 0, 0,...]
    ppermute x7 -> x12, waiting for transfers between devices: 8.86 us -> 13.1 us  [the longest x9 11.9 us: swapped(): lax.ppermute(array, 'tm', [(i, i ^ distance) for i in range(devices)])]
    all_to_all x1, starting transfers between devices: 10.9 us -> 7.39 us  [local(): lax.all_to_all(partial.reshape(devices, day_count, factors), 'tm', 0, 0,...]
    pallas_call x10 -> x11, Pallas kernels: 25.4 us -> 22.3 us  [the longest x1 13 us: transitions_of(): pl.pallas_call(kernel, grid=(steps,), in_specs=[smem(), pl.BlockSpec((chu...]
    reshape x2 -> x0, local copies, waits for them, and re-layouts: 0.83 us -> none  [the longest x1 0.81 us: transitions_of(): decay.reshape(factors, 1)]
    unnamed x28 -> x26, local copies, waits for them, and re-layouts: 4.97 us -> 4.29 us
  transfers between devices with their start and end apart: 8 -> 13, of which waited for: 4 -> 7; matrix products, arithmetic and copies ran while one was open for 0% -> 0% of each run, Pallas kernels for 6% -> 24%
where the time goes in v2:
time: 67.8 us; the launch traced here: 67.4 us
  starting transfers between devices  26.1 us (38%)
  Pallas kernels  22.3 us (33%)
  waiting for transfers between devices  13.1 us (19%)
  local copies, waits for them, and re-layouts  4.96 us (7%)
  between operations  0.86 us (1%)
    ppermute x9, starting transfers between devices, swapped(): lax.ppermute(array, 'tm', [(i, i ^ distance) for i in range(devices)])  13.7 us
    pallas_call x1, Pallas kernels, transitions_of(): pl.pallas_call(kernel, grid=(steps,), in_specs=[smem(), pl.BlockSpec((chu...  13 us
    ppermute x9, waiting for transfers between devices, swapped(): lax.ppermute(array, 'tm', [(i, i ^ distance) for i in range(devices)])  11.9 us
    all_to_all x1, starting transfers between devices, local(): lax.all_to_all(partial.reshape(devices, day_count, factors), 'tm', 0, 0,...  7.39 us
    ppermute x3, starting transfers between devices, local(): arrived = lax.ppermute(moved, 'tm', pairs)  4.95 us
    unnamed x26, local copies, waits for them, and re-layouts  4.29 us
    pallas_call x1, Pallas kernels, finish(): pl.pallas_call(kernel, in_specs=[smem()] + vmem(count + 3) + hbm(6), out_...  2.73 us
    pallas_call x1, Pallas kernels, partial_drive(): pl.pallas_call(kernel, in_specs=[smem()] + hbm(6), out_specs=pl.BlockSpec...  1.5 us
  transfers between devices with their start and end apart: 13, of which 7 were waited for; matrix products, arithmetic and copies ran while one was open for 0% of the time, Pallas kernels for 24%

profile of v2, /device:TPU:0, one launch (start us, length us, event | category | flops | bytes accessed | tf_op | source)
XLA Modules:
  0.0 67.4 jit_solution(11554042222671458000)
XLA Ops:
  0.6 0.0 copy-start.11
  0.6 0.0 copy-start
  0.7 0.9 %copy-done = bf16[64,1024]{1,0:T(8,128)(2,1)S(1)} copy-done((bf16[64,1024]{1,0:T(8,128)(2,1)S(1)}, bf16[64,1024]{1,0:T(8,128)(2,1)}, u32[]{:S(2)}) %copy-start) | copy-done | bytes 131096
  1.6 0.8 %copy-done.2 = f32[16384]{0:T(1024)S(1)} copy-done((f32[16384]{0:T(1024)S(1)}, f32[16384]{0:T(1024)}, u32[]{:S(2)}) %copy-start.2) | copy-done | bytes 65560
  2.4 0.8 %copy-done.4 = s32[16384]{0:T(1024)S(1)} copy-done((s32[16384]{0:T(1024)S(1)}, s32[16384]{0:T(1024)}, u32[]{:S(2)}) %copy-start.4) | copy-done | bytes 65560
  3.2 0.8 %copy-done.6 = s32[16384]{0:T(1024)S(1)} copy-done((s32[16384]{0:T(1024)S(1)}, s32[16384]{0:T(1024)}, u32[]{:S(2)}) %copy-start.6) | copy-done | bytes 65560
  4.1 0.8 %copy-done.8 = s32[16384]{0:T(1024)S(1)} copy-done((s32[16384]{0:T(1024)S(1)}, s32[16384]{0:T(1024)}, u32[]{:S(2)}) %copy-start.8) | copy-done | bytes 65560
  4.9 1.5 %partial_drive.1 = f32[64,256]{1,0:T(8,128)S(1)} custom-call(s32[1]{0:T(128)} %bitcast.index_ref, bf16[64,1024]{1,0:T(8,128)(2,1)S(1)} %copy-done, bf16[16384,256]{1,0:T(8,128)(2,1)} %refs_8_.1, f32[1,16384]{1,0:T(1,128)S(1)} %bitcast.11, s32[1,16384]{1,0:T(1,128)S(1)} %bitcast.14, s32[1,16384]{1,0:T(1,128)S(1)} %bitcast.17, s32[1,16384]{1,0:T(1,128)S(1)} %bitcast.20), custom_call_target="tpu_custom_call" | custom-call | flops 33554432 | bytes 1048576 | tf_op jit(solution)/shard_map/partial_drive/pallas_call | solution.py:97
  6.4 0.7 reshape.27
  7.1 7.4 %all-to-all-start = ((f32[16,4,256]{2,1,0:T(4,128)}), f32[16,4,256]{2,1,0:T(4,128)S(1)}, u32[]{:S(2)}, u32[]{:S(2)}) async-start(f32[16,4,256]{2,1,0:T(4,128)} %reshape.27), calls=%async_computation | async-start | bytes 131072 | tf_op jit(solution)/shard_map/all_to_all | solution.py:495
  14.5 0.0 copy-start.12
  14.6 13.0 %transitions.1 = (f32[4,256,256]{2,1,0:T(8,128)S(1)}, f32[4,256,256]{2,1,0:T(8,128)S(1)}, bf16[256,256]{1,0:T(8,128)(2,1)S(1)}, f32[1,256]{1,0:T(1,128)S(1)}) custom-call(s32[1]{0:T(128)S(6)} %mul.3.day_ref, bf16[16384,256]{1,0:T(8,128)(2,1)} %refs_8_.1, f32[1,16384]{1,0:T(1,128)S(1)} %bitcast.12, s32[1,16384]{1,0:T(1,128)S(1)} %bitcast.15, ...), custom_call_target="tpu_custom_call" | custom-call | flops 8589934592 | bytes 10485760 | tf_op jit(solution)/shard_map/transitions/pallas_call | solution.py:179
  27.6 0.0 copy-start.1
  27.6 0.5 collective-permute-start
  28.0 0.0 all-to-all-done.terms_ref
  28.0 0.8 %own_states.1 = (f32[4,256]{1,0:T(4,128)S(1)}, f32[2,256]{1,0:T(2,128)S(1)}) custom-call(f32[16,4,256]{2,1,0:T(4,128)S(1)} %all-to-all-done.terms_ref, f32[4,256,256]{2,1,0:T(8,128)S(1)} %get-tuple-element.23.step_ref, bf16[256,256]{1,0:T(8,128)(2,1)S(1)} %copy-done.10, f32[1,256]{1,0:T(1,128)S(1)} %get-tuple-element.24.diag_ref), custom_call_target="tpu_custom_call" | custom-call | flops 10485760 | bytes 1048576 | tf_op jit(solution)/shard_map/own_states/pallas_call | solution.py:234
  28.9 0.1 collective-permute-start.1
  29.0 1.0 %collective-permute-done.1.other_ref.refs_3_ = f32[2,256]{1,0:T(2,128)S(1)} collective-permute-done((f32[2,256]{1,0:T(2,128)S(1)}, f32[2,256]{1,0:T(2,128)S(1)}, u32[]{:S(2)}, u32[]{:S(2)}) %collective-permute-start.1) | collective-permute-done | bytes 2080 | tf_op jit(solution)/shard_map/ppermute | solution.py:491
  30.1 0.0 collective-permute-done.rest_ref.refs_2_
  30.1 0.3 combined.2
  30.4 1.8 %collective-permute-start.2 = (bf16[256,256]{1,0:T(8,128)(2,1)S(1)}, bf16[256,256]{1,0:T(8,128)(2,1)S(1)}, u32[]{:S(2)}, u32[]{:S(2)}) collective-permute-start(bf16[256,256]{1,0:T(8,128)(2,1)S(1)} %get-tuple-element.29), channel_id=1, source_target_pairs={{0,2},{1,3},{2,0},{3,1},{4,6},{5,7},{6,4},{7,5},{8,10},{9,11},{10,... | collective-permute-start | bytes 393224 | tf_op jit(solution)/shard_map/ppermute | solution.py:491
  32.2 0.3 collective-permute-start.3
  32.5 3.7 %collective-permute-done.3.other_ref.refs_5_ = f32[2,256]{1,0:T(2,128)S(1)} collective-permute-done((f32[2,256]{1,0:T(2,128)S(1)}, f32[2,256]{1,0:T(2,128)S(1)}, u32[]{:S(2)}, u32[]{:S(2)}) %collective-permute-start.3) | collective-permute-done | bytes 2080 | tf_op jit(solution)/shard_map/ppermute | solution.py:491
  36.2 0.0 collective-permute-done.2.rest_ref.refs_4_
  36.2 1.0 %combined.3 = (f32[256,256]{1,0:T(8,128)S(1)}, bf16[256,256]{1,0:T(8,128)(2,1)}, f32[2,256]{1,0:T(2,128)S(1)}) custom-call(s32[1]{0:T(128)} %bitcast.1.upper_ref.refs_1_, f32[256,256]{1,0:T(8,128)S(1)} %get-tuple-element.27.mine_ref, f32[2,256]{1,0:T(2,128)S(1)} %get-tuple-element.28.packet_ref, ...), custom_call_target="tpu_custom_call" | custom-call | flops 201326592 | bytes 1048576 | tf_op jit(solution)/shard_map/combined/pallas_call | solution.py:272
  37.2 3.6 %collective-permute-start.4 = (f32[1,256]{1,0:T(1,128)S(1)}, f32[1,256]{1,0:T(1,128)S(1)}, u32[]{:S(2)}, u32[]{:S(2)}) collective-permute-start(f32[1,256]{1,0:T(1,128)S(1)} %slice.7), channel_id=1, source_target_pairs={{0,4},{1,5},{2,6},{3,7},{16,20},{17,21},{18,22},{19,23}} | collective-permute-start | bytes 3080 | tf_op jit(solution)/shard_map/ppermute | solution.py:521
  40.9 1.3 %collective-permute-done.4.state_ref = f32[1,256]{1,0:T(1,128)S(1)} collective-permute-done((f32[1,256]{1,0:T(1,128)S(1)}, f32[1,256]{1,0:T(1,128)S(1)}, u32[]{:S(2)}, u32[]{:S(2)}) %collective-permute-start.4) | collective-permute-done | bytes 1056 | tf_op jit(solution)/shard_map/ppermute | solution.py:521
  42.2 0.2 advanced.2
  42.3 0.7 collective-permute-start.5
  43.0 0.0 collective-permute-done.5
  43.0 0.2 advanced.3
  43.2 0.7 collective-permute-start.6
  43.9 0.8 %prefixed.1 = (bf16[256,1024]{1,0:T(8,128)(2,1)S(1)}, bf16[256,1024]{1,0:T(8,128)(2,1)S(1)}, f32[1,1024]{1,0:T(1,128)S(1)}) custom-call(s32[1]{0:T(128)} %bitcast.2.upper_ref.refs_0_, s32[1]{0:T(128)} %bitcast.1.upper_ref.refs_1_, bf16[256,256]{1,0:T(8,128)(2,1)S(1)} %collective-permute-done.rest_ref.refs_2_, ...), custom_call_target="tpu_custom_call" | custom-call | flops 603979776 | bytes 3145728 | tf_op jit(solution)/shard_map/prefixed/pallas_call | solution.py:333
  44.7 0.0 collective-permute-done.6.arrived_ref
  44.7 0.3 filtered.1
  45.0 0.1 collective-permute-start.7
  45.1 1.2 %collective-permute-done.7 = f32[1,4,256]{2,1,0:T(4,128)S(1)} collective-permute-done((f32[1,4,256]{2,1,0:T(4,128)S(1)}, f32[1,4,256]{2,1,0:T(4,128)S(1)}, u32[]{:S(2)}, u32[]{:S(2)}) %collective-permute-start.7) | collective-permute-done | bytes 4128 | tf_op jit(solution)/shard_map/ppermute | solution.py:491
  46.2 1.8 %collective-permute-start.8 = (f32[2,4,256]{2,1,0:T(4,128)S(1)}, f32[2,4,256]{2,1,0:T(4,128)S(1)}, u32[]{:S(2)}, u32[]{:S(2)}) collective-permute-start(f32[2,4,256]{2,1,0:T(4,128)S(1)} %pad_maximum_fusion.1), channel_id=1, source_target_pairs={{0,2},{1,3},{2,0},{3,1},{4,6},{5,7},{6,4},{7,5},{8,10},{9,11},{10,... | collective-permute-start | bytes 24584 | tf_op jit(solution)/shard_map/ppermute | solution.py:491
  48.0 1.9 %collective-permute-done.8 = f32[2,4,256]{2,1,0:T(4,128)S(1)} collective-permute-done((f32[2,4,256]{2,1,0:T(4,128)S(1)}, f32[2,4,256]{2,1,0:T(4,128)S(1)}, u32[]{:S(2)}, u32[]{:S(2)}) %collective-permute-start.8) | collective-permute-done | bytes 8224 | tf_op jit(solution)/shard_map/ppermute | solution.py:491
  49.9 4.2 %collective-permute-start.9 = (f32[4,4,256]{2,1,0:T(4,128)S(1)}, f32[4,4,256]{2,1,0:T(4,128)S(1)}, u32[]{:S(2)}, u32[]{:S(2)}) collective-permute-start(f32[4,4,256]{2,1,0:T(4,128)S(1)} %pad_maximum_fusion.refs_0_), channel_id=1, source_target_pairs={{0,4},{1,5},{2,6},{3,7},{4,0},{5,1},{6,2},{7,3},{8,12},{9,13},{10,... | collective-permute-start | bytes 49160 | tf_op jit(solution)/shard_map/ppermute | solution.py:491
  54.1 5.1 %collective-permute-start.10 = (f32[4,4,256]{2,1,0:T(4,128)S(1)}, f32[4,4,256]{2,1,0:T(4,128)S(1)}, u32[]{:S(2)}, u32[]{:S(2)}) collective-permute-start(f32[4,4,256]{2,1,0:T(4,128)S(1)} %pad_maximum_fusion.refs_0_), channel_id=1, source_target_pairs={{0,8},{1,9},{2,10},{3,11},{4,12},{5,13},{6,14},{7,15},{8,0},{9,1},... | collective-permute-start | bytes 49160 | tf_op jit(solution)/shard_map/ppermute | solution.py:491
  59.1 0.0 collective-permute-start.11
  59.1 0.0 copy-done.12
  59.1 1.4 %smoother_powers.1 = (bf16[5,256,256]{2,1,0:T(8,128)(2,1)S(1)}, bf16[5,256,256]{2,1,0:T(8,128)(2,1)S(1)}) custom-call(f32[256,256]{1,0:T(8,128)S(1)} %copy-done.12), custom_call_target="tpu_custom_call" | custom-call | flops 402653184 | bytes 2097152 | tf_op jit(solution)/shard_map/smoother_powers/pallas_call | solution.py:381
  60.5 0.0 collective-permute-done.9.refs_1_
  60.5 0.3 collective-permute-done.10.refs_2_
  60.8 3.8 %collective-permute-done.11.refs_3_ = f32[4,4,256]{2,1,0:T(4,128)S(1)} collective-permute-done((f32[4,4,256]{2,1,0:T(4,128)S(1)}, f32[4,4,256]{2,1,0:T(4,128)S(1)}, u32[]{:S(2)}, u32[]{:S(2)}) %collective-permute-start.11) | collective-permute-done | bytes 16416 | tf_op jit(solution)/shard_map/ppermute | solution.py:491
  64.6 2.7 %finish.1 = (f32[4,256]{1,0:T(4,128)}, bf16[64,1024]{1,0:T(8,128)(2,1)}) custom-call(s32[1]{0:T(128)} %bitcast.index_ref, f32[4,4,256]{2,1,0:T(4,128)S(1)} %pad_maximum_fusion.refs_0_, f32[4,4,256]{2,1,0:T(4,128)S(1)} %collective-permute-done.9.refs_1_, f32[4,4,256]{2,1,0:T(4,128)S(1)} %collective-permute-done.10.refs_2_, ...), custom_call_target="tpu_custom_call" | custom-call | flops 33554432 | bytes 2097152 | tf_op jit(solution)/shard_map/finish/pallas_call | solution.py:458
  (21 shorter events, 0.1 us)
Async XLA Ops:
  0.6 13.9 %copy-start.11 = (f32[256]{0:T(256)S(1)}, f32[256]{0:T(256)}, u32[]{:S(2)}) copy-start(f32[256]{0:T(256)} %param.15) | copy-start | bytes 3076
  0.6 0.9 %copy-start = (bf16[64,1024]{1,0:T(8,128)(2,1)S(1)}, bf16[64,1024]{1,0:T(8,128)(2,1)}, u32[]{:S(2)}) copy-start(bf16[64,1024]{1,0:T(8,128)(2,1)} %refs_7_.1) | copy-start | bytes 393220
  1.6 0.8 %copy-start.2 = (f32[16384]{0:T(1024)S(1)}, f32[16384]{0:T(1024)}, u32[]{:S(2)}) copy-start(f32[16384]{0:T(1024)} %param.11) | copy-start | bytes 196612
  2.4 0.8 %copy-start.4 = (s32[16384]{0:T(1024)S(1)}, s32[16384]{0:T(1024)}, u32[]{:S(2)}) copy-start(s32[16384]{0:T(1024)} %param.12) | copy-start | bytes 196612
  3.2 0.8 %copy-start.6 = (s32[16384]{0:T(1024)S(1)}, s32[16384]{0:T(1024)}, u32[]{:S(2)}) copy-start(s32[16384]{0:T(1024)} %param.13) | copy-start | bytes 196612
  4.1 0.8 %copy-start.8 = (s32[16384]{0:T(1024)S(1)}, s32[16384]{0:T(1024)}, u32[]{:S(2)}) copy-start(s32[16384]{0:T(1024)} %param.14) | copy-start | bytes 196612
  4.9 9.6 %copy-start.3 = (f32[16384]{0:T(1024)S(1)}, f32[16384]{0:T(1024)}, u32[]{:S(2)}) copy-start(f32[16384]{0:T(1024)} %param.11) | copy-start | bytes 196612
  4.9 9.6 %copy-start.5 = (s32[16384]{0:T(1024)S(1)}, s32[16384]{0:T(1024)}, u32[]{:S(2)}) copy-start(s32[16384]{0:T(1024)} %param.12) | copy-start | bytes 196612
  4.9 9.6 %copy-start.7 = (s32[16384]{0:T(1024)S(1)}, s32[16384]{0:T(1024)}, u32[]{:S(2)}) copy-start(s32[16384]{0:T(1024)} %param.13) | copy-start | bytes 196612
  4.9 9.6 %copy-start.9 = (s32[16384]{0:T(1024)S(1)}, s32[16384]{0:T(1024)}, u32[]{:S(2)}) copy-start(s32[16384]{0:T(1024)} %param.14) | copy-start | bytes 196612
  4.9 9.6 %copy-start.10 = (bf16[256,256]{1,0:T(8,128)(2,1)S(1)}, bf16[256,256]{1,0:T(8,128)(2,1)}, u32[]{:S(2)}) copy-start(bf16[256,256]{1,0:T(8,128)(2,1)} %gain_ref.1) | copy-start | bytes 393220
  7.1 20.9 %all-to-all-start = ((f32[16,4,256]{2,1,0:T(4,128)}), f32[16,4,256]{2,1,0:T(4,128)S(1)}, u32[]{:S(2)}, u32[]{:S(2)}) async-start(f32[16,4,256]{2,1,0:T(4,128)} %reshape.27), calls=%async_computation | async-start | bytes 131072 | tf_op jit(solution)/shard_map/all_to_all | solution.py:495
  14.5 44.6 %copy-start.12 = (f32[256,256]{1,0:T(8,128)S(1)}, f32[256,256]{1,0:T(8,128)}, u32[]{:S(2)}) copy-start(f32[256,256]{1,0:T(8,128)} %in_ref.1) | copy-start | bytes 786436
  27.6 37.1 %copy-start.1 = (bf16[64,1024]{1,0:T(8,128)(2,1)S(1)}, bf16[64,1024]{1,0:T(8,128)(2,1)}, u32[]{:S(2)}) copy-start(bf16[64,1024]{1,0:T(8,128)(2,1)} %refs_7_.1) | copy-start | bytes 393220
  27.6 2.5 %collective-permute-start = (bf16[256,256]{1,0:T(8,128)(2,1)S(1)}, bf16[256,256]{1,0:T(8,128)(2,1)S(1)}, u32[]{:S(2)}, u32[]{:S(2)}) collective-permute-start(bf16[256,256]{1,0:T(8,128)(2,1)S(1)} %get-tuple-element.26), channel_id=1, source_target_pairs={{0,1},{1,0},{2,3},{3,2},{4,5},{5,4},{6,7},{7,6},{8,9},{9,8},{10,11... | collective-permute-start | bytes 393224 | tf_op jit(solution)/shard_map/ppermute | solution.py:491
  28.9 1.2 %collective-permute-start.1 = (f32[2,256]{1,0:T(2,128)S(1)}, f32[2,256]{1,0:T(2,128)S(1)}, u32[]{:S(2)}, u32[]{:S(2)}) collective-permute-start(f32[2,256]{1,0:T(2,128)S(1)} %get-tuple-element.25.packet_ref), channel_id=1, source_target_pairs={{0,1},{1,0},{2,3},{3,2},{4,5},{5,4},{6,7},{7,6},{8,9},{9,8},{10,11... | collective-permute-start | bytes 6152 | tf_op jit(solution)/shard_map/ppermute | solution.py:491
  30.4 5.8 %collective-permute-start.2 = (bf16[256,256]{1,0:T(8,128)(2,1)S(1)}, bf16[256,256]{1,0:T(8,128)(2,1)S(1)}, u32[]{:S(2)}, u32[]{:S(2)}) collective-permute-start(bf16[256,256]{1,0:T(8,128)(2,1)S(1)} %get-tuple-element.29), channel_id=1, source_target_pairs={{0,2},{1,3},{2,0},{3,1},{4,6},{5,7},{6,4},{7,5},{8,10},{9,11},{10,... | collective-permute-start | bytes 393224 | tf_op jit(solution)/shard_map/ppermute | solution.py:491
  32.2 4.0 %collective-permute-start.3 = (f32[2,256]{1,0:T(2,128)S(1)}, f32[2,256]{1,0:T(2,128)S(1)}, u32[]{:S(2)}, u32[]{:S(2)}) collective-permute-start(f32[2,256]{1,0:T(2,128)S(1)} %get-tuple-element.28.packet_ref), channel_id=1, source_target_pairs={{0,2},{1,3},{2,0},{3,1},{4,6},{5,7},{6,4},{7,5},{8,10},{9,11},{10,... | collective-permute-start | bytes 6152 | tf_op jit(solution)/shard_map/ppermute | solution.py:491
  37.2 4.9 %collective-permute-start.4 = (f32[1,256]{1,0:T(1,128)S(1)}, f32[1,256]{1,0:T(1,128)S(1)}, u32[]{:S(2)}, u32[]{:S(2)}) collective-permute-start(f32[1,256]{1,0:T(1,128)S(1)} %slice.7), channel_id=1, source_target_pairs={{0,4},{1,5},{2,6},{3,7},{16,20},{17,21},{18,22},{19,23}} | collective-permute-start | bytes 3080 | tf_op jit(solution)/shard_map/ppermute | solution.py:521
  42.3 0.7 collective-permute-start.5
  43.2 1.5 %collective-permute-start.6 = (f32[1,256]{1,0:T(1,128)S(1)}, f32[1,256]{1,0:T(1,128)S(1)}, u32[]{:S(2)}, u32[]{:S(2)}) collective-permute-start(f32[1,256]{1,0:T(1,128)S(1)} %advanced.3), channel_id=1, source_target_pairs={{8,12},{9,13},{10,14},{11,15},{24,28},{25,29},{26,30},{27,31}} | collective-permute-start | bytes 3080 | tf_op jit(solution)/shard_map/ppermute | solution.py:521
  45.0 1.2 %collective-permute-start.7 = (f32[1,4,256]{2,1,0:T(4,128)S(1)}, f32[1,4,256]{2,1,0:T(4,128)S(1)}, u32[]{:S(2)}, u32[]{:S(2)}) collective-permute-start(f32[1,4,256]{2,1,0:T(4,128)S(1)} %bitcast.23), channel_id=1, source_target_pairs={{0,1},{1,0},{2,3},{3,2},{4,5},{5,4},{6,7},{7,6},{8,9},{9,8},{10,11... | collective-permute-start | bytes 12296 | tf_op jit(solution)/shard_map/ppermute | solution.py:491
  46.2 3.7 %collective-permute-start.8 = (f32[2,4,256]{2,1,0:T(4,128)S(1)}, f32[2,4,256]{2,1,0:T(4,128)S(1)}, u32[]{:S(2)}, u32[]{:S(2)}) collective-permute-start(f32[2,4,256]{2,1,0:T(4,128)S(1)} %pad_maximum_fusion.1), channel_id=1, source_target_pairs={{0,2},{1,3},{2,0},{3,1},{4,6},{5,7},{6,4},{7,5},{8,10},{9,11},{10,... | collective-permute-start | bytes 24584 | tf_op jit(solution)/shard_map/ppermute | solution.py:491
  49.9 10.6 %collective-permute-start.9 = (f32[4,4,256]{2,1,0:T(4,128)S(1)}, f32[4,4,256]{2,1,0:T(4,128)S(1)}, u32[]{:S(2)}, u32[]{:S(2)}) collective-permute-start(f32[4,4,256]{2,1,0:T(4,128)S(1)} %pad_maximum_fusion.refs_0_), channel_id=1, source_target_pairs={{0,4},{1,5},{2,6},{3,7},{4,0},{5,1},{6,2},{7,3},{8,12},{9,13},{10,... | collective-permute-start | bytes 49160 | tf_op jit(solution)/shard_map/ppermute | solution.py:491
  54.1 6.8 %collective-permute-start.10 = (f32[4,4,256]{2,1,0:T(4,128)S(1)}, f32[4,4,256]{2,1,0:T(4,128)S(1)}, u32[]{:S(2)}, u32[]{:S(2)}) collective-permute-start(f32[4,4,256]{2,1,0:T(4,128)S(1)} %pad_maximum_fusion.refs_0_), channel_id=1, source_target_pairs={{0,8},{1,9},{2,10},{3,11},{4,12},{5,13},{6,14},{7,15},{8,0},{9,1},... | collective-permute-start | bytes 49160 | tf_op jit(solution)/shard_map/ppermute | solution.py:491
  59.1 5.5 %collective-permute-start.11 = (f32[4,4,256]{2,1,0:T(4,128)S(1)}, f32[4,4,256]{2,1,0:T(4,128)S(1)}, u32[]{:S(2)}, u32[]{:S(2)}) collective-permute-start(f32[4,4,256]{2,1,0:T(4,128)S(1)} %pad_maximum_fusion.refs_0_), channel_id=1, source_target_pairs={{0,12},{1,13},{2,14},{3,15},{4,8},{5,9},{6,10},{7,11},{8,4},{9,5},... | collective-permute-start | bytes 49160 | tf_op jit(solution)/shard_map/ppermute | solution.py:491

commit v3 on v2

--- a/solution.py
+++ b/solution.py
@@ -13,8 +13,8 @@
 POWERS = 5
 
 
-def params(**more):
-    return pltpu.CompilerParams(vmem_limit_bytes=48 << 20, **more)
+def params(mebibytes=48, **more):
+    return pltpu.CompilerParams(vmem_limit_bytes=mebibytes << 20, **more)
 
 
 def cost(flops, nbytes):
@@ -60,8 +60,9 @@
     return (day >= start) & (day < stop) & (lax.rem(day, 7) != off)
 
 
-def partial_drive(index, series, loadings, tables):
+def partial_drive(index, devices, series, loadings, tables):
     days, own = series.shape
+    day_count = days // devices
     factors = loadings.shape[1]
 
     def kernel(
@@ -92,13 +93,15 @@
         weights = jnp.where(active, prec_ref[...], 0.0)
         weighted = (weights * series_ref[...].astype(F32)).astype(BF16)
         copies[5].wait()
-        out_ref[...] = mul(weighted, load_ref[...])
+        drive = mul(weighted, load_ref[...])
+        for p in range(devices):
+            out_ref[p] = drive[p * day_count : (p + 1) * day_count]
 
     return pl.pallas_call(
         kernel,
         in_specs=[smem()] + hbm(6),
         out_specs=pl.BlockSpec(memory_space=VMEM),
-        out_shape=shape(days, factors),
+        out_shape=shape(devices, day_count, factors),
         scratch_shapes=[
             pltpu.VMEM((days, own), BF16),
             pltpu.VMEM((own, factors), BF16),
@@ -108,7 +111,7 @@
             pltpu.VMEM((1, own), jnp.int32),
             pltpu.SemaphoreType.DMA((6,)),
         ],
-        compiler_params=params(),
+        compiler_params=params(63),
         cost_estimate=cost(2 * days * own * factors, 1 << 20),
         name="partial_drive",
     )(index, series, loadings, *tables)
@@ -121,7 +124,7 @@
 
     def kernel(
         day_ref, load_ref, prec_hbm, start_hbm, stop_hbm, off_hbm, decay_hbm, gain_hbm,
-        step_ref, run_ref, rest_ref, diag_ref,
+        step_ref, run_ref, last_ref, rest_ref, diag_ref,
         acc, prec_ref, start_ref, stop_ref, off_ref, decay_ref, gain_ref, sems,
     ):
         step = pl.program_id(0)
@@ -168,10 +171,12 @@
                     damped, gain_ref[...], (((1,), (1,)), ((), ())), preferred_element_type=F32
                 )
                 step_ref[d] = diagonal - pulled
-            run_ref[0] = step_ref[0]
+            running = step_ref[0]
             for d in range(1, day_count):
-                run_ref[d] = product(run_ref[d - 1], split(step_ref[d]))
-            last = run_ref[day_count - 1]
+                run_ref[d - 1] = running
+                running = product(running, split(step_ref[d]))
+            last = running
+            last_ref[...] = last
             rest_ref[...] = jnp.where(same, 0.0, last).astype(BF16)
             diag_ref[...] = jnp.sum(jnp.where(same, last, 0.0), axis=0, keepdims=True)
 
@@ -182,13 +187,15 @@
         in_specs=[smem(), pl.BlockSpec((chunk, factors), lambda i: (i, 0))] + hbm(6),
         out_specs=[
             cube,
-            cube,
+            pl.BlockSpec((day_count - 1, factors, factors), lambda i: (0, 0, 0)),
+            pl.BlockSpec((factors, factors), lambda i: (0, 0)),
             pl.BlockSpec((factors, factors), lambda i: (0, 0)),
             pl.BlockSpec((1, factors), lambda i: (0, 0)),
         ],
         out_shape=[
             shape(day_count, factors, factors),
-            shape(day_count, factors, factors),
+            shape(day_count - 1, factors, factors),
+            shape(factors, factors),
             shape(factors, factors, dtype=BF16),
             shape(1, factors),
         ],
@@ -202,7 +209,7 @@
             pltpu.VMEM((factors, factors), BF16),
             pltpu.SemaphoreType.DMA((6,)),
         ],
-        compiler_params=params(dimension_semantics=("arbitrary",)),
+        compiler_params=params(48, dimension_semantics=("arbitrary",)),
         cost_estimate=cost(2 * day_count * providers * factors * factors, 10 << 20),
         name="transitions",
     )(first_day, loadings, *tables, decay, gain)
@@ -246,49 +253,80 @@
     return rest.astype(F32) + jnp.where(same, diag, 0.0)
 
 
-def combined(upper, matrix, packet, other_rest, other_packet):
+PACKED = 16
+
+
+def unpacked(packed_ref, same):
+    factors = packed_ref.shape[1]
+    rows = packed_ref[factors:].astype(F32)
+    matrix = rebuilt(packed_ref[:factors], rows[2:3] + rows[3:4], same)
+    return matrix, rows[0:1] + rows[1:2]
+
+
+def combine_into(low, low_tail, high, high_tail, same, map_ref, tail_ref, packed_ref):
+    factors = low.shape[0]
+    high = split(high)
+    total = None if map_ref is None else product(low, high)
+    tail = product(low_tail, high) + high_tail
+    if map_ref is not None:
+        map_ref[...] = total
+    tail_ref[...] = tail
+    if packed_ref is not None:
+        packed_ref[:factors] = jnp.where(same, 0.0, total).astype(BF16)
+        diag = jnp.sum(jnp.where(same, total, 0.0), axis=0, keepdims=True)
+        rows = [*split(tail), *split(diag), jnp.zeros((PACKED - 4, factors), BF16)]
+        packed_ref[factors:] = jnp.concatenate(rows, 0)
+
+
+def combined(upper, matrix, tail, other, last, need_map):
     factors = matrix.shape[0]
 
-    def kernel(upper_ref, mine_ref, packet_ref, rest_ref, other_ref, map_ref, part_ref, next_ref):
+    def kernel(upper_ref, mine_ref, tail_ref, *refs):
+        others, outs = refs[: len(other)], refs[len(other) :]
+        outs = list(outs)
+        next_ref = outs.pop(0)
+        map_ref = outs.pop(0) if need_map else None
+        packed_ref = None if last else outs.pop(0)
         same = eye(factors)
-        other = rebuilt(rest_ref[...], other_ref[1:2], same)
-
-        def write(low, low_tail, high, high_tail):
-            high = split(high)
-            total = product(low, high)
-            map_ref[...] = total
-            part_ref[...] = jnp.where(same, 0.0, total).astype(BF16)
-            next_ref[0:1] = product(low_tail, high) + high_tail
-            next_ref[1:2] = jnp.sum(jnp.where(same, total, 0.0), axis=0, keepdims=True)
+        if len(other) == 2:
+            theirs = rebuilt(others[0][...], others[1][1:2], same)
+            their_tail = others[1][0:1]
+        else:
+            theirs, their_tail = unpacked(others[0], same)
 
         @pl.when(upper_ref[0] == 1)
         def _():
-            write(other, other_ref[0:1], mine_ref[...], packet_ref[0:1])
+            combine_into(
+                theirs, their_tail, mine_ref[...], tail_ref[0:1], same, map_ref, next_ref, packed_ref
+            )
 
         @pl.when(upper_ref[0] == 0)
         def _():
-            write(mine_ref[...], packet_ref[0:1], other, other_ref[0:1])
-
-    return pl.pallas_call(
-        kernel,
-        in_specs=[smem()] + vmem(4),
-        out_specs=vmem(3),
-        out_shape=[
-            shape(factors, factors),
-            shape(factors, factors, dtype=BF16),
-            shape(2, factors),
-        ],
+            combine_into(
+                mine_ref[...], tail_ref[0:1], theirs, their_tail, same, map_ref, next_ref, packed_ref
+            )
+
+    out_shape = [shape(1, factors)]
+    if need_map:
+        out_shape.append(shape(factors, factors))
+    if not last:
+        out_shape.append(shape(factors + PACKED, factors, dtype=BF16))
+    return pl.pallas_call(
+        kernel,
+        in_specs=[smem()] + vmem(2 + len(other)),
+        out_specs=vmem(len(out_shape)),
+        out_shape=out_shape,
         compiler_params=params(),
         cost_estimate=cost(12 * factors**3, 1 << 20),
         name="combined",
-    )(upper, matrix, packet, other_rest, other_packet)
-
-
-def advanced(state, matrix, packet):
+    )(upper, matrix, tail, *other)
+
+
+def advanced(state, matrix, tail):
     factors = matrix.shape[0]
 
-    def kernel(state_ref, matrix_ref, packet_ref, out_ref):
-        out_ref[...] = product(state_ref[...], split(matrix_ref[...])) + packet_ref[0:1]
+    def kernel(state_ref, matrix_ref, tail_ref, out_ref):
+        out_ref[...] = product(state_ref[...], split(matrix_ref[...])) + tail_ref[...]
 
     return pl.pallas_call(
         kernel,
@@ -298,17 +336,20 @@
         compiler_params=params(),
         cost_estimate=cost(12 * factors**2, 1 << 18),
         name="advanced",
-    )(state, matrix, packet)
-
-
-def prefixed(uppers, levels, running, states):
+    )(state, matrix, tail)
+
+
+def prefixed(uppers, levels, running, last, states):
     day_count, factors = states.shape
     count = len(levels)
 
+    flat = [a for level in levels for a in level]
+
     def kernel(*refs):
         upper_refs = refs[:count]
-        parts = refs[count : 3 * count]
-        run_ref, states_ref, high_ref, low_ref, add_ref, work, tail = refs[3 * count :]
+        parts = list(refs[count : count + len(flat)])
+        run_ref, last_ref, states_ref, high_ref, low_ref, add_ref, work, tail = refs[count + len(flat) :]
+        parts = [[parts.pop(0) for _ in level] for level in levels]
         same = eye(factors)
         work[...] = jnp.where(same, 1.0, 0.0)
         tail[...] = jnp.zeros_like(tail)
@@ -316,13 +357,17 @@
 
             @pl.when(upper_refs[level][0] == 1)
             def _():
-                packet = parts[2 * level + 1]
-                step = split(rebuilt(parts[2 * level][...], packet[1:2], same))
+                if len(parts[level]) == 2:
+                    rest, packet = parts[level]
+                    matrix, add = rebuilt(rest[...], packet[1:2], same), packet[0:1]
+                else:
+                    matrix, add = unpacked(parts[level][0], same)
+                step = split(matrix)
                 work[...] = product(work[...], step)
-                tail[...] = product(tail[...], step) + packet[0:1]
+                tail[...] = product(tail[...], step) + add
 
         for d in range(day_count):
-            step = split(run_ref[d])
+            step = split(run_ref[d] if d < day_count - 1 else last_ref[...])
             place = slice(d * factors, (d + 1) * factors)
             high, low = split(product(work[...], step))
             high_ref[:, place] = high
@@ -332,7 +377,7 @@
     wide = day_count * factors
     return pl.pallas_call(
         kernel,
-        in_specs=[smem()] * count + vmem(2 * count + 2),
+        in_specs=[smem()] * count + vmem(len(flat) + 3),
         out_specs=vmem(3),
         out_shape=[
             shape(factors, wide, dtype=BF16),
@@ -343,7 +388,7 @@
         compiler_params=params(),
         cost_estimate=cost(36 * factors**3, 3 << 20),
         name="prefixed",
-    )(*uppers, *[a for level in levels for a in level], running, states)
+    )(*uppers, *flat, running, last, states)
 
 
 def filtered_of(state, arrived, high, low, add):
@@ -389,20 +434,17 @@
     )(smoother)
 
 
-def finish(index, day_count, pieces, powers, decay, series, loadings, tables):
+def finish(index, day_count, gathered, powers, decay, series, loadings, tables):
     days, own = series.shape
     factors = loadings.shape[1]
     stride = 2 ** (POWERS - 1)
     blocks = days // stride
-    count = len(pieces)
-
-    def kernel(index_ref, *refs):
-        piece_refs = refs[:count]
-        (
-            high_ref, low_ref, decay_ref, series_hbm, load_hbm, prec_hbm, start_hbm, stop_hbm,
-            off_hbm, smooth_ref, score_ref, filt, work, series_ref, load_ref, prec_ref, start_ref,
-            stop_ref, off_ref, sems,
-        ) = refs[count:]
+
+    def kernel(
+        index_ref, gathered_ref, high_ref, low_ref, decay_ref, series_hbm, load_hbm, prec_hbm,
+        start_hbm, stop_hbm, off_hbm, smooth_ref, score_ref, filt, work, series_ref, load_ref,
+        prec_ref, start_ref, stop_ref, off_ref, sems,
+    ):
         me = index_ref[0]
         mine = pl.ds(pl.multiple_of(me * own, own), own)
         copies = [
@@ -420,13 +462,8 @@
         ]
         for copy in copies:
             copy.start()
-        block = 0
-        for piece in piece_refs:
-            for b in range(piece.shape[0]):
-                first = (me ^ block) * day_count
-                for d in range(day_count):
-                    filt[pl.ds(first + d, 1), :] = piece[b, d : d + 1]
-                block += 1
+        for m in range(days // day_count):
+            filt[m * day_count : (m + 1) * day_count, :] = gathered_ref[m]
         filtered = filt[...]
         carried = filtered * decay_ref[...]
         carried = jnp.concatenate([jnp.zeros((1, factors), F32), carried[:-1]], 0)
@@ -457,7 +494,7 @@
 
     return pl.pallas_call(
         kernel,
-        in_specs=[smem()] + vmem(count + 3) + hbm(6),
+        in_specs=[smem()] + vmem(4) + hbm(6),
         out_specs=vmem(2),
         out_shape=[shape(day_count, factors), shape(days, own, dtype=BF16)],
         scratch_shapes=[
@@ -474,7 +511,7 @@
         compiler_params=params(),
         cost_estimate=cost(2 * days * own * factors, 2 << 20),
         name="finish",
-    )(index, *pieces, *powers, decay, series, loadings, *tables)
+    )(index, gathered, *powers, decay, series, loadings, *tables)
 
 
 def local(series, loadings, precision, start_day, stop_day, off_day, decay, gain, smoother):
@@ -490,46 +527,47 @@
     def swapped(array, distance):
         return lax.ppermute(array, "tm", [(i, i ^ distance) for i in range(devices)])
 
-    partial = partial_drive(index, series, loadings, tables)
+    partial = partial_drive(index, devices, series, loadings, tables)
     partial, first_day = lax.optimization_barrier((partial, index * day_count))
-    terms = lax.all_to_all(
-        partial.reshape(devices, day_count, factors), "tm", 0, 0, tiled=True
-    )
-    steps, running, rest, diag = transitions_of(first_day, day_count, loadings, tables, decay, gain)
+    terms = lax.all_to_all(partial, "tm", 0, 0, tiled=True)
+    steps, running, mine, rest, diag = transitions_of(first_day, day_count, loadings, tables, decay, gain)
+    rest, terms = lax.optimization_barrier((rest, terms))
     states, packet = own_states(terms, steps, gain, diag)
 
-    group = min(4, devices)
-    matrix = running[day_count - 1]
+    group = min(8, devices)
+    matrix, tail = mine, packet
+    sent = (rest, packet)
     levels, uppers = [], []
     reach = 1
     while reach < group:
-        other_rest = swapped(rest, reach)
-        other_packet = swapped(packet, reach)
+        other = tuple(swapped(a, reach) for a in sent)
         upper = jnp.where((place & reach) != 0, 1, 0).astype(jnp.int32)[None]
-        levels.append((other_rest, other_packet))
+        levels.append(other)
         uppers.append(upper)
-        matrix, rest, packet = combined(upper, matrix, packet, other_rest, other_packet)
+        last = reach * 2 == group
+        if reach == 2:
+            sent, smoother = lax.optimization_barrier((sent, smoother))
+            powers = smoother_powers(smoother)
+            tail, powers = lax.optimization_barrier((tail, powers))
+        need_map = not last or devices // group > 2
+        tail, *rest_of = combined(upper, matrix, tail, other, last, need_map)
+        matrix, sent = (rest_of[0], rest_of[1:]) if need_map else (None, None)
         reach *= 2
 
-    ahead = prefixed(uppers, levels, running, states)
+    ahead = prefixed(uppers, levels, running, mine, states)
     state = jnp.zeros((1, factors), F32)
-    arrived = jnp.zeros((1, factors), F32)
-    for g in range(devices // group - 1):
+    arrived = jnp.where(place // group == 1, swapped(tail, group), 0.0)
+    for g in range(1, devices // group - 1):
         state = state + arrived
-        moved = packet[0:1] if g == 0 else advanced(state, matrix, packet)
+        moved = advanced(state, matrix, tail)
         pairs = [(g * group + j, (g + 1) * group + j) for j in range(group)]
         arrived = lax.ppermute(moved, "tm", pairs)
 
-    pieces = filtered_of(state, arrived, *ahead)[None]
-    reach = 1
-    while reach * 4 < devices:
-        pieces = jnp.concatenate([pieces, swapped(pieces, reach)], 0)
-        reach *= 2
-    pieces = [pieces] + [
-        swapped(pieces, reach * n) for n in range(1, devices // reach)
-    ]
-    powers = smoother_powers(smoother)
-    return tuple(finish(index, day_count, pieces, powers, decay, series, loadings, tables))
+    mine = filtered_of(state, arrived, *ahead)[None]
+    gathered = lax.all_to_all(
+        jnp.broadcast_to(mine, (devices, day_count, factors)), "tm", 0, 0, tiled=True
+    )
+    return tuple(finish(index, day_count, gathered, powers, decay, series, loadings, tables))
 
 
 def solution(mesh):

time: 67.8 us -> 59.1 us (0.87)
  blocking collectives: 0 us -> 12.4 us
  starting transfers between devices: 26.1 us -> 14.1 us
  waiting for transfers between devices: 13.1 us -> 7.19 us
  local copies, waits for them, and re-layouts: 4.96 us -> 2.08 us
    all_to_all x0 -> x1, blocking collectives: none -> 12.4 us  [local(): lax.all_to_all(jnp.broadcast_to(mine, (devices, day_count, factors)), 'tm...]
    ppermute x9 -> x5, starting transfers between devices: 13.7 us -> 6.75 us  [swapped(): lax.ppermute(array, 'tm', [(i, i ^ distance) for i in range(devices)])]
    ppermute x3 -> x0, starting transfers between devices: 4.95 us -> none  [local(): arrived = lax.ppermute(moved, 'tm', pairs)]
    ppermute x9 -> x5, waiting for transfers between devices: 11.9 us -> 7.18 us  [swapped(): lax.ppermute(array, 'tm', [(i, i ^ distance) for i in range(devices)])]
    unnamed x26 -> x20, local copies, waits for them, and re-layouts: 4.29 us -> 2.05 us
    ppermute x3 -> x0, waiting for transfers between devices: 1.29 us -> none  [local(): arrived = lax.ppermute(moved, 'tm', pairs)]
    pallas_call x6 -> x5, Pallas kernels: 5.26 us -> 4.39 us  [the longest x1 2.65 us: finish(): pl.pallas_call(kernel, in_specs=[smem()] + vmem(4) + hbm(6), out_specs=vm...]
  transfers between devices with their start and end apart: 13 -> 6, of which waited for: 7 -> 3; matrix products, arithmetic and copies ran while one was open for 0% -> 0% of each run, Pallas kernels for 24% -> 27%
where the time goes in v3:
time: 59.1 us; the launch traced here: 58.8 us
  Pallas kernels  22.2 us (38%)
  starting transfers between devices  14.1 us (24%)
  blocking collectives  12.4 us (21%)
  waiting for transfers between devices  7.19 us (12%)
  local copies, waits for them, and re-layouts  2.08 us (4%)
  between operations  0.84 us (1%)
    pallas_call x1, Pallas kernels, transitions_of(): pl.pallas_call(kernel, grid=(steps,), in_specs=[smem(), pl.BlockSpec((chu...  13 us
    all_to_all x1, blocking collectives, local(): lax.all_to_all(jnp.broadcast_to(mine, (devices, day_count, factors)), 'tm...  12.4 us
    all_to_all x1, starting transfers between devices, local(): terms = lax.all_to_all(partial, 'tm', 0, 0, tiled=True)  7.4 us
    ppermute x5, waiting for transfers between devices, swapped(): lax.ppermute(array, 'tm', [(i, i ^ distance) for i in range(devices)])  7.18 us
    ppermute x5, starting transfers between devices, swapped(): lax.ppermute(array, 'tm', [(i, i ^ distance) for i in range(devices)])  6.75 us
    pallas_call x1, Pallas kernels, finish(): pl.pallas_call(kernel, in_specs=[smem()] + vmem(4) + hbm(6), out_specs=vm...  2.65 us
    pallas_call x1, Pallas kernels, partial_drive(): pl.pallas_call(kernel, in_specs=[smem()] + hbm(6), out_specs=pl.BlockSpec...  2.17 us
    unnamed x20, local copies, waits for them, and re-layouts  2.05 us
  transfers between devices with their start and end apart: 6, of which 3 were waited for; matrix products, arithmetic and copies ran while one was open for 0% of the time, Pallas kernels for 27%

profile of v3, /device:TPU:0, one launch (start us, length us, event | category | flops | bytes accessed | tf_op | source)
XLA Modules:
  0.0 58.8 jit_solution(9609129654358597840)
XLA Ops:
  0.6 0.0 copy-start.1
  0.6 0.0 copy-start.2
  0.7 0.0 copy-start.3
  0.7 0.0 copy-start.4
  0.7 0.0 copy-start.6
  0.7 0.0 copy-start.5
  0.7 2.2 %partial_drive.1 = f32[16,4,256]{2,1,0:T(4,128)} custom-call(s32[1]{0:T(128)} %bitcast.index_ref, bf16[64,1024]{1,0:T(8,128)(2,1)} %series_hbm.3, bf16[16384,256]{1,0:T(8,128)(2,1)} %load_hbm.3, f32[1,16384]{1,0:T(1,128)} %bitcast.9, s32[1,16384]{1,0:T(1,128)} %bitcast.12, s32[1,16384]{1,0:T(1,128)} %bitcast.15, s32[1,16384]{1,0:T(1,128)} %bitcast.18), custom_call_target="tpu_custom_call" | custom-call | flops 33554432 | bytes 1048576 | tf_op jit(solution)/shard_map/partial_drive/pallas_call | solution.py:100
  2.9 7.4 %all-to-all-start = ((f32[16,4,256]{2,1,0:T(4,128)}), f32[16,4,256]{2,1,0:T(4,128)S(1)}, u32[]{:S(2)}, u32[]{:S(2)}) async-start(f32[16,4,256]{2,1,0:T(4,128)} %partial_drive.1), calls=%async_computation | async-start | bytes 131072 | tf_op jit(solution)/shard_map/all_to_all | solution.py:532
  10.3 0.0 copy-done.1
  10.3 0.0 copy-done.2
  10.3 0.0 copy-done.3
  10.3 0.0 copy-done.4
  10.3 0.0 copy-done.6
  10.3 0.0 copy-done.5
  10.3 0.0 copy-start.7
  10.4 13.0 %transitions.1 = (f32[4,256,256]{2,1,0:T(8,128)S(1)}, f32[3,256,256]{2,1,0:T(8,128)S(1)}, f32[256,256]{1,0:T(8,128)S(1)}, bf16[256,256]{1,0:T(8,128)(2,1)S(1)}, f32[1,256]{1,0:T(1,128)S(1)}) custom-call(s32[1]{0:T(128)S(6)} %mul.3.day_ref, bf16[16384,256]{1,0:T(8,128)(2,1)} %load_hbm.3, f32[1,16384]{1,0:T(1,128)S(1)} %bitcast.10, s32[1,16384]{1,0:T(1,128)S(1)} %bitcast.13, ...), custom_call_target="tpu_custom_call" | custom-call | flops 8589934592 | bytes 10485760 | tf_op jit(solution)/shard_map/transitions/pallas_call | solution.py:184
  23.4 0.0 copy-start.8
  23.4 0.9 %copy-done.8 = f32[3,256,256]{2,1,0:T(8,128)} copy-done((f32[3,256,256]{2,1,0:T(8,128)}, f32[3,256,256]{2,1,0:T(8,128)S(1)}, u32[]{:S(2)}) %copy-start.8) | copy-done | bytes 786456
  24.3 0.0 copy-start
  24.3 0.0 all-to-all-done.terms_ref
  24.3 0.4 collective-permute-start
  24.7 0.8 %own_states.1 = (f32[4,256]{1,0:T(4,128)S(1)}, f32[2,256]{1,0:T(2,128)S(1)}) custom-call(f32[16,4,256]{2,1,0:T(4,128)S(1)} %all-to-all-done.terms_ref, f32[4,256,256]{2,1,0:T(8,128)S(1)} %get-tuple-element.33.step_ref, bf16[256,256]{1,0:T(8,128)(2,1)S(1)} %copy-done.5, f32[1,256]{1,0:T(1,128)S(1)} %get-tuple-element.34.diag_ref), custom_call_target="tpu_custom_call" | custom-call | flops 10485760 | bytes 1048576 | tf_op jit(solution)/shard_map/own_states/pallas_call | solution.py:241
  25.6 0.1 collective-permute-start.1
  25.7 1.1 %collective-permute-done.1.refs_1_.refs_4_ = f32[2,256]{1,0:T(2,128)S(1)} collective-permute-done((f32[2,256]{1,0:T(2,128)S(1)}, f32[2,256]{1,0:T(2,128)S(1)}, u32[]{:S(2)}, u32[]{:S(2)}) %collective-permute-start.1) | collective-permute-done | bytes 2080 | tf_op jit(solution)/shard_map/ppermute | solution.py:528
  26.7 0.0 collective-permute-done.refs_0_.refs_3_
  26.7 0.4 combined.3
  27.1 1.8 %collective-permute-start.2 = (bf16[272,256]{1,0:T(8,128)(2,1)S(1)}, bf16[272,256]{1,0:T(8,128)(2,1)S(1)}, u32[]{:S(2)}, u32[]{:S(2)}) collective-permute-start(bf16[272,256]{1,0:T(8,128)(2,1)S(1)} %get-tuple-element.39), channel_id=1, source_target_pairs={{0,2},{1,3},{2,0},{3,1},{4,6},{5,7},{6,4},{7,5},{8,10},{9,11},{10,... | collective-permute-start | bytes 417800 | tf_op jit(solution)/shard_map/ppermute | solution.py:528
  28.9 0.0 copy-done.7
  28.9 1.4 %smoother_powers.1 = (bf16[5,256,256]{2,1,0:T(8,128)(2,1)S(1)}, bf16[5,256,256]{2,1,0:T(8,128)(2,1)S(1)}) custom-call(f32[256,256]{1,0:T(8,128)S(1)} %copy-done.7), custom_call_target="tpu_custom_call" | custom-call | flops 402653184 | bytes 2097152 | tf_op jit(solution)/shard_map/smoother_powers/pallas_call | solution.py:426
  30.3 2.8 %collective-permute-done.2.refs_0_.refs_5_ = bf16[272,256]{1,0:T(8,128)(2,1)S(1)} collective-permute-done((bf16[272,256]{1,0:T(8,128)(2,1)S(1)}, bf16[272,256]{1,0:T(8,128)(2,1)S(1)}, u32[]{:S(2)}, u32[]{:S(2)}) %collective-permute-start.2) | collective-permute-done | bytes 139296 | tf_op jit(solution)/shard_map/ppermute | solution.py:528
  33.0 0.3 combined.4
  33.4 1.8 %collective-permute-start.3 = (bf16[272,256]{1,0:T(8,128)(2,1)S(1)}, bf16[272,256]{1,0:T(8,128)(2,1)S(1)}, u32[]{:S(2)}, u32[]{:S(2)}) collective-permute-start(bf16[272,256]{1,0:T(8,128)(2,1)S(1)} %get-tuple-element.46), channel_id=1, source_target_pairs={{0,4},{1,5},{2,6},{3,7},{4,0},{5,1},{6,2},{7,3},{8,12},{9,13},{10,... | collective-permute-start | bytes 417800 | tf_op jit(solution)/shard_map/ppermute | solution.py:528
  35.2 3.4 %collective-permute-done.3.refs_0_.refs_6_ = bf16[272,256]{1,0:T(8,128)(2,1)S(1)} collective-permute-done((bf16[272,256]{1,0:T(8,128)(2,1)S(1)}, bf16[272,256]{1,0:T(8,128)(2,1)S(1)}, u32[]{:S(2)}, u32[]{:S(2)}) %collective-permute-start.3) | collective-permute-done | bytes 139296 | tf_op jit(solution)/shard_map/ppermute | solution.py:528
  38.6 0.2 combined.5
  38.8 2.7 %collective-permute-start.4 = (f32[1,256]{1,0:T(1,128)S(1)}, f32[1,256]{1,0:T(1,128)S(1)}, u32[]{:S(2)}, u32[]{:S(2)}) collective-permute-start(f32[1,256]{1,0:T(1,128)S(1)} %combined.5), channel_id=1, source_target_pairs={{0,8},{1,9},{2,10},{3,11},{4,12},{5,13},{6,14},{7,15},{8,0},{9,1},... | collective-permute-start | bytes 3080 | tf_op jit(solution)/shard_map/ppermute | solution.py:528
  41.4 0.0 copy-start.9
  41.4 1.1 %copy-done.9 = f32[3,256,256]{2,1,0:T(8,128)S(1)} copy-done((f32[3,256,256]{2,1,0:T(8,128)S(1)}, f32[3,256,256]{2,1,0:T(8,128)}, u32[]{:S(2)}) %copy-start.9) | copy-done | bytes 786456
  42.6 0.8 %prefixed.1 = (bf16[256,1024]{1,0:T(8,128)(2,1)S(1)}, bf16[256,1024]{1,0:T(8,128)(2,1)S(1)}, f32[1,1024]{1,0:T(1,128)S(1)}) custom-call(s32[1]{0:T(128)} %bitcast.3.upper_ref.refs_0_, s32[1]{0:T(128)} %bitcast.2.upper_ref.refs_1_, s32[1]{0:T(128)} %bitcast.1.upper_ref.refs_2_, bf16[256,256]{1,0:T(8,128)(2,1)S(1)} %collective-permute-done.refs_0_.refs_3_, ...), custom_call_target="tpu_custom_call" | custom-call | flops 603979776 | bytes 3145728 | tf_op jit(solution)/shard_map/prefixed/pallas_call | solution.py:378
  43.4 0.0 collective-permute-done.4
  43.4 0.3 filtered.1
  43.8 12.4 %all_to_all.10.gathered_ref = f32[16,4,256]{2,1,0:T(4,128)S(1)} all-to-all(f32[16,4,256]{2,1,0:T(4,128)S(1)} %broadcast_in_dim.28), channel_id=1, replica_groups=mesh['spec'=2,'tm'=16] {'tm'}, dimensions={0} | all-to-all | bytes 131072 | tf_op jit(solution)/shard_map/all_to_all | solution.py:567
  56.2 0.0 copy-done
  56.2 2.6 %finish.1 = (f32[4,256]{1,0:T(4,128)}, bf16[64,1024]{1,0:T(8,128)(2,1)}) custom-call(s32[1]{0:T(128)} %bitcast.index_ref, f32[16,4,256]{2,1,0:T(4,128)S(1)} %all_to_all.10.gathered_ref, bf16[5,256,256]{2,1,0:T(8,128)(2,1)S(1)} %get-tuple-element.52.high_ref, bf16[5,256,256]{2,1,0:T(8,128)(2,1)S(1)} %get-tuple-element.53.low_ref, f32[1,256]{1,0:T(1,128)S(1)} %bitcast.22, ...), custom_call_target="tpu_custom_call" | custom-call | flops 33554432 | bytes 2097152 | tf_op jit(solution)/shard_map/finish/pallas_call | solution.py:495
  (3 shorter events, 0.0 us)
Async XLA Ops:
  0.6 9.7 %copy-start.1 = (f32[16384]{0:T(1024)S(1)}, f32[16384]{0:T(1024)}, u32[]{:S(2)}) copy-start(f32[16384]{0:T(1024)} %param.11) | copy-start | bytes 196612
  0.6 9.7 %copy-start.2 = (s32[16384]{0:T(1024)S(1)}, s32[16384]{0:T(1024)}, u32[]{:S(2)}) copy-start(s32[16384]{0:T(1024)} %param.12) | copy-start | bytes 196612
  0.7 9.7 %copy-start.3 = (s32[16384]{0:T(1024)S(1)}, s32[16384]{0:T(1024)}, u32[]{:S(2)}) copy-start(s32[16384]{0:T(1024)} %param.13) | copy-start | bytes 196612
  0.7 9.7 %copy-start.4 = (s32[16384]{0:T(1024)S(1)}, s32[16384]{0:T(1024)}, u32[]{:S(2)}) copy-start(s32[16384]{0:T(1024)} %param.14) | copy-start | bytes 196612
  0.7 9.7 %copy-start.6 = (f32[256]{0:T(256)S(1)}, f32[256]{0:T(256)}, u32[]{:S(2)}) copy-start(f32[256]{0:T(256)} %param.15) | copy-start | bytes 3076
  0.7 9.7 %copy-start.5 = (bf16[256,256]{1,0:T(8,128)(2,1)S(1)}, bf16[256,256]{1,0:T(8,128)(2,1)}, u32[]{:S(2)}) copy-start(bf16[256,256]{1,0:T(8,128)(2,1)} %gain_ref.1) | copy-start | bytes 393220
  2.9 21.4 %all-to-all-start = ((f32[16,4,256]{2,1,0:T(4,128)}), f32[16,4,256]{2,1,0:T(4,128)S(1)}, u32[]{:S(2)}, u32[]{:S(2)}) async-start(f32[16,4,256]{2,1,0:T(4,128)} %partial_drive.1), calls=%async_computation | async-start | bytes 131072 | tf_op jit(solution)/shard_map/all_to_all | solution.py:532
  10.3 18.5 %copy-start.7 = (f32[256,256]{1,0:T(8,128)S(1)}, f32[256,256]{1,0:T(8,128)}, u32[]{:S(2)}) copy-start(f32[256,256]{1,0:T(8,128)} %in_ref) | copy-start | bytes 786436
  23.4 0.9 %copy-start.8 = (f32[3,256,256]{2,1,0:T(8,128)}, f32[3,256,256]{2,1,0:T(8,128)S(1)}, u32[]{:S(2)}) copy-start(f32[3,256,256]{2,1,0:T(8,128)S(1)} %get-tuple-element.47.refs_7_) | copy-start | bytes 2359300
  24.3 31.9 %copy-start = (bf16[64,1024]{1,0:T(8,128)(2,1)S(1)}, bf16[64,1024]{1,0:T(8,128)(2,1)}, u32[]{:S(2)}) copy-start(bf16[64,1024]{1,0:T(8,128)(2,1)} %series_hbm.3) | copy-start | bytes 393220
  24.3 2.4 %collective-permute-start = (bf16[256,256]{1,0:T(8,128)(2,1)S(1)}, bf16[256,256]{1,0:T(8,128)(2,1)S(1)}, u32[]{:S(2)}, u32[]{:S(2)}) collective-permute-start(bf16[256,256]{1,0:T(8,128)(2,1)S(1)} %get-tuple-element.36), channel_id=1, source_target_pairs={{0,1},{1,0},{2,3},{3,2},{4,5},{5,4},{6,7},{7,6},{8,9},{9,8},{10,11... | collective-permute-start | bytes 393224 | tf_op jit(solution)/shard_map/ppermute | solution.py:528
  25.6 1.2 %collective-permute-start.1 = (f32[2,256]{1,0:T(2,128)S(1)}, f32[2,256]{1,0:T(2,128)S(1)}, u32[]{:S(2)}, u32[]{:S(2)}) collective-permute-start(f32[2,256]{1,0:T(2,128)S(1)} %get-tuple-element.35.tail_ref), channel_id=1, source_target_pairs={{0,1},{1,0},{2,3},{3,2},{4,5},{5,4},{6,7},{7,6},{8,9},{9,8},{10,11... | collective-permute-start | bytes 6152 | tf_op jit(solution)/shard_map/ppermute | solution.py:528
  27.1 5.9 %collective-permute-start.2 = (bf16[272,256]{1,0:T(8,128)(2,1)S(1)}, bf16[272,256]{1,0:T(8,128)(2,1)S(1)}, u32[]{:S(2)}, u32[]{:S(2)}) collective-permute-start(bf16[272,256]{1,0:T(8,128)(2,1)S(1)} %get-tuple-element.39), channel_id=1, source_target_pairs={{0,2},{1,3},{2,0},{3,1},{4,6},{5,7},{6,4},{7,5},{8,10},{9,11},{10,... | collective-permute-start | bytes 417800 | tf_op jit(solution)/shard_map/ppermute | solution.py:528
  33.4 5.2 %collective-permute-start.3 = (bf16[272,256]{1,0:T(8,128)(2,1)S(1)}, bf16[272,256]{1,0:T(8,128)(2,1)S(1)}, u32[]{:S(2)}, u32[]{:S(2)}) collective-permute-start(bf16[272,256]{1,0:T(8,128)(2,1)S(1)} %get-tuple-element.46), channel_id=1, source_target_pairs={{0,4},{1,5},{2,6},{3,7},{4,0},{5,1},{6,2},{7,3},{8,12},{9,13},{10,... | collective-permute-start | bytes 417800 | tf_op jit(solution)/shard_map/ppermute | solution.py:528
  38.8 4.6 %collective-permute-start.4 = (f32[1,256]{1,0:T(1,128)S(1)}, f32[1,256]{1,0:T(1,128)S(1)}, u32[]{:S(2)}, u32[]{:S(2)}) collective-permute-start(f32[1,256]{1,0:T(1,128)S(1)} %combined.5), channel_id=1, source_target_pairs={{0,8},{1,9},{2,10},{3,11},{4,12},{5,13},{6,14},{7,15},{8,0},{9,1},... | collective-permute-start | bytes 3080 | tf_op jit(solution)/shard_map/ppermute | solution.py:528
  41.4 1.1 %copy-start.9 = (f32[3,256,256]{2,1,0:T(8,128)S(1)}, f32[3,256,256]{2,1,0:T(8,128)}, u32[]{:S(2)}) copy-start(f32[3,256,256]{2,1,0:T(8,128)} %copy-done.8) | copy-start | bytes 2359300

commit v4 on v3

--- a/solution.py
+++ b/solution.py
@@ -119,81 +119,70 @@
 
 def transitions_of(first_day, day_count, loadings, tables, decay, gain):
     providers, factors = loadings.shape
-    chunk = min(4096, providers)
-    steps = providers // chunk
+    unit = providers // 16
+    sizes = [unit, unit, 2 * unit, 4 * unit, 8 * unit]
+    parts = [slice(sum(sizes[:n]), sum(sizes[: n + 1])) for n in range(len(sizes))]
 
     def kernel(
-        day_ref, load_ref, prec_hbm, start_hbm, stop_hbm, off_hbm, decay_hbm, gain_hbm,
+        day_ref, load_hbm, prec_hbm, start_hbm, stop_hbm, off_hbm, decay_hbm, gain_hbm,
         step_ref, run_ref, last_ref, rest_ref, diag_ref,
-        acc, prec_ref, start_ref, stop_ref, off_ref, decay_ref, gain_ref, sems,
+        acc, load_ref, prec_ref, start_ref, stop_ref, off_ref, decay_ref, gain_ref, sems,
     ):
-        step = pl.program_id(0)
-
-        @pl.when(step == 0)
-        def _():
-            copies = [
-                pltpu.make_async_copy(source, target, sems.at[n])
-                for n, (source, target) in enumerate(
-                    [
-                        (prec_hbm, prec_ref),
-                        (start_hbm, start_ref),
-                        (stop_hbm, stop_ref),
-                        (off_hbm, off_ref),
-                        (decay_hbm, decay_ref),
-                        (gain_hbm, gain_ref),
-                    ]
+        pairs = [
+            (prec_hbm, prec_ref),
+            (start_hbm, start_ref),
+            (stop_hbm, stop_ref),
+            (off_hbm, off_ref),
+        ]
+        pairs += [(load_hbm.at[part], load_ref.at[part]) for part in parts]
+        pairs += [(decay_hbm, decay_ref), (gain_hbm, gain_ref)]
+        copies = [
+            pltpu.make_async_copy(source, target, sems.at[n])
+            for n, (source, target) in enumerate(pairs)
+        ]
+        for copy in copies:
+            copy.start()
+        for copy in copies[:4]:
+            copy.wait()
+        for n, part in enumerate(parts):
+            copies[4 + n].wait()
+            block = load_ref[part]
+            scaled = (block.T.astype(F32) * prec_ref[:, part]).astype(BF16)
+            for d in range(day_count):
+                active = activity(
+                    day_ref[0] + d, start_ref[:, part], stop_ref[:, part], off_ref[:, part]
                 )
-            ]
-            for copy in copies:
-                copy.start()
-            acc[...] = jnp.zeros_like(acc)
-            for copy in copies:
-                copy.wait()
-
-        place = pl.ds(pl.multiple_of(step * chunk, chunk), chunk)
-        block = load_ref[...]
-        scaled = (block.T.astype(F32) * prec_ref[:, place]).astype(BF16)
+                mask = active.astype(F32).astype(BF16)
+                term = mul(scaled * mask, block)
+                acc[d] = term if n == 0 else acc[d] + term
+        for copy in copies[4 + len(parts) :]:
+            copy.wait()
+        same = eye(factors)
+        diagonal = jnp.where(same, decay_ref[...], 0.0)
+        column = jnp.sum(diagonal, axis=1, keepdims=True)
+        steps_of = []
         for d in range(day_count):
-            active = activity(
-                day_ref[0] + d, start_ref[:, place], stop_ref[:, place], off_ref[:, place]
+            damped = (acc[d] * column).astype(BF16)
+            pulled = lax.dot_general(
+                damped, gain_ref[...], (((1,), (1,)), ((), ())), preferred_element_type=F32
             )
-            mask = active.astype(F32).astype(BF16)
-            acc[d] += mul(scaled * mask, block)
-
-        @pl.when(step == steps - 1)
-        def _():
-            same = eye(factors)
-            diagonal = jnp.where(same, decay_ref[...], 0.0)
-            column = jnp.sum(diagonal, axis=1, keepdims=True)
-            for d in range(day_count):
-                damped = (acc[d] * column).astype(BF16)
-                pulled = lax.dot_general(
-                    damped, gain_ref[...], (((1,), (1,)), ((), ())), preferred_element_type=F32
-                )
-                step_ref[d] = diagonal - pulled
-            running = step_ref[0]
-            for d in range(1, day_count):
-                run_ref[d - 1] = running
-                running = product(running, split(step_ref[d]))
-            last = running
-            last_ref[...] = last
-            rest_ref[...] = jnp.where(same, 0.0, last).astype(BF16)
-            diag_ref[...] = jnp.sum(jnp.where(same, last, 0.0), axis=0, keepdims=True)
-
-    cube = pl.BlockSpec((day_count, factors, factors), lambda i: (0, 0, 0))
-    return pl.pallas_call(
-        kernel,
-        grid=(steps,),
-        in_specs=[smem(), pl.BlockSpec((chunk, factors), lambda i: (i, 0))] + hbm(6),
-        out_specs=[
-            cube,
-            pl.BlockSpec((day_count - 1, factors, factors), lambda i: (0, 0, 0)),
-            pl.BlockSpec((factors, factors), lambda i: (0, 0)),
-            pl.BlockSpec((factors, factors), lambda i: (0, 0)),
-            pl.BlockSpec((1, factors), lambda i: (0, 0)),
-        ],
+            steps_of.append(diagonal - pulled)
+        running = steps_of[0]
+        for d in range(1, day_count):
+            run_ref[d - 1] = running
+            step_ref[d - 1] = steps_of[d]
+            running = product(running, split(steps_of[d]))
+        last = running
+        last_ref[...] = last
+        rest_ref[...] = jnp.where(same, 0.0, last).astype(BF16)
+        diag_ref[...] = jnp.sum(jnp.where(same, last, 0.0), axis=0, keepdims=True)
+
+    return pl.pallas_call(
+        kernel,
+        in_specs=[smem()] + hbm(7),
+        out_specs=vmem(5),
         out_shape=[
-            shape(day_count, factors, factors),
+            shape(day_count - 1, factors, factors),
             shape(day_count - 1, factors, factors),
             shape(factors, factors),
             shape(factors, factors, dtype=BF16),
@@ -201,15 +190,16 @@
         ],
         scratch_shapes=[
             pltpu.VMEM((day_count, factors, factors), F32),
+            pltpu.VMEM((providers, factors), BF16),
             pltpu.VMEM((1, providers), F32),
             pltpu.VMEM((1, providers), jnp.int32),
             pltpu.VMEM((1, providers), jnp.int32),
             pltpu.VMEM((1, providers), jnp.int32),
             pltpu.VMEM((1, factors), F32),
             pltpu.VMEM((factors, factors), BF16),
-            pltpu.SemaphoreType.DMA((6,)),
+            pltpu.SemaphoreType.DMA((6 + len(parts),)),
         ],
-        compiler_params=params(48, dimension_semantics=("arbitrary",)),
+        compiler_params=params(),
         cost_estimate=cost(2 * day_count * providers * factors * factors, 10 << 20),
         name="transitions",
     )(first_day, loadings, *tables, decay, gain)
@@ -233,7 +223,7 @@
         state = offsets[0:1]
         out_ref[0:1] = state
         for d in range(1, day_count):
-            state = product(state, split(step_ref[d])) + offsets[d : d + 1]
+            state = product(state, split(step_ref[d - 1])) + offsets[d : d + 1]
             out_ref[d : d + 1] = state
         packet_ref[0:1] = state
         packet_ref[1:2] = diag_ref[...]
@@ -249,122 +239,107 @@
     )(terms, steps, gain, diag)
 
 
-def rebuilt(rest, diag, same):
-    return rest.astype(F32) + jnp.where(same, diag, 0.0)
-
-
 PACKED = 16
 
 
-def unpacked(packed_ref, same):
+def unpacked(packed_ref):
     factors = packed_ref.shape[1]
     rows = packed_ref[factors:].astype(F32)
-    matrix = rebuilt(packed_ref[:factors], rows[2:3] + rows[3:4], same)
-    return matrix, rows[0:1] + rows[1:2]
-
-
-def combine_into(low, low_tail, high, high_tail, same, map_ref, tail_ref, packed_ref):
-    factors = low.shape[0]
-    high = split(high)
-    total = None if map_ref is None else product(low, high)
-    tail = product(low_tail, high) + high_tail
-    if map_ref is not None:
-        map_ref[...] = total
-    tail_ref[...] = tail
-    if packed_ref is not None:
-        packed_ref[:factors] = jnp.where(same, 0.0, total).astype(BF16)
-        diag = jnp.sum(jnp.where(same, total, 0.0), axis=0, keepdims=True)
-        rows = [*split(tail), *split(diag), jnp.zeros((PACKED - 4, factors), BF16)]
-        packed_ref[factors:] = jnp.concatenate(rows, 0)
-
-
-def combined(upper, matrix, tail, other, last, need_map):
+    return packed_ref[:factors], rows[2:3] + rows[3:4], rows[0:1] + rows[1:2]
+
+
+def through(a, rest, diag):
+    high, low = split(a)
+    return mul(high, rest) + mul(low, rest) + a * diag
+
+
+def combined(upper, matrix, packet, other_rest, other_packet):
     factors = matrix.shape[0]
 
-    def kernel(upper_ref, mine_ref, tail_ref, *refs):
-        others, outs = refs[: len(other)], refs[len(other) :]
-        outs = list(outs)
-        next_ref = outs.pop(0)
-        map_ref = outs.pop(0) if need_map else None
-        packed_ref = None if last else outs.pop(0)
+    def kernel(upper_ref, mine_ref, packet_ref, rest_ref, other_ref, packed_ref):
         same = eye(factors)
-        if len(other) == 2:
-            theirs = rebuilt(others[0][...], others[1][1:2], same)
-            their_tail = others[1][0:1]
-        else:
-            theirs, their_tail = unpacked(others[0], same)
+
+        def pack(total, tail):
+            packed_ref[:factors] = jnp.where(same, 0.0, total).astype(BF16)
+            diag = jnp.sum(jnp.where(same, total, 0.0), axis=0, keepdims=True)
+            rows = [*split(tail), *split(diag), jnp.zeros((PACKED - 4, factors), BF16)]
+            packed_ref[factors:] = jnp.concatenate(rows, 0)
 
         @pl.when(upper_ref[0] == 1)
         def _():
-            combine_into(
-                theirs, their_tail, mine_ref[...], tail_ref[0:1], same, map_ref, next_ref, packed_ref
-            )
+            mine = split(mine_ref[...])
+            theirs = rest_ref[...].astype(F32) + jnp.where(same, other_ref[1:2], 0.0)
+            pack(product(theirs, mine), product(other_ref[0:1], mine) + packet_ref[0:1])
 
         @pl.when(upper_ref[0] == 0)
         def _():
-            combine_into(
-                mine_ref[...], tail_ref[0:1], theirs, their_tail, same, map_ref, next_ref, packed_ref
+            rest, diag = rest_ref[...], other_ref[1:2]
+            pack(
+                through(mine_ref[...], rest, diag),
+                through(packet_ref[0:1], rest, diag) + other_ref[0:1],
             )
 
-    out_shape = [shape(1, factors)]
-    if need_map:
-        out_shape.append(shape(factors, factors))
-    if not last:
-        out_shape.append(shape(factors + PACKED, factors, dtype=BF16))
-    return pl.pallas_call(
-        kernel,
-        in_specs=[smem()] + vmem(2 + len(other)),
-        out_specs=vmem(len(out_shape)),
-        out_shape=out_shape,
-        compiler_params=params(),
-        cost_estimate=cost(12 * factors**3, 1 << 20),
+    return pl.pallas_call(
+        kernel,
+        in_specs=[smem()] + vmem(4),
+        out_specs=pl.BlockSpec(memory_space=VMEM),
+        out_shape=shape(factors + PACKED, factors, dtype=BF16),
+        compiler_params=params(),
+        cost_estimate=cost(6 * factors**3, 1 << 20),
         name="combined",
-    )(upper, matrix, tail, *other)
-
-
-def advanced(state, matrix, tail):
-    factors = matrix.shape[0]
-
-    def kernel(state_ref, matrix_ref, tail_ref, out_ref):
-        out_ref[...] = product(state_ref[...], split(matrix_ref[...])) + tail_ref[...]
-
-    return pl.pallas_call(
-        kernel,
-        in_specs=vmem(3),
+    )(upper, matrix, packet, other_rest, other_packet)
+
+
+def advanced(pair, state, pieces):
+    count = len(pieces)
+    factors = pieces[0].shape[1]
+
+    def kernel(pair_ref, state_ref, *refs):
+        out_ref = refs[-1]
+        out_ref[...] = state_ref[...]
+        for turn in range(count):
+            for m in range(count):
+
+                @pl.when((pair_ref[0] ^ m) == turn)
+                def _():
+                    rest, diag, tail = unpacked(refs[m])
+                    out_ref[...] = through(out_ref[...], rest, diag) + tail
+
+    return pl.pallas_call(
+        kernel,
+        in_specs=[smem()] + vmem(count + 1),
         out_specs=pl.BlockSpec(memory_space=VMEM),
         out_shape=shape(1, factors),
         compiler_params=params(),
         cost_estimate=cost(12 * factors**2, 1 << 18),
         name="advanced",
-    )(state, matrix, tail)
-
-
-def prefixed(uppers, levels, running, last, states):
+    )(pair, state, *pieces)
+
+
+def prefixed(pair, upper, pieces, other_rest, other_packet, running, last, states):
     day_count, factors = states.shape
-    count = len(levels)
-
-    flat = [a for level in levels for a in level]
-
-    def kernel(*refs):
-        upper_refs = refs[:count]
-        parts = list(refs[count : count + len(flat)])
-        run_ref, last_ref, states_ref, high_ref, low_ref, add_ref, work, tail = refs[count + len(flat) :]
-        parts = [[parts.pop(0) for _ in level] for level in levels]
-        same = eye(factors)
-        work[...] = jnp.where(same, 1.0, 0.0)
+    count = len(pieces)
+
+    def kernel(pair_ref, upper_ref, *refs):
+        rest_ref, packet_ref, run_ref, last_ref, states_ref = refs[count : count + 5]
+        high_ref, low_ref, add_ref, work, tail = refs[count + 5 :]
+        work[...] = jnp.where(eye(factors), 1.0, 0.0)
         tail[...] = jnp.zeros_like(tail)
-        for level in reversed(range(count)):
-
-            @pl.when(upper_refs[level][0] == 1)
-            def _():
-                if len(parts[level]) == 2:
-                    rest, packet = parts[level]
-                    matrix, add = rebuilt(rest[...], packet[1:2], same), packet[0:1]
-                else:
-                    matrix, add = unpacked(parts[level][0], same)
-                step = split(matrix)
-                work[...] = product(work[...], step)
-                tail[...] = product(tail[...], step) + add
+
+        def follow(rest, diag, add):
+            work[...] = through(work[...], rest, diag)
+            tail[...] = through(tail[...], rest, diag) + add
+
+        for turn in range(count - 1):
+            for m in range(1, count):
+
+                @pl.when(((pair_ref[0] ^ m) == turn) & (pair_ref[0] > turn))
+                def _():
+                    follow(*unpacked(refs[m]))
+
+        @pl.when(upper_ref[0] == 1)
+        def _():
+            follow(rest_ref[...], packet_ref[1:2], packet_ref[0:1])
 
         for d in range(day_count):
             step = split(run_ref[d] if d < day_count - 1 else last_ref[...])
@@ -377,7 +352,7 @@
     wide = day_count * factors
     return pl.pallas_call(
         kernel,
-        in_specs=[smem()] * count + vmem(len(flat) + 3),
+        in_specs=[smem()] * 2 + vmem(count + 5),
         out_specs=vmem(3),
         out_shape=[
             shape(factors, wide, dtype=BF16),
@@ -388,7 +363,7 @@
         compiler_params=params(),
         cost_estimate=cost(36 * factors**3, 3 << 20),
         name="prefixed",
-    )(*uppers, *flat, running, last, states)
+    )(pair, upper, *pieces, other_rest, other_packet, running, last, states)
 
 
 def filtered_of(state, arrived, high, low, add):
@@ -534,38 +509,30 @@
     rest, terms = lax.optimization_barrier((rest, terms))
     states, packet = own_states(terms, steps, gain, diag)
 
+    upper = (place & 1)[None]
+    other_rest, other_packet = swapped(rest, 1), swapped(packet, 1)
+    packed = combined(upper, mine, packet, other_rest, other_packet)
     group = min(8, devices)
-    matrix, tail = mine, packet
-    sent = (rest, packet)
-    levels, uppers = [], []
-    reach = 1
-    while reach < group:
-        other = tuple(swapped(a, reach) for a in sent)
-        upper = jnp.where((place & reach) != 0, 1, 0).astype(jnp.int32)[None]
-        levels.append(other)
-        uppers.append(upper)
-        last = reach * 2 == group
-        if reach == 2:
-            sent, smoother = lax.optimization_barrier((sent, smoother))
-            powers = smoother_powers(smoother)
-            tail, powers = lax.optimization_barrier((tail, powers))
-        need_map = not last or devices // group > 2
-        tail, *rest_of = combined(upper, matrix, tail, other, last, need_map)
-        matrix, sent = (rest_of[0], rest_of[1:]) if need_map else (None, None)
-        reach *= 2
-
-    ahead = prefixed(uppers, levels, running, mine, states)
-    state = jnp.zeros((1, factors), F32)
+    pair = ((place % group) >> 1)[None]
+    pieces = [packed] + [swapped(packed, 2 * m) for m in range(1, group // 2)]
+    smoother, packed = lax.optimization_barrier((smoother, packed))
+    powers = smoother_powers(smoother)
+    nothing = jnp.zeros((1, factors), F32)
+    nothing, powers = lax.optimization_barrier((nothing, powers))
+    tail = advanced(pair, nothing, pieces)
+    ahead = prefixed(pair, upper, pieces, other_rest, other_packet, running, mine, states)
+
+    state = nothing
     arrived = jnp.where(place // group == 1, swapped(tail, group), 0.0)
     for g in range(1, devices // group - 1):
         state = state + arrived
-        moved = advanced(state, matrix, tail)
+        moved = advanced(pair, state, pieces)
         pairs = [(g * group + j, (g + 1) * group + j) for j in range(group)]
         arrived = lax.ppermute(moved, "tm", pairs)
 
-    mine = filtered_of(state, arrived, *ahead)[None]
+    own = filtered_of(state, arrived, *ahead)[None]
     gathered = lax.all_to_all(
-        jnp.broadcast_to(mine, (devices, day_count, factors)), "tm", 0, 0, tiled=True
+        jnp.broadcast_to(own, (devices, day_count, factors)), "tm", 0, 0, tiled=True
     )
     return tuple(finish(index, day_count, gathered, powers, decay, series, loadings, tables))
 

time: 59.1 us -> 56 us (0.948)
  local copies, waits for them, and re-layouts: 2.08 us -> 0.06 us
  Pallas kernels: 22.2 us -> 21.2 us
    unnamed x20 -> x16, local copies, waits for them, and re-layouts: 2.05 us -> 0.04 us
    pallas_call x5 -> x4, Pallas kernels: 14.8 us -> 13.9 us  [the longest x1 11.9 us: transitions_of(): pl.pallas_call(kernel, in_specs=[smem()] + hbm(7), out_specs=vmem(5), out...]
    ppermute x5 -> x6, starting transfers between devices: 6.75 us -> 6.53 us  [swapped(): lax.ppermute(array, 'tm', [(i, i ^ distance) for i in range(devices)])]
    ppermute x5 -> x6, waiting for transfers between devices: 7.18 us -> 7.3 us  [swapped(): lax.ppermute(array, 'tm', [(i, i ^ distance) for i in range(devices)])]
  transfers between devices with their start and end apart: 6 -> 7, of which waited for: 3 -> 4; matrix products, arithmetic and copies ran while one was open for 0% -> 0% of each run, Pallas kernels for 27% -> 27%
where the time goes in v4:
time: 56 us; the launch traced here: 55.7 us
  Pallas kernels  21.2 us (38%)
  starting transfers between devices  13.9 us (25%)
  blocking collectives  12.2 us (22%)
  waiting for transfers between devices  7.31 us (13%)
  between operations  0.97 us (2%)
    all_to_all x1, blocking collectives, local(): lax.all_to_all(jnp.broadcast_to(own, (devices, day_count, factors)), 'tm'...  12.2 us
    pallas_call x1, Pallas kernels, transitions_of(): pl.pallas_call(kernel, in_specs=[smem()] + hbm(7), out_specs=vmem(5), out...  11.9 us
    all_to_all x1, starting transfers between devices, local(): terms = lax.all_to_all(partial, 'tm', 0, 0, tiled=True)  7.4 us
    ppermute x6, waiting for transfers between devices, swapped(): lax.ppermute(array, 'tm', [(i, i ^ distance) for i in range(devices)])  7.3 us
    ppermute x6, starting transfers between devices, swapped(): lax.ppermute(array, 'tm', [(i, i ^ distance) for i in range(devices)])  6.53 us
    pallas_call x1, Pallas kernels, finish(): pl.pallas_call(kernel, in_specs=[smem()] + vmem(4) + hbm(6), out_specs=vm...  2.65 us
    pallas_call x1, Pallas kernels, partial_drive(): pl.pallas_call(kernel, in_specs=[smem()] + hbm(6), out_specs=pl.BlockSpec...  2.16 us
    pallas_call x1, Pallas kernels, smoother_powers(): pl.pallas_call(kernel, in_specs=vmem(1), out_specs=vmem(2), out_shape=[sh...  1.41 us
  transfers between devices with their start and end apart: 7, of which 4 were waited for; matrix products, arithmetic and copies ran while one was open for 0% of the time, Pallas kernels for 27%

profile of v4, /device:TPU:0, one launch (start us, length us, event | category | flops | bytes accessed | tf_op | source)
XLA Modules:
  0.0 55.7 jit_solution(17969620794744113443)
XLA Ops:
  0.6 0.0 copy-start.4
  0.6 0.0 copy-start.3
  0.7 0.0 copy-start.2
  0.7 0.0 copy-start.1
  0.7 0.0 copy-start.5
  0.7 0.0 copy-start.6
  0.7 2.2 %partial_drive.1 = f32[16,4,256]{2,1,0:T(4,128)} custom-call(s32[1]{0:T(128)} %bitcast.index_ref, bf16[64,1024]{1,0:T(8,128)(2,1)} %series_hbm.3, bf16[16384,256]{1,0:T(8,128)(2,1)} %load_hbm.5, f32[1,16384]{1,0:T(1,128)} %bitcast.8, s32[1,16384]{1,0:T(1,128)} %bitcast.11, s32[1,16384]{1,0:T(1,128)} %bitcast.14, s32[1,16384]{1,0:T(1,128)} %bitcast.17), custom_call_target="tpu_custom_call" | custom-call | flops 33554432 | bytes 1048576 | tf_op jit(solution)/shard_map/partial_drive/pallas_call | solution.py:100
  2.9 7.4 %all-to-all-start = ((f32[16,4,256]{2,1,0:T(4,128)}), f32[16,4,256]{2,1,0:T(4,128)S(1)}, u32[]{:S(2)}, u32[]{:S(2)}) async-start(f32[16,4,256]{2,1,0:T(4,128)} %partial_drive.1), calls=%async_computation | async-start | bytes 131072 | tf_op jit(solution)/shard_map/all_to_all | solution.py:507
  10.3 0.0 copy-done.4
  10.3 0.0 copy-done.3
  10.3 0.0 copy-done.2
  10.3 0.0 copy-done.1
  10.3 0.0 copy-done.5
  10.3 0.0 copy-done.6
  10.3 0.0 copy-start.7
  10.3 0.0 copy-start
  10.3 11.9 %transitions.1 = (f32[3,256,256]{2,1,0:T(8,128)S(1)}, f32[3,256,256]{2,1,0:T(8,128)S(1)}, f32[256,256]{1,0:T(8,128)S(1)}, bf16[256,256]{1,0:T(8,128)(2,1)S(1)}, f32[1,256]{1,0:T(1,128)S(1)}) custom-call(s32[1]{0:T(128)S(6)} %mul.3.day_ref, bf16[16384,256]{1,0:T(8,128)(2,1)} %load_hbm.5, f32[1,16384]{1,0:T(1,128)S(1)} %bitcast.9, s32[1,16384]{1,0:T(1,128)S(1)} %bitcast.12, ...), custom_call_target="tpu_custom_call" | custom-call | flops 8589934592 | bytes 10485760 | tf_op jit(solution)/shard_map/transitions/pallas_call | solution.py:180
  22.3 0.0 all-to-all-done.terms_ref
  22.3 0.5 collective-permute-start
  22.7 0.8 %own_states.1 = (f32[4,256]{1,0:T(4,128)S(1)}, f32[2,256]{1,0:T(2,128)S(1)}) custom-call(f32[16,4,256]{2,1,0:T(4,128)S(1)} %all-to-all-done.terms_ref, f32[3,256,256]{2,1,0:T(8,128)S(1)} %get-tuple-element.27.step_ref, bf16[256,256]{1,0:T(8,128)(2,1)S(1)} %copy-done.5, f32[1,256]{1,0:T(1,128)S(1)} %get-tuple-element.28.diag_ref), custom_call_target="tpu_custom_call" | custom-call | flops 10485760 | bytes 1048576 | tf_op jit(solution)/shard_map/own_states/pallas_call | solution.py:231
  23.6 0.1 collective-permute-start.1
  23.7 1.1 %collective-permute-done.1.other_ref.refs_5_ = f32[2,256]{1,0:T(2,128)S(1)} collective-permute-done((f32[2,256]{1,0:T(2,128)S(1)}, f32[2,256]{1,0:T(2,128)S(1)}, u32[]{:S(2)}, u32[]{:S(2)}) %collective-permute-start.1) | collective-permute-done | bytes 2080 | tf_op jit(solution)/shard_map/ppermute | solution.py:503
  24.8 0.0 collective-permute-done.rest_ref.refs_4_
  24.8 0.3 combined.1.refs_0_
  25.1 2.7 %collective-permute-start.4 = (bf16[272,256]{1,0:T(8,128)(2,1)S(1)}, bf16[272,256]{1,0:T(8,128)(2,1)S(1)}, u32[]{:S(2)}, u32[]{:S(2)}) collective-permute-start(bf16[272,256]{1,0:T(8,128)(2,1)S(1)} %combined.1.refs_0_), channel_id=1, source_target_pairs={{0,6},{1,7},{2,4},{3,5},{4,2},{5,3},{6,0},{7,1},{8,14},{9,15},{10,... | collective-permute-start | bytes 417800 | tf_op jit(solution)/shard_map/ppermute | solution.py:503
  27.7 0.6 %collective-permute-start.3 = (bf16[272,256]{1,0:T(8,128)(2,1)S(1)}, bf16[272,256]{1,0:T(8,128)(2,1)S(1)}, u32[]{:S(2)}, u32[]{:S(2)}) collective-permute-start(bf16[272,256]{1,0:T(8,128)(2,1)S(1)} %combined.1.refs_0_), channel_id=1, source_target_pairs={{0,4},{1,5},{2,6},{3,7},{4,0},{5,1},{6,2},{7,3},{8,12},{9,13},{10,... | collective-permute-start | bytes 417800 | tf_op jit(solution)/shard_map/ppermute | solution.py:503
  28.3 0.3 collective-permute-start.2
  28.6 0.0 copy-done.7
  28.6 1.4 %smoother_powers.1 = (bf16[5,256,256]{2,1,0:T(8,128)(2,1)S(1)}, bf16[5,256,256]{2,1,0:T(8,128)(2,1)S(1)}) custom-call(f32[256,256]{1,0:T(8,128)S(1)} %copy-done.7), custom_call_target="tpu_custom_call" | custom-call | flops 402653184 | bytes 2097152 | tf_op jit(solution)/shard_map/smoother_powers/pallas_call | solution.py:401
  30.0 2.5 %collective-permute-done.4.refs_3_ = bf16[272,256]{1,0:T(8,128)(2,1)S(1)} collective-permute-done((bf16[272,256]{1,0:T(8,128)(2,1)S(1)}, bf16[272,256]{1,0:T(8,128)(2,1)S(1)}, u32[]{:S(2)}, u32[]{:S(2)}) %collective-permute-start.4) | collective-permute-done | bytes 139296 | tf_op jit(solution)/shard_map/ppermute | solution.py:503
  32.5 2.7 %collective-permute-done.3.refs_2_ = bf16[272,256]{1,0:T(8,128)(2,1)S(1)} collective-permute-done((bf16[272,256]{1,0:T(8,128)(2,1)S(1)}, bf16[272,256]{1,0:T(8,128)(2,1)S(1)}, u32[]{:S(2)}, u32[]{:S(2)}) %collective-permute-start.3) | collective-permute-done | bytes 139296 | tf_op jit(solution)/shard_map/ppermute | solution.py:503
  35.2 0.0 collective-permute-done.2.refs_1_
  35.2 0.6 %advanced.1 = f32[1,256]{1,0:T(1,128)S(1)} custom-call(s32[1]{0:T(128)} %bitcast.7.pair_ref, f32[1,256]{1,0:T(1,128)S(1)} %broadcast_in_dim.21.state_ref, bf16[272,256]{1,0:T(8,128)(2,1)S(1)} %combined.1.refs_0_, bf16[272,256]{1,0:T(8,128)(2,1)S(1)} %collective-permute-done.2.refs_1_, bf16[272,256]{1,0:T(8,128)(2,1)S(1)} %collective-permute-done.3.refs_2_, ...), custom_call_target="tpu_custom_call" | custom-call | flops 786432 | bytes 262144 | tf_op jit(solution)/shard_map/advanced/pallas_call | solution.py:308
  35.9 2.4 %collective-permute-start.5 = (f32[1,256]{1,0:T(1,128)S(1)}, f32[1,256]{1,0:T(1,128)S(1)}, u32[]{:S(2)}, u32[]{:S(2)}) collective-permute-start(f32[1,256]{1,0:T(1,128)S(1)} %advanced.1), channel_id=1, source_target_pairs={{0,8},{1,9},{2,10},{3,11},{4,12},{5,13},{6,14},{7,15},{8,0},{9,1},... | collective-permute-start | bytes 3080 | tf_op jit(solution)/shard_map/ppermute | solution.py:503
  38.2 1.1 %prefixed.1 = (bf16[256,1024]{1,0:T(8,128)(2,1)S(1)}, bf16[256,1024]{1,0:T(8,128)(2,1)S(1)}, f32[1,1024]{1,0:T(1,128)S(1)}) custom-call(s32[1]{0:T(128)} %bitcast.7.pair_ref, s32[1]{0:T(128)} %bitcast.1.upper_ref, bf16[272,256]{1,0:T(8,128)(2,1)S(1)} %combined.1.refs_0_, bf16[272,256]{1,0:T(8,128)(2,1)S(1)} %collective-permute-done.2.refs_1_, ...), custom_call_target="tpu_custom_call" | custom-call | flops 603979776 | bytes 3145728 | tf_op jit(solution)/shard_map/prefixed/pallas_call | solution.py:353
  39.3 1.0 %collective-permute-done.5 = f32[1,256]{1,0:T(1,128)S(1)} collective-permute-done((f32[1,256]{1,0:T(1,128)S(1)}, f32[1,256]{1,0:T(1,128)S(1)}, u32[]{:S(2)}, u32[]{:S(2)}) %collective-permute-start.5) | collective-permute-done | bytes 1056 | tf_op jit(solution)/shard_map/ppermute | solution.py:503
  40.4 0.3 filtered.1
  40.7 12.2 %all_to_all.10.gathered_ref = f32[16,4,256]{2,1,0:T(4,128)S(1)} all-to-all(f32[16,4,256]{2,1,0:T(4,128)S(1)} %broadcast_in_dim.24), channel_id=1, replica_groups=mesh['spec'=2,'tm'=16] {'tm'}, dimensions={0} | all-to-all | bytes 131072 | tf_op jit(solution)/shard_map/all_to_all | solution.py:534
  52.9 0.0 copy-done
  52.9 2.6 %finish.1 = (f32[4,256]{1,0:T(4,128)}, bf16[64,1024]{1,0:T(8,128)(2,1)}) custom-call(s32[1]{0:T(128)} %bitcast.index_ref, f32[16,4,256]{2,1,0:T(4,128)S(1)} %all_to_all.10.gathered_ref, bf16[5,256,256]{2,1,0:T(8,128)(2,1)S(1)} %get-tuple-element.40.high_ref, bf16[5,256,256]{2,1,0:T(8,128)(2,1)S(1)} %get-tuple-element.41.low_ref, f32[1,256]{1,0:T(1,128)S(1)} %bitcast.21, ...), custom_call_target="tpu_custom_call" | custom-call | flops 33554432 | bytes 2097152 | tf_op jit(solution)/shard_map/finish/pallas_call | solution.py:470
  (3 shorter events, 0.0 us)
Async XLA Ops:
  0.6 9.6 %copy-start.4 = (s32[16384]{0:T(1024)S(1)}, s32[16384]{0:T(1024)}, u32[]{:S(2)}) copy-start(s32[16384]{0:T(1024)} %param.14) | copy-start | bytes 196612
  0.6 9.6 %copy-start.3 = (s32[16384]{0:T(1024)S(1)}, s32[16384]{0:T(1024)}, u32[]{:S(2)}) copy-start(s32[16384]{0:T(1024)} %param.13) | copy-start | bytes 196612
  0.7 9.6 %copy-start.2 = (s32[16384]{0:T(1024)S(1)}, s32[16384]{0:T(1024)}, u32[]{:S(2)}) copy-start(s32[16384]{0:T(1024)} %param.12) | copy-start | bytes 196612
  0.7 9.6 %copy-start.1 = (f32[16384]{0:T(1024)S(1)}, f32[16384]{0:T(1024)}, u32[]{:S(2)}) copy-start(f32[16384]{0:T(1024)} %param.11) | copy-start | bytes 196612
  0.7 9.6 %copy-start.5 = (bf16[256,256]{1,0:T(8,128)(2,1)S(1)}, bf16[256,256]{1,0:T(8,128)(2,1)}, u32[]{:S(2)}) copy-start(bf16[256,256]{1,0:T(8,128)(2,1)} %gain_ref.1) | copy-start | bytes 393220
  0.7 9.6 %copy-start.6 = (f32[256]{0:T(256)S(1)}, f32[256]{0:T(256)}, u32[]{:S(2)}) copy-start(f32[256]{0:T(256)} %param.15) | copy-start | bytes 3076
  2.9 19.4 %all-to-all-start = ((f32[16,4,256]{2,1,0:T(4,128)}), f32[16,4,256]{2,1,0:T(4,128)S(1)}, u32[]{:S(2)}, u32[]{:S(2)}) async-start(f32[16,4,256]{2,1,0:T(4,128)} %partial_drive.1), calls=%async_computation | async-start | bytes 131072 | tf_op jit(solution)/shard_map/all_to_all | solution.py:507
  10.3 18.3 %copy-start.7 = (f32[256,256]{1,0:T(8,128)S(1)}, f32[256,256]{1,0:T(8,128)}, u32[]{:S(2)}) copy-start(f32[256,256]{1,0:T(8,128)} %in_ref) | copy-start | bytes 786436
  10.3 42.6 %copy-start = (bf16[64,1024]{1,0:T(8,128)(2,1)S(1)}, bf16[64,1024]{1,0:T(8,128)(2,1)}, u32[]{:S(2)}) copy-start(bf16[64,1024]{1,0:T(8,128)(2,1)} %series_hbm.3) | copy-start | bytes 393220
  22.3 2.5 %collective-permute-start = (bf16[256,256]{1,0:T(8,128)(2,1)S(1)}, bf16[256,256]{1,0:T(8,128)(2,1)S(1)}, u32[]{:S(2)}, u32[]{:S(2)}) collective-permute-start(bf16[256,256]{1,0:T(8,128)(2,1)S(1)} %get-tuple-element.30), channel_id=1, source_target_pairs={{0,1},{1,0},{2,3},{3,2},{4,5},{5,4},{6,7},{7,6},{8,9},{9,8},{10,11... | collective-permute-start | bytes 393224 | tf_op jit(solution)/shard_map/ppermute | solution.py:503
  23.6 1.2 %collective-permute-start.1 = (f32[2,256]{1,0:T(2,128)S(1)}, f32[2,256]{1,0:T(2,128)S(1)}, u32[]{:S(2)}, u32[]{:S(2)}) collective-permute-start(f32[2,256]{1,0:T(2,128)S(1)} %get-tuple-element.29.packet_ref), channel_id=1, source_target_pairs={{0,1},{1,0},{2,3},{3,2},{4,5},{5,4},{6,7},{7,6},{8,9},{9,8},{10,11... | collective-permute-start | bytes 6152 | tf_op jit(solution)/shard_map/ppermute | solution.py:503
  25.1 7.5 %collective-permute-start.4 = (bf16[272,256]{1,0:T(8,128)(2,1)S(1)}, bf16[272,256]{1,0:T(8,128)(2,1)S(1)}, u32[]{:S(2)}, u32[]{:S(2)}) collective-permute-start(bf16[272,256]{1,0:T(8,128)(2,1)S(1)} %combined.1.refs_0_), channel_id=1, source_target_pairs={{0,6},{1,7},{2,4},{3,5},{4,2},{5,3},{6,0},{7,1},{8,14},{9,15},{10,... | collective-permute-start | bytes 417800 | tf_op jit(solution)/shard_map/ppermute | solution.py:503
  27.7 7.5 %collective-permute-start.3 = (bf16[272,256]{1,0:T(8,128)(2,1)S(1)}, bf16[272,256]{1,0:T(8,128)(2,1)S(1)}, u32[]{:S(2)}, u32[]{:S(2)}) collective-permute-start(bf16[272,256]{1,0:T(8,128)(2,1)S(1)} %combined.1.refs_0_), channel_id=1, source_target_pairs={{0,4},{1,5},{2,6},{3,7},{4,0},{5,1},{6,2},{7,3},{8,12},{9,13},{10,... | collective-permute-start | bytes 417800 | tf_op jit(solution)/shard_map/ppermute | solution.py:503
  28.3 6.9 %collective-permute-start.2 = (bf16[272,256]{1,0:T(8,128)(2,1)S(1)}, bf16[272,256]{1,0:T(8,128)(2,1)S(1)}, u32[]{:S(2)}, u32[]{:S(2)}) collective-permute-start(bf16[272,256]{1,0:T(8,128)(2,1)S(1)} %combined.1.refs_0_), channel_id=1, source_target_pairs={{0,2},{1,3},{2,0},{3,1},{4,6},{5,7},{6,4},{7,5},{8,10},{9,11},{10,... | collective-permute-start | bytes 417800 | tf_op jit(solution)/shard_map/ppermute | solution.py:503
  35.9 4.5 %collective-permute-start.5 = (f32[1,256]{1,0:T(1,128)S(1)}, f32[1,256]{1,0:T(1,128)S(1)}, u32[]{:S(2)}, u32[]{:S(2)}) collective-permute-start(f32[1,256]{1,0:T(1,128)S(1)} %advanced.1), channel_id=1, source_target_pairs={{0,8},{1,9},{2,10},{3,11},{4,12},{5,13},{6,14},{7,15},{8,0},{9,1},... | collective-permute-start | bytes 3080 | tf_op jit(solution)/shard_map/ppermute | solution.py:503

commit v5 on v4

--- a/solution.py
+++ b/solution.py
@@ -117,16 +117,15 @@
     )(index, series, loadings, *tables)
 
 
-def transitions_of(first_day, day_count, loadings, tables, decay, gain):
+def damped_of(first_day, day_count, loadings, tables, decay):
     providers, factors = loadings.shape
     unit = providers // 16
     sizes = [unit, unit, 2 * unit, 4 * unit, 8 * unit]
     parts = [slice(sum(sizes[:n]), sum(sizes[: n + 1])) for n in range(len(sizes))]
 
     def kernel(
-        day_ref, load_hbm, prec_hbm, start_hbm, stop_hbm, off_hbm, decay_hbm, gain_hbm,
-        step_ref, run_ref, last_ref, rest_ref, diag_ref,
-        acc, load_ref, prec_ref, start_ref, stop_ref, off_ref, decay_ref, gain_ref, sems,
+        day_ref, decay_ref, load_hbm, prec_hbm, start_hbm, stop_hbm, off_hbm, out_ref, acc, load_ref,
+        prec_ref, start_ref, stop_ref, off_ref, sems,
     ):
         pairs = [
             (prec_hbm, prec_ref),
@@ -135,13 +134,13 @@
             (off_hbm, off_ref),
         ]
         pairs += [(load_hbm.at[part], load_ref.at[part]) for part in parts]
-        pairs += [(decay_hbm, decay_ref), (gain_hbm, gain_ref)]
         copies = [
             pltpu.make_async_copy(source, target, sems.at[n])
             for n, (source, target) in enumerate(pairs)
         ]
         for copy in copies:
             copy.start()
+        column = jnp.sum(jnp.where(eye(factors), decay_ref[...], 0.0), axis=1, keepdims=True)
         for copy in copies[:4]:
             copy.wait()
         for n, part in enumerate(parts):
@@ -154,40 +153,18 @@
                 )
                 mask = active.astype(F32).astype(BF16)
                 term = mul(scaled * mask, block)
-                acc[d] = term if n == 0 else acc[d] + term
-        for copy in copies[4 + len(parts) :]:
-            copy.wait()
-        same = eye(factors)
-        diagonal = jnp.where(same, decay_ref[...], 0.0)
-        column = jnp.sum(diagonal, axis=1, keepdims=True)
-        steps_of = []
-        for d in range(day_count):
-            damped = (acc[d] * column).astype(BF16)
-            pulled = lax.dot_general(
-                damped, gain_ref[...], (((1,), (1,)), ((), ())), preferred_element_type=F32
-            )
-            steps_of.append(diagonal - pulled)
-        running = steps_of[0]
-        for d in range(1, day_count):
-            run_ref[d - 1] = running
-            step_ref[d - 1] = steps_of[d]
-            running = product(running, split(steps_of[d]))
-        last = running
-        last_ref[...] = last
-        rest_ref[...] = jnp.where(same, 0.0, last).astype(BF16)
-        diag_ref[...] = jnp.sum(jnp.where(same, last, 0.0), axis=0, keepdims=True)
-
-    return pl.pallas_call(
-        kernel,
-        in_specs=[smem()] + hbm(7),
-        out_specs=vmem(5),
-        out_shape=[
-            shape(day_count - 1, factors, factors),
-            shape(day_count - 1, factors, factors),
-            shape(factors, factors),
-            shape(factors, factors, dtype=BF16),
-            shape(1, factors),
-        ],
+                if n == 0:
+                    acc[d] = term
+                elif n < len(parts) - 1:
+                    acc[d] += term
+                else:
+                    out_ref[d] = ((acc[d] + term) * column).astype(BF16)
+
+    return pl.pallas_call(
+        kernel,
+        in_specs=[smem()] + vmem(1) + hbm(5),
+        out_specs=pl.BlockSpec(memory_space=VMEM),
+        out_shape=shape(day_count, factors, factors, dtype=BF16),
         scratch_shapes=[
             pltpu.VMEM((day_count, factors, factors), F32),
             pltpu.VMEM((providers, factors), BF16),
@@ -195,99 +172,116 @@
             pltpu.VMEM((1, providers), jnp.int32),
             pltpu.VMEM((1, providers), jnp.int32),
             pltpu.VMEM((1, providers), jnp.int32),
-            pltpu.VMEM((1, factors), F32),
-            pltpu.VMEM((factors, factors), BF16),
-            pltpu.SemaphoreType.DMA((6 + len(parts),)),
+            pltpu.SemaphoreType.DMA((4 + len(parts),)),
         ],
         compiler_params=params(),
         cost_estimate=cost(2 * day_count * providers * factors * factors, 10 << 20),
-        name="transitions",
-    )(first_day, loadings, *tables, decay, gain)
-
-
-def own_states(terms, steps, gain, diag):
+        name="damped",
+    )(first_day, decay, loadings, *tables)
+
+
+PACKED = 16
+
+
+def unpacked(packed_ref):
+    factors = packed_ref.shape[1]
+    rows = packed_ref[factors:].astype(F32)
+    return packed_ref[:factors], rows[2:3] + rows[3:4], rows[0:1] + rows[1:2]
+
+
+def pack(packed_ref, total, tail, same):
+    factors = total.shape[0]
+    packed_ref[:factors] = jnp.where(same, 0.0, total).astype(BF16)
+    diag = jnp.sum(jnp.where(same, total, 0.0), axis=0, keepdims=True)
+    rows = [*split(tail), *split(diag), jnp.zeros((PACKED - 4, factors), BF16)]
+    packed_ref[factors:] = jnp.concatenate(rows, 0)
+
+
+def through(a, rest, diag):
+    high, low = split(a)
+    return mul(high, rest) + mul(low, rest) + a * diag
+
+
+def block_of(damped, terms, decay, gain):
     parts, day_count, factors = terms.shape
 
-    def kernel(terms_ref, step_ref, gain_ref, diag_ref, out_ref, packet_ref):
+    def kernel(
+        damped_ref, terms_ref, decay_ref, gain_ref, run_ref, last_ref, states_ref, tail_ref, packed_ref
+    ):
+        same = eye(factors)
+        weights = gain_ref[...]
+        dims = (((1,), (1,)), ((), ()))
         drive = terms_ref[0]
         for p in range(1, parts):
             drive = drive + terms_ref[p]
         high, low = split(drive)
-        weights = gain_ref[...]
-        dims = (((1,), (1,)), ((), ()))
-        rest = (drive - high.astype(F32) - low.astype(F32)).astype(BF16)
+        least = (drive - high.astype(F32) - low.astype(F32)).astype(BF16)
         offsets = sum(
             lax.dot_general(part, weights, dims, preferred_element_type=F32)
-            for part in (high, low, rest)
+            for part in (high, low, least)
         )
-        state = offsets[0:1]
-        out_ref[0:1] = state
-        for d in range(1, day_count):
-            state = product(state, split(step_ref[d - 1])) + offsets[d : d + 1]
-            out_ref[d : d + 1] = state
-        packet_ref[0:1] = state
-        packet_ref[1:2] = diag_ref[...]
+        diagonal = jnp.where(same, decay_ref[...], 0.0)
+        for d in range(day_count):
+            step = diagonal - lax.dot_general(
+                damped_ref[d], weights, dims, preferred_element_type=F32
+            )
+            if d == 0:
+                running, state = step, offsets[0:1]
+            else:
+                run_ref[d - 1] = running
+                step = split(step)
+                running = product(running, step)
+                state = product(state, step) + offsets[d : d + 1]
+            states_ref[d : d + 1] = state
+        last_ref[...] = running
+        tail_ref[...] = state
+        pack(packed_ref, running, state, same)
 
     return pl.pallas_call(
         kernel,
         in_specs=vmem(4),
-        out_specs=vmem(2),
-        out_shape=[shape(day_count, factors), shape(2, factors)],
-        compiler_params=params(),
-        cost_estimate=cost(20 * factors * factors * 8, 1 << 20),
-        name="own_states",
-    )(terms, steps, gain, diag)
-
-
-PACKED = 16
-
-
-def unpacked(packed_ref):
-    factors = packed_ref.shape[1]
-    rows = packed_ref[factors:].astype(F32)
-    return packed_ref[:factors], rows[2:3] + rows[3:4], rows[0:1] + rows[1:2]
-
-
-def through(a, rest, diag):
-    high, low = split(a)
-    return mul(high, rest) + mul(low, rest) + a * diag
-
-
-def combined(upper, matrix, packet, other_rest, other_packet):
+        out_specs=vmem(5),
+        out_shape=[
+            shape(day_count - 1, factors, factors),
+            shape(factors, factors),
+            shape(day_count, factors),
+            shape(1, factors),
+            shape(factors + PACKED, factors, dtype=BF16),
+        ],
+        compiler_params=params(),
+        cost_estimate=cost(50 * factors**3, 3 << 20),
+        name="block",
+    )(damped, terms, decay, gain)
+
+
+def combined(upper, matrix, tail, other):
     factors = matrix.shape[0]
 
-    def kernel(upper_ref, mine_ref, packet_ref, rest_ref, other_ref, packed_ref):
+    def kernel(upper_ref, mine_ref, tail_ref, other_ref, packed_ref):
         same = eye(factors)
-
-        def pack(total, tail):
-            packed_ref[:factors] = jnp.where(same, 0.0, total).astype(BF16)
-            diag = jnp.sum(jnp.where(same, total, 0.0), axis=0, keepdims=True)
-            rows = [*split(tail), *split(diag), jnp.zeros((PACKED - 4, factors), BF16)]
-            packed_ref[factors:] = jnp.concatenate(rows, 0)
+        rest, diag, other_tail = unpacked(other_ref)
 
         @pl.when(upper_ref[0] == 1)
         def _():
             mine = split(mine_ref[...])
-            theirs = rest_ref[...].astype(F32) + jnp.where(same, other_ref[1:2], 0.0)
-            pack(product(theirs, mine), product(other_ref[0:1], mine) + packet_ref[0:1])
+            theirs = rest.astype(F32) + jnp.where(same, diag, 0.0)
+            total = product(theirs, mine)
+            pack(packed_ref, total, product(other_tail, mine) + tail_ref[...], same)
 
         @pl.when(upper_ref[0] == 0)
         def _():
-            rest, diag = rest_ref[...], other_ref[1:2]
-            pack(
-                through(mine_ref[...], rest, diag),
-                through(packet_ref[0:1], rest, diag) + other_ref[0:1],
-            )
-
-    return pl.pallas_call(
-        kernel,
-        in_specs=[smem()] + vmem(4),
+            total = through(mine_ref[...], rest, diag)
+            pack(packed_ref, total, through(tail_ref[...], rest, diag) + other_tail, same)
+
+    return pl.pallas_call(
+        kernel,
+        in_specs=[smem()] + vmem(3),
         out_specs=pl.BlockSpec(memory_space=VMEM),
         out_shape=shape(factors + PACKED, factors, dtype=BF16),
         compiler_params=params(),
         cost_estimate=cost(6 * factors**3, 1 << 20),
         name="combined",
-    )(upper, matrix, packet, other_rest, other_packet)
+    )(upper, matrix, tail, other)
 
 
 def advanced(pair, state, pieces):
@@ -316,13 +310,13 @@
     )(pair, state, *pieces)
 
 
-def prefixed(pair, upper, pieces, other_rest, other_packet, running, last, states):
+def prefixed(pair, upper, pieces, other, running, last, states):
     day_count, factors = states.shape
     count = len(pieces)
 
     def kernel(pair_ref, upper_ref, *refs):
-        rest_ref, packet_ref, run_ref, last_ref, states_ref = refs[count : count + 5]
-        high_ref, low_ref, add_ref, work, tail = refs[count + 5 :]
+        other_ref, run_ref, last_ref, states_ref = refs[count : count + 4]
+        high_ref, low_ref, add_ref, work, tail = refs[count + 4 :]
         work[...] = jnp.where(eye(factors), 1.0, 0.0)
         tail[...] = jnp.zeros_like(tail)
 
@@ -339,7 +333,7 @@
 
         @pl.when(upper_ref[0] == 1)
         def _():
-            follow(rest_ref[...], packet_ref[1:2], packet_ref[0:1])
+            follow(*unpacked(other_ref))
 
         for d in range(day_count):
             step = split(run_ref[d] if d < day_count - 1 else last_ref[...])
@@ -352,7 +346,7 @@
     wide = day_count * factors
     return pl.pallas_call(
         kernel,
-        in_specs=[smem()] * 2 + vmem(count + 5),
+        in_specs=[smem()] * 2 + vmem(count + 4),
         out_specs=vmem(3),
         out_shape=[
             shape(factors, wide, dtype=BF16),
@@ -363,7 +357,7 @@
         compiler_params=params(),
         cost_estimate=cost(36 * factors**3, 3 << 20),
         name="prefixed",
-    )(pair, upper, *pieces, other_rest, other_packet, running, last, states)
+    )(pair, upper, *pieces, other, running, last, states)
 
 
 def filtered_of(state, arrived, high, low, add):
@@ -505,13 +499,12 @@
     partial = partial_drive(index, devices, series, loadings, tables)
     partial, first_day = lax.optimization_barrier((partial, index * day_count))
     terms = lax.all_to_all(partial, "tm", 0, 0, tiled=True)
-    steps, running, mine, rest, diag = transitions_of(first_day, day_count, loadings, tables, decay, gain)
-    rest, terms = lax.optimization_barrier((rest, terms))
-    states, packet = own_states(terms, steps, gain, diag)
+    damped = damped_of(first_day, day_count, loadings, tables, decay)
+    running, last, states, tail, packed = block_of(damped, terms, decay, gain)
 
     upper = (place & 1)[None]
-    other_rest, other_packet = swapped(rest, 1), swapped(packet, 1)
-    packed = combined(upper, mine, packet, other_rest, other_packet)
+    other = swapped(packed, 1)
+    packed = combined(upper, last, tail, other)
     group = min(8, devices)
     pair = ((place % group) >> 1)[None]
     pieces = [packed] + [swapped(packed, 2 * m) for m in range(1, group // 2)]
@@ -520,7 +513,7 @@
     nothing = jnp.zeros((1, factors), F32)
     nothing, powers = lax.optimization_barrier((nothing, powers))
     tail = advanced(pair, nothing, pieces)
-    ahead = prefixed(pair, upper, pieces, other_rest, other_packet, running, mine, states)
+    ahead = prefixed(pair, upper, pieces, other, running, last, states)
 
     state = nothing
     arrived = jnp.where(place // group == 1, swapped(tail, group), 0.0)

time: 56 us -> 55 us (0.982)
  Pallas kernels: 21.2 us -> 20.5 us
    pallas_call x4, Pallas kernels: 14.1 us -> 13.3 us  [the longest x1 10.6 us: damped_of(): pl.pallas_call(kernel, in_specs=[smem()] + vmem(1) + hbm(5), out_specs=pl...]
    ppermute x6 -> x5, waiting for transfers between devices: 7.3 us -> 7.19 us  [swapped(): lax.ppermute(array, 'tm', [(i, i ^ distance) for i in range(devices)])]
    ppermute x6 -> x5, starting transfers between devices: 6.53 us -> 6.42 us  [swapped(): lax.ppermute(array, 'tm', [(i, i ^ distance) for i in range(devices)])]
  transfers between devices with their start and end apart: 7 -> 6, of which waited for: 4 -> 4; matrix products, arithmetic and copies ran while one was open for 0% -> 0% of each run, Pallas kernels for 27% -> 24%
where the time goes in v5:
time: 55 us; the launch traced here: 54.7 us
  Pallas kernels  20.5 us (37%)
  starting transfers between devices  13.8 us (25%)
  blocking collectives  12.2 us (22%)
  waiting for transfers between devices  7.19 us (13%)
  between operations  0.97 us (2%)
    all_to_all x1, blocking collectives, local(): lax.all_to_all(jnp.broadcast_to(own, (devices, day_count, factors)), 'tm'...  12.2 us
    pallas_call x1, Pallas kernels, damped_of(): pl.pallas_call(kernel, in_specs=[smem()] + vmem(1) + hbm(5), out_specs=pl...  10.6 us
    all_to_all x1, starting transfers between devices, local(): terms = lax.all_to_all(partial, 'tm', 0, 0, tiled=True)  7.4 us
    ppermute x5, waiting for transfers between devices, swapped(): lax.ppermute(array, 'tm', [(i, i ^ distance) for i in range(devices)])  7.19 us
    ppermute x5, starting transfers between devices, swapped(): lax.ppermute(array, 'tm', [(i, i ^ distance) for i in range(devices)])  6.42 us
    pallas_call x1, Pallas kernels, finish(): pl.pallas_call(kernel, in_specs=[smem()] + vmem(4) + hbm(6), out_specs=vm...  2.65 us
    pallas_call x1, Pallas kernels, partial_drive(): pl.pallas_call(kernel, in_specs=[smem()] + hbm(6), out_specs=pl.BlockSpec...  2.15 us
    pallas_call x1, Pallas kernels, smoother_powers(): pl.pallas_call(kernel, in_specs=vmem(1), out_specs=vmem(2), out_shape=[sh...  1.41 us
  transfers between devices with their start and end apart: 6, of which 4 were waited for; matrix products, arithmetic and copies ran while one was open for 0% of the time, Pallas kernels for 24%

profile of v5, /device:TPU:0, one launch (start us, length us, event | category | flops | bytes accessed | tf_op | source)
XLA Modules:
  0.0 54.7 jit_solution(10025678455467032024)
XLA Ops:
  0.6 0.0 copy-start.4
  0.6 0.0 copy-start.3
  0.7 0.0 copy-start.2
  0.7 0.0 copy-start.1
  0.7 0.0 copy-start.5
  0.7 2.1 %partial_drive.1 = f32[16,4,256]{2,1,0:T(4,128)} custom-call(s32[1]{0:T(128)} %bitcast.index_ref, bf16[64,1024]{1,0:T(8,128)(2,1)} %series_hbm.3, bf16[16384,256]{1,0:T(8,128)(2,1)} %load_hbm.5, f32[1,16384]{1,0:T(1,128)} %bitcast.8, s32[1,16384]{1,0:T(1,128)} %bitcast.11, s32[1,16384]{1,0:T(1,128)} %bitcast.14, s32[1,16384]{1,0:T(1,128)} %bitcast.17), custom_call_target="tpu_custom_call" | custom-call | flops 33554432 | bytes 1048576 | tf_op jit(solution)/shard_map/partial_drive/pallas_call | solution.py:100
  2.8 7.4 %all-to-all-start = ((f32[16,4,256]{2,1,0:T(4,128)}), f32[16,4,256]{2,1,0:T(4,128)S(1)}, u32[]{:S(2)}, u32[]{:S(2)}) async-start(f32[16,4,256]{2,1,0:T(4,128)} %partial_drive.1), calls=%async_computation | async-start | bytes 131072 | tf_op jit(solution)/shard_map/all_to_all | solution.py:501
  10.2 0.0 copy-done.4
  10.3 0.0 copy-done.3
  10.3 0.0 copy-done.2
  10.3 0.0 copy-done.1
  10.3 0.0 copy-done.5
  10.3 0.0 copy-start.7
  10.3 0.0 copy-start.6
  10.3 10.6 %damped.1.damped_ref = bf16[4,256,256]{2,1,0:T(8,128)(2,1)S(1)} custom-call(s32[1]{0:T(128)S(6)} %mul.3.day_ref, f32[1,256]{1,0:T(1,128)S(1)} %bitcast.20, bf16[16384,256]{1,0:T(8,128)(2,1)} %load_hbm.5, f32[1,16384]{1,0:T(1,128)S(1)} %bitcast.9, s32[1,16384]{1,0:T(1,128)S(1)} %bitcast.12, s32[1,16384]{1,0:T(1,128)S(1)} %bitcast.15, s32[1,16384]{1,0:T(1,128)S(1)} %bitcast.18), custom_call_target="tpu_custom_call" | custom-call | flops 8589934592 | bytes 10485760 | tf_op jit(solution)/shard_map/damped/pallas_call | solution.py:163
  21.0 0.0 copy-start
  21.0 0.0 all-to-all-done.terms_ref
  21.0 0.0 copy-done.7
  21.0 1.3 %block.1 = (f32[3,256,256]{2,1,0:T(8,128)S(1)}, f32[256,256]{1,0:T(8,128)S(1)}, f32[4,256]{1,0:T(4,128)S(1)}, f32[1,256]{1,0:T(1,128)S(1)}, bf16[272,256]{1,0:T(8,128)(2,1)S(1)}) custom-call(bf16[4,256,256]{2,1,0:T(8,128)(2,1)S(1)} %damped.1.damped_ref, f32[16,4,256]{2,1,0:T(4,128)S(1)} %all-to-all-done.terms_ref, f32[1,256]{1,0:T(1,128)S(1)} %bitcast.21, ...), custom_call_target="tpu_custom_call" | custom-call | flops 838860800 | bytes 3145728 | tf_op jit(solution)/shard_map/block/pallas_call | solution.py:240
  22.3 0.5 collective-permute-start
  22.8 1.0 %collective-permute-done.other_ref.refs_4_ = bf16[272,256]{1,0:T(8,128)(2,1)S(1)} collective-permute-done((bf16[272,256]{1,0:T(8,128)(2,1)S(1)}, bf16[272,256]{1,0:T(8,128)(2,1)S(1)}, u32[]{:S(2)}, u32[]{:S(2)}) %collective-permute-start) | collective-permute-done | bytes 139296 | tf_op jit(solution)/shard_map/ppermute | solution.py:497
  23.8 0.3 combined.1.refs_0_
  24.1 2.8 %collective-permute-start.3 = (bf16[272,256]{1,0:T(8,128)(2,1)S(1)}, bf16[272,256]{1,0:T(8,128)(2,1)S(1)}, u32[]{:S(2)}, u32[]{:S(2)}) collective-permute-start(bf16[272,256]{1,0:T(8,128)(2,1)S(1)} %combined.1.refs_0_), channel_id=1, source_target_pairs={{0,6},{1,7},{2,4},{3,5},{4,2},{5,3},{6,0},{7,1},{8,14},{9,15},{10,... | collective-permute-start | bytes 417800 | tf_op jit(solution)/shard_map/ppermute | solution.py:497
  26.9 0.5 collective-permute-start.2
  27.5 0.2 collective-permute-start.1
  27.6 0.0 copy-done.6
  27.6 1.4 %smoother_powers.1 = (bf16[5,256,256]{2,1,0:T(8,128)(2,1)S(1)}, bf16[5,256,256]{2,1,0:T(8,128)(2,1)S(1)}) custom-call(f32[256,256]{1,0:T(8,128)S(1)} %copy-done.6), custom_call_target="tpu_custom_call" | custom-call | flops 402653184 | bytes 2097152 | tf_op jit(solution)/shard_map/smoother_powers/pallas_call | solution.py:395
  29.1 2.5 %collective-permute-done.3.refs_3_ = bf16[272,256]{1,0:T(8,128)(2,1)S(1)} collective-permute-done((bf16[272,256]{1,0:T(8,128)(2,1)S(1)}, bf16[272,256]{1,0:T(8,128)(2,1)S(1)}, u32[]{:S(2)}, u32[]{:S(2)}) %collective-permute-start.3) | collective-permute-done | bytes 139296 | tf_op jit(solution)/shard_map/ppermute | solution.py:497
  31.5 2.7 %collective-permute-done.2.refs_2_ = bf16[272,256]{1,0:T(8,128)(2,1)S(1)} collective-permute-done((bf16[272,256]{1,0:T(8,128)(2,1)S(1)}, bf16[272,256]{1,0:T(8,128)(2,1)S(1)}, u32[]{:S(2)}, u32[]{:S(2)}) %collective-permute-start.2) | collective-permute-done | bytes 139296 | tf_op jit(solution)/shard_map/ppermute | solution.py:497
  34.2 0.0 collective-permute-done.1.refs_1_
  34.3 0.6 %advanced.1 = f32[1,256]{1,0:T(1,128)S(1)} custom-call(s32[1]{0:T(128)} %bitcast.7.pair_ref, f32[1,256]{1,0:T(1,128)S(1)} %broadcast_in_dim.21.state_ref, bf16[272,256]{1,0:T(8,128)(2,1)S(1)} %combined.1.refs_0_, bf16[272,256]{1,0:T(8,128)(2,1)S(1)} %collective-permute-done.1.refs_1_, bf16[272,256]{1,0:T(8,128)(2,1)S(1)} %collective-permute-done.2.refs_2_, ...), custom_call_target="tpu_custom_call" | custom-call | flops 786432 | bytes 262144 | tf_op jit(solution)/shard_map/advanced/pallas_call | solution.py:302
  34.9 2.4 %collective-permute-start.4 = (f32[1,256]{1,0:T(1,128)S(1)}, f32[1,256]{1,0:T(1,128)S(1)}, u32[]{:S(2)}, u32[]{:S(2)}) collective-permute-start(f32[1,256]{1,0:T(1,128)S(1)} %advanced.1), channel_id=1, source_target_pairs={{0,8},{1,9},{2,10},{3,11},{4,12},{5,13},{6,14},{7,15},{8,0},{9,1},... | collective-permute-start | bytes 3080 | tf_op jit(solution)/shard_map/ppermute | solution.py:497
  37.3 1.1 %prefixed.1 = (bf16[256,1024]{1,0:T(8,128)(2,1)S(1)}, bf16[256,1024]{1,0:T(8,128)(2,1)S(1)}, f32[1,1024]{1,0:T(1,128)S(1)}) custom-call(s32[1]{0:T(128)} %bitcast.7.pair_ref, s32[1]{0:T(128)} %bitcast.1.upper_ref, bf16[272,256]{1,0:T(8,128)(2,1)S(1)} %combined.1.refs_0_, bf16[272,256]{1,0:T(8,128)(2,1)S(1)} %collective-permute-done.1.refs_1_, ...), custom_call_target="tpu_custom_call" | custom-call | flops 603979776 | bytes 3145728 | tf_op jit(solution)/shard_map/prefixed/pallas_call | solution.py:347
  38.3 1.0 %collective-permute-done.4 = f32[1,256]{1,0:T(1,128)S(1)} collective-permute-done((f32[1,256]{1,0:T(1,128)S(1)}, f32[1,256]{1,0:T(1,128)S(1)}, u32[]{:S(2)}, u32[]{:S(2)}) %collective-permute-start.4) | collective-permute-done | bytes 1056 | tf_op jit(solution)/shard_map/ppermute | solution.py:497
  39.4 0.3 filtered.1
  39.7 12.2 %all_to_all.10.gathered_ref = f32[16,4,256]{2,1,0:T(4,128)S(1)} all-to-all(f32[16,4,256]{2,1,0:T(4,128)S(1)} %broadcast_in_dim.24), channel_id=1, replica_groups=mesh['spec'=2,'tm'=16] {'tm'}, dimensions={0} | all-to-all | bytes 131072 | tf_op jit(solution)/shard_map/all_to_all | solution.py:527
  51.9 0.0 copy-done
  51.9 2.6 %finish.1 = (f32[4,256]{1,0:T(4,128)}, bf16[64,1024]{1,0:T(8,128)(2,1)}) custom-call(s32[1]{0:T(128)} %bitcast.index_ref, f32[16,4,256]{2,1,0:T(4,128)S(1)} %all_to_all.10.gathered_ref, bf16[5,256,256]{2,1,0:T(8,128)(2,1)S(1)} %get-tuple-element.32.high_ref, bf16[5,256,256]{2,1,0:T(8,128)(2,1)S(1)} %get-tuple-element.33.low_ref, f32[1,256]{1,0:T(1,128)S(1)} %bitcast.22, ...), custom_call_target="tpu_custom_call" | custom-call | flops 33554432 | bytes 2097152 | tf_op jit(solution)/shard_map/finish/pallas_call | solution.py:464
  (3 shorter events, 0.0 us)
Async XLA Ops:
  0.6 9.6 %copy-start.4 = (s32[16384]{0:T(1024)S(1)}, s32[16384]{0:T(1024)}, u32[]{:S(2)}) copy-start(s32[16384]{0:T(1024)} %param.14) | copy-start | bytes 196612
  0.6 9.6 %copy-start.3 = (s32[16384]{0:T(1024)S(1)}, s32[16384]{0:T(1024)}, u32[]{:S(2)}) copy-start(s32[16384]{0:T(1024)} %param.13) | copy-start | bytes 196612
  0.7 9.6 %copy-start.2 = (s32[16384]{0:T(1024)S(1)}, s32[16384]{0:T(1024)}, u32[]{:S(2)}) copy-start(s32[16384]{0:T(1024)} %param.12) | copy-start | bytes 196612
  0.7 9.6 %copy-start.1 = (f32[16384]{0:T(1024)S(1)}, f32[16384]{0:T(1024)}, u32[]{:S(2)}) copy-start(f32[16384]{0:T(1024)} %param.11) | copy-start | bytes 196612
  0.7 9.6 %copy-start.5 = (f32[256]{0:T(256)S(1)}, f32[256]{0:T(256)}, u32[]{:S(2)}) copy-start(f32[256]{0:T(256)} %param.15) | copy-start | bytes 3076
  2.8 18.1 %all-to-all-start = ((f32[16,4,256]{2,1,0:T(4,128)}), f32[16,4,256]{2,1,0:T(4,128)S(1)}, u32[]{:S(2)}, u32[]{:S(2)}) async-start(f32[16,4,256]{2,1,0:T(4,128)} %partial_drive.1), calls=%async_computation | async-start | bytes 131072 | tf_op jit(solution)/shard_map/all_to_all | solution.py:501
  10.3 10.7 %copy-start.7 = (bf16[256,256]{1,0:T(8,128)(2,1)S(1)}, bf16[256,256]{1,0:T(8,128)(2,1)}, u32[]{:S(2)}) copy-start(bf16[256,256]{1,0:T(8,128)(2,1)} %gain_ref.1) | copy-start | bytes 393220
  10.3 17.3 %copy-start.6 = (f32[256,256]{1,0:T(8,128)S(1)}, f32[256,256]{1,0:T(8,128)}, u32[]{:S(2)}) copy-start(f32[256,256]{1,0:T(8,128)} %in_ref) | copy-start | bytes 786436
  21.0 30.9 %copy-start = (bf16[64,1024]{1,0:T(8,128)(2,1)S(1)}, bf16[64,1024]{1,0:T(8,128)(2,1)}, u32[]{:S(2)}) copy-start(bf16[64,1024]{1,0:T(8,128)(2,1)} %series_hbm.3) | copy-start | bytes 393220
  22.3 1.5 %collective-permute-start = (bf16[272,256]{1,0:T(8,128)(2,1)S(1)}, bf16[272,256]{1,0:T(8,128)(2,1)S(1)}, u32[]{:S(2)}, u32[]{:S(2)}) collective-permute-start(bf16[272,256]{1,0:T(8,128)(2,1)S(1)} %get-tuple-element.22), channel_id=1, source_target_pairs={{0,1},{1,0},{2,3},{3,2},{4,5},{5,4},{6,7},{7,6},{8,9},{9,8},{10,11... | collective-permute-start | bytes 417800 | tf_op jit(solution)/shard_map/ppermute | solution.py:497
  24.1 7.4 %collective-permute-start.3 = (bf16[272,256]{1,0:T(8,128)(2,1)S(1)}, bf16[272,256]{1,0:T(8,128)(2,1)S(1)}, u32[]{:S(2)}, u32[]{:S(2)}) collective-permute-start(bf16[272,256]{1,0:T(8,128)(2,1)S(1)} %combined.1.refs_0_), channel_id=1, source_target_pairs={{0,6},{1,7},{2,4},{3,5},{4,2},{5,3},{6,0},{7,1},{8,14},{9,15},{10,... | collective-permute-start | bytes 417800 | tf_op jit(solution)/shard_map/ppermute | solution.py:497
  26.9 7.3 %collective-permute-start.2 = (bf16[272,256]{1,0:T(8,128)(2,1)S(1)}, bf16[272,256]{1,0:T(8,128)(2,1)S(1)}, u32[]{:S(2)}, u32[]{:S(2)}) collective-permute-start(bf16[272,256]{1,0:T(8,128)(2,1)S(1)} %combined.1.refs_0_), channel_id=1, source_target_pairs={{0,4},{1,5},{2,6},{3,7},{4,0},{5,1},{6,2},{7,3},{8,12},{9,13},{10,... | collective-permute-start | bytes 417800 | tf_op jit(solution)/shard_map/ppermute | solution.py:497
  27.5 6.8 %collective-permute-start.1 = (bf16[272,256]{1,0:T(8,128)(2,1)S(1)}, bf16[272,256]{1,0:T(8,128)(2,1)S(1)}, u32[]{:S(2)}, u32[]{:S(2)}) collective-permute-start(bf16[272,256]{1,0:T(8,128)(2,1)S(1)} %combined.1.refs_0_), channel_id=1, source_target_pairs={{0,2},{1,3},{2,0},{3,1},{4,6},{5,7},{6,4},{7,5},{8,10},{9,11},{10,... | collective-permute-start | bytes 417800 | tf_op jit(solution)/shard_map/ppermute | solution.py:497
  34.9 4.5 %collective-permute-start.4 = (f32[1,256]{1,0:T(1,128)S(1)}, f32[1,256]{1,0:T(1,128)S(1)}, u32[]{:S(2)}, u32[]{:S(2)}) collective-permute-start(f32[1,256]{1,0:T(1,128)S(1)} %advanced.1), channel_id=1, source_target_pairs={{0,8},{1,9},{2,10},{3,11},{4,12},{5,13},{6,14},{7,15},{8,0},{9,1},... | collective-permute-start | bytes 3080 | tf_op jit(solution)/shard_map/ppermute | solution.py:497

commit v6 on v5

--- a/solution.py
+++ b/solution.py
@@ -48,7 +48,11 @@
 
 def product(a, b):
     high, low = split(a)
-    return mul(high, b[0]) + mul(low, b[0]) + mul(high, b[1])
+    rows = a.shape[0]
+    if rows > 64:
+        return mul(high, b[0]) + mul(low, b[0]) + mul(high, b[1])
+    both = mul(jnp.concatenate([high, low], 0), b[0])
+    return both[:rows] + both[rows:] + mul(high, b[1])
 
 
 def eye(factors):
@@ -198,8 +202,12 @@
 
 
 def through(a, rest, diag):
+    rows = a.shape[0]
     high, low = split(a)
-    return mul(high, rest) + mul(low, rest) + a * diag
+    if rows > 64:
+        return mul(high, rest) + mul(low, rest) + a * diag
+    both = mul(jnp.concatenate([high, low], 0), rest)
+    return both[:rows] + both[rows:] + a * diag
 
 
 def block_of(damped, terms, decay, gain):
@@ -284,7 +292,7 @@
     )(upper, matrix, tail, other)
 
 
-def advanced(pair, state, pieces):
+def advanced(pair, state, pieces, nothing=False):
     count = len(pieces)
     factors = pieces[0].shape[1]
 
@@ -297,7 +305,10 @@
                 @pl.when((pair_ref[0] ^ m) == turn)
                 def _():
                     rest, diag, tail = unpacked(refs[m])
-                    out_ref[...] = through(out_ref[...], rest, diag) + tail
+                    if nothing and turn == 0:
+                        out_ref[...] = tail
+                    else:
+                        out_ref[...] = through(out_ref[...], rest, diag) + tail
 
     return pl.pallas_call(
         kernel,
@@ -338,9 +349,7 @@
         for d in range(day_count):
             step = split(run_ref[d] if d < day_count - 1 else last_ref[...])
             place = slice(d * factors, (d + 1) * factors)
-            high, low = split(product(work[...], step))
-            high_ref[:, place] = high
-            low_ref[:, place] = low
+            high_ref[:, place], low_ref[:, place] = split(product(work[...], step))
             add_ref[:, place] = product(tail[...], step) + states_ref[d : d + 1]
 
     wide = day_count * factors
@@ -381,56 +390,74 @@
     )(state, arrived, high, low, add)
 
 
-def smoother_powers(smoother):
+def prepared(index, days, own, smoother, loadings, tables):
     factors = smoother.shape[0]
 
-    def kernel(in_ref, high_ref, low_ref):
+    def kernel(
+        index_ref, in_ref, load_hbm, prec_hbm, start_hbm, stop_hbm, off_hbm, high_ref, low_ref,
+        load_ref, scale_ref, prec_ref, start_ref, stop_ref, off_ref, sems,
+    ):
+        mine = pl.ds(pl.multiple_of(index_ref[0] * own, own), own)
+        copies = [
+            pltpu.make_async_copy(source, target, sems.at[n])
+            for n, (source, target) in enumerate(
+                [
+                    (prec_hbm.at[:, mine], prec_ref),
+                    (start_hbm.at[:, mine], start_ref),
+                    (stop_hbm.at[:, mine], stop_ref),
+                    (off_hbm.at[:, mine], off_ref),
+                    (load_hbm.at[mine], load_ref),
+                ]
+            )
+        ]
+        for copy in copies:
+            copy.start()
         power = in_ref[...].T
         for p in range(POWERS):
             parts = split(power)
             high_ref[p], low_ref[p] = parts
             if p < POWERS - 1:
                 power = product(power, parts)
-
-    return pl.pallas_call(
-        kernel,
-        in_specs=vmem(1),
-        out_specs=vmem(2),
-        out_shape=[shape(POWERS, factors, factors, dtype=BF16)] * 2,
-        compiler_params=params(),
-        cost_estimate=cost(24 * factors**3, 2 << 20),
-        name="smoother_powers",
-    )(smoother)
-
-
-def finish(index, day_count, gathered, powers, decay, series, loadings, tables):
+        for copy in copies:
+            copy.wait()
+        day = lax.broadcasted_iota(jnp.int32, (days, 1), 0)
+        active = activity(day, start_ref[...], stop_ref[...], off_ref[...])
+        scale_ref[...] = jnp.where(active, jnp.sqrt(prec_ref[...]), 0.0)
+
+    return pl.pallas_call(
+        kernel,
+        in_specs=[smem()] + vmem(1) + hbm(5),
+        out_specs=vmem(4),
+        out_shape=[
+            shape(POWERS, factors, factors, dtype=BF16),
+            shape(POWERS, factors, factors, dtype=BF16),
+            shape(own, factors, dtype=BF16),
+            shape(days, own),
+        ],
+        scratch_shapes=[
+            pltpu.VMEM((1, own), F32),
+            pltpu.VMEM((1, own), jnp.int32),
+            pltpu.VMEM((1, own), jnp.int32),
+            pltpu.VMEM((1, own), jnp.int32),
+            pltpu.SemaphoreType.DMA((5,)),
+        ],
+        compiler_params=params(),
+        cost_estimate=cost(24 * factors**3, 3 << 20),
+        name="prepared",
+    )(index, smoother, loadings, *tables)
+
+
+def finish(index, day_count, gathered, ready, decay, series):
     days, own = series.shape
-    factors = loadings.shape[1]
+    factors = decay.shape[1]
     stride = 2 ** (POWERS - 1)
     blocks = days // stride
 
     def kernel(
-        index_ref, gathered_ref, high_ref, low_ref, decay_ref, series_hbm, load_hbm, prec_hbm,
-        start_hbm, stop_hbm, off_hbm, smooth_ref, score_ref, filt, work, series_ref, load_ref,
-        prec_ref, start_ref, stop_ref, off_ref, sems,
+        index_ref, gathered_ref, high_ref, low_ref, load_ref, scale_ref, decay_ref, series_ref,
+        smooth_ref, score_ref, filt, work,
     ):
         me = index_ref[0]
-        mine = pl.ds(pl.multiple_of(me * own, own), own)
-        copies = [
-            pltpu.make_async_copy(source, target, sems.at[n])
-            for n, (source, target) in enumerate(
-                [
-                    (load_hbm.at[mine], load_ref),
-                    (series_hbm, series_ref),
-                    (prec_hbm.at[:, mine], prec_ref),
-                    (start_hbm.at[:, mine], start_ref),
-                    (stop_hbm.at[:, mine], stop_ref),
-                    (off_hbm.at[:, mine], off_ref),
-                ]
-            )
-        ]
-        for copy in copies:
-            copy.start()
         for m in range(days // day_count):
             filt[m * day_count : (m + 1) * day_count, :] = gathered_ref[m]
         filtered = filt[...]
@@ -450,37 +477,26 @@
         work[...] += carried
         for d in range(day_count):
             smooth_ref[d : d + 1, :] = work[pl.ds(me * day_count + d, 1), :]
-        for copy in copies:
-            copy.wait()
         fitted = lax.dot_general(
             work[...].astype(BF16), load_ref[...], (((1,), (1,)), ((), ())),
             preferred_element_type=F32,
         )
-        day = lax.broadcasted_iota(jnp.int32, (days, 1), 0)
-        active = activity(day, start_ref[...], stop_ref[...], off_ref[...])
-        residual = (series_ref[...].astype(F32) - fitted) * jnp.sqrt(prec_ref[...])
-        score_ref[...] = jnp.where(active, residual, 0.0).astype(BF16)
-
-    return pl.pallas_call(
-        kernel,
-        in_specs=[smem()] + vmem(4) + hbm(6),
+        residual = series_ref[...].astype(F32) - fitted
+        score_ref[...] = (residual * scale_ref[...]).astype(BF16)
+
+    return pl.pallas_call(
+        kernel,
+        in_specs=[smem()] + vmem(7),
         out_specs=vmem(2),
         out_shape=[shape(day_count, factors), shape(days, own, dtype=BF16)],
         scratch_shapes=[
             pltpu.VMEM((days, factors), F32),
             pltpu.VMEM((days, factors), F32),
-            pltpu.VMEM((days, own), BF16),
-            pltpu.VMEM((own, factors), BF16),
-            pltpu.VMEM((1, own), F32),
-            pltpu.VMEM((1, own), jnp.int32),
-            pltpu.VMEM((1, own), jnp.int32),
-            pltpu.VMEM((1, own), jnp.int32),
-            pltpu.SemaphoreType.DMA((6,)),
         ],
         compiler_params=params(),
         cost_estimate=cost(2 * days * own * factors, 2 << 20),
         name="finish",
-    )(index, gathered, *powers, decay, series, loadings, *tables)
+    )(index, gathered, *ready, decay, series)
 
 
 def local(series, loadings, precision, start_day, stop_day, off_day, decay, gain, smoother):
@@ -509,10 +525,10 @@
     pair = ((place % group) >> 1)[None]
     pieces = [packed] + [swapped(packed, 2 * m) for m in range(1, group // 2)]
     smoother, packed = lax.optimization_barrier((smoother, packed))
-    powers = smoother_powers(smoother)
+    ready = prepared(index, days, series.shape[1], smoother, loadings, tables)
     nothing = jnp.zeros((1, factors), F32)
-    nothing, powers = lax.optimization_barrier((nothing, powers))
-    tail = advanced(pair, nothing, pieces)
+    nothing, ready = lax.optimization_barrier((nothing, ready))
+    tail = advanced(pair, nothing, pieces, True)
     ahead = prefixed(pair, upper, pieces, other, running, last, states)
 
     state = nothing
@@ -527,7 +543,7 @@
     gathered = lax.all_to_all(
         jnp.broadcast_to(own, (devices, day_count, factors)), "tm", 0, 0, tiled=True
     )
-    return tuple(finish(index, day_count, gathered, powers, decay, series, loadings, tables))
+    return tuple(finish(index, day_count, gathered, ready, decay, series))
 
 
 def solution(mesh):

time: 55 us -> 54.1 us (0.984)
  Pallas kernels: 20.5 us -> 19.8 us
  transfers between devices with their start and end apart: 6 -> 6, of which waited for: 4 -> 4; matrix products, arithmetic and copies ran while one was open for 0% -> 0% of each run, Pallas kernels for 24% -> 25%
where the time goes in v6:
time: 54.1 us; the launch traced here: 53.8 us
  Pallas kernels  19.8 us (37%)
  starting transfers between devices  13.8 us (26%)
  blocking collectives  12.2 us (23%)
  waiting for transfers between devices  7.15 us (13%)
  between operations  0.82 us (2%)
    all_to_all x1, blocking collectives, local(): lax.all_to_all(jnp.broadcast_to(own, (devices, day_count, factors)), 'tm'...  12.2 us
    pallas_call x1, Pallas kernels, damped_of(): pl.pallas_call(kernel, in_specs=[smem()] + vmem(1) + hbm(5), out_specs=pl...  10.6 us
    all_to_all x1, starting transfers between devices, local(): terms = lax.all_to_all(partial, 'tm', 0, 0, tiled=True)  7.4 us
    ppermute x5, waiting for transfers between devices, swapped(): lax.ppermute(array, 'tm', [(i, i ^ distance) for i in range(devices)])  7.15 us
    ppermute x5, starting transfers between devices, swapped(): lax.ppermute(array, 'tm', [(i, i ^ distance) for i in range(devices)])  6.42 us
    pallas_call x1, Pallas kernels, partial_drive(): pl.pallas_call(kernel, in_specs=[smem()] + hbm(6), out_specs=pl.BlockSpec...  2.15 us
    pallas_call x1, Pallas kernels, finish(): pl.pallas_call(kernel, in_specs=[smem()] + vmem(7), out_specs=vmem(2), ou...  2.07 us
    pallas_call x1, Pallas kernels, prepared(): pl.pallas_call(kernel, in_specs=[smem()] + vmem(1) + hbm(5), out_specs=vm...  1.55 us
  transfers between devices with their start and end apart: 6, of which 4 were waited for; matrix products, arithmetic and copies ran while one was open for 0% of the time, Pallas kernels for 25%

profile of v6, /device:TPU:0, one launch (start us, length us, event | category | flops | bytes accessed | tf_op | source)
XLA Modules:
  0.0 53.8 jit_solution(11465105912559562528)
XLA Ops:
  0.6 0.0 copy-start.4
  0.6 0.0 copy-start.3
  0.7 0.0 copy-start.2
  0.7 0.0 copy-start.1
  0.7 0.0 copy-start.6
  0.7 2.1 %partial_drive.1 = f32[16,4,256]{2,1,0:T(4,128)} custom-call(s32[1]{0:T(128)} %bitcast.index_ref, bf16[64,1024]{1,0:T(8,128)(2,1)} %series_ref.1, bf16[16384,256]{1,0:T(8,128)(2,1)} %load_hbm.5, f32[1,16384]{1,0:T(1,128)} %bitcast.8, s32[1,16384]{1,0:T(1,128)} %bitcast.11, s32[1,16384]{1,0:T(1,128)} %bitcast.14, s32[1,16384]{1,0:T(1,128)} %bitcast.17), custom_call_target="tpu_custom_call" | custom-call | flops 33554432 | bytes 1048576 | tf_op jit(solution)/shard_map/partial_drive/pallas_call | solution.py:104
  2.8 7.4 %all-to-all-start = ((f32[16,4,256]{2,1,0:T(4,128)}), f32[16,4,256]{2,1,0:T(4,128)S(1)}, u32[]{:S(2)}, u32[]{:S(2)}) async-start(f32[16,4,256]{2,1,0:T(4,128)} %partial_drive.1), calls=%async_computation | async-start | bytes 131072 | tf_op jit(solution)/shard_map/all_to_all | solution.py:517
  10.2 0.0 copy-done.4
  10.3 0.0 copy-done.3
  10.3 0.0 copy-done.2
  10.3 0.0 copy-done.1
  10.3 0.0 copy-done.6
  10.3 0.0 copy-start.7
  10.3 0.0 copy-start.5
  10.3 10.6 %damped.1.damped_ref = bf16[4,256,256]{2,1,0:T(8,128)(2,1)S(1)} custom-call(s32[1]{0:T(128)S(6)} %mul.3.day_ref, f32[1,256]{1,0:T(1,128)S(1)} %bitcast.20, bf16[16384,256]{1,0:T(8,128)(2,1)} %load_hbm.5, f32[1,16384]{1,0:T(1,128)S(1)} %bitcast.9, s32[1,16384]{1,0:T(1,128)S(1)} %bitcast.12, s32[1,16384]{1,0:T(1,128)S(1)} %bitcast.15, s32[1,16384]{1,0:T(1,128)S(1)} %bitcast.18), custom_call_target="tpu_custom_call" | custom-call | flops 8589934592 | bytes 10485760 | tf_op jit(solution)/shard_map/damped/pallas_call | solution.py:167
  21.0 0.0 copy-start
  21.0 0.0 all-to-all-done.terms_ref
  21.0 0.0 copy-done.7
  21.0 1.3 %block.1 = (f32[3,256,256]{2,1,0:T(8,128)S(1)}, f32[256,256]{1,0:T(8,128)S(1)}, f32[4,256]{1,0:T(4,128)S(1)}, f32[1,256]{1,0:T(1,128)S(1)}, bf16[272,256]{1,0:T(8,128)(2,1)S(1)}) custom-call(bf16[4,256,256]{2,1,0:T(8,128)(2,1)S(1)} %damped.1.damped_ref, f32[16,4,256]{2,1,0:T(4,128)S(1)} %all-to-all-done.terms_ref, f32[1,256]{1,0:T(1,128)S(1)} %bitcast.21, ...), custom_call_target="tpu_custom_call" | custom-call | flops 838860800 | bytes 3145728 | tf_op jit(solution)/shard_map/block/pallas_call | solution.py:248
  22.4 0.5 collective-permute-start
  22.8 1.0 %collective-permute-done.other_ref.refs_4_ = bf16[272,256]{1,0:T(8,128)(2,1)S(1)} collective-permute-done((bf16[272,256]{1,0:T(8,128)(2,1)S(1)}, bf16[272,256]{1,0:T(8,128)(2,1)S(1)}, u32[]{:S(2)}, u32[]{:S(2)}) %collective-permute-start) | collective-permute-done | bytes 139296 | tf_op jit(solution)/shard_map/ppermute | solution.py:513
  23.8 0.3 combined.1.refs_0_
  24.1 2.8 %collective-permute-start.3 = (bf16[272,256]{1,0:T(8,128)(2,1)S(1)}, bf16[272,256]{1,0:T(8,128)(2,1)S(1)}, u32[]{:S(2)}, u32[]{:S(2)}) collective-permute-start(bf16[272,256]{1,0:T(8,128)(2,1)S(1)} %combined.1.refs_0_), channel_id=1, source_target_pairs={{0,6},{1,7},{2,4},{3,5},{4,2},{5,3},{6,0},{7,1},{8,14},{9,15},{10,... | collective-permute-start | bytes 417800 | tf_op jit(solution)/shard_map/ppermute | solution.py:513
  27.0 0.5 %collective-permute-start.2 = (bf16[272,256]{1,0:T(8,128)(2,1)S(1)}, bf16[272,256]{1,0:T(8,128)(2,1)S(1)}, u32[]{:S(2)}, u32[]{:S(2)}) collective-permute-start(bf16[272,256]{1,0:T(8,128)(2,1)S(1)} %combined.1.refs_0_), channel_id=1, source_target_pairs={{0,4},{1,5},{2,6},{3,7},{4,0},{5,1},{6,2},{7,3},{8,12},{9,13},{10,... | collective-permute-start | bytes 417800 | tf_op jit(solution)/shard_map/ppermute | solution.py:513
  27.5 0.2 collective-permute-start.1
  27.7 0.0 copy-done.5
  27.7 1.6 %prepared.1 = (bf16[5,256,256]{2,1,0:T(8,128)(2,1)S(1)}, bf16[5,256,256]{2,1,0:T(8,128)(2,1)S(1)}, bf16[1024,256]{1,0:T(8,128)(2,1)S(1)}, f32[64,1024]{1,0:T(8,128)S(1)}) custom-call(s32[1]{0:T(128)} %bitcast.index_ref, f32[256,256]{1,0:T(8,128)S(1)} %copy-done.5, bf16[16384,256]{1,0:T(8,128)(2,1)} %load_hbm.5, f32[1,16384]{1,0:T(1,128)S(1)} %bitcast.10, ...), custom_call_target="tpu_custom_call" | custom-call | flops 402653184 | bytes 3145728 | tf_op jit(solution)/shard_map/prepared/pallas_call | solution.py:427
  29.2 2.3 %collective-permute-done.3.refs_3_ = bf16[272,256]{1,0:T(8,128)(2,1)S(1)} collective-permute-done((bf16[272,256]{1,0:T(8,128)(2,1)S(1)}, bf16[272,256]{1,0:T(8,128)(2,1)S(1)}, u32[]{:S(2)}, u32[]{:S(2)}) %collective-permute-start.3) | collective-permute-done | bytes 139296 | tf_op jit(solution)/shard_map/ppermute | solution.py:513
  31.6 2.7 %collective-permute-done.2.refs_2_ = bf16[272,256]{1,0:T(8,128)(2,1)S(1)} collective-permute-done((bf16[272,256]{1,0:T(8,128)(2,1)S(1)}, bf16[272,256]{1,0:T(8,128)(2,1)S(1)}, u32[]{:S(2)}, u32[]{:S(2)}) %collective-permute-start.2) | collective-permute-done | bytes 139296 | tf_op jit(solution)/shard_map/ppermute | solution.py:513
  34.3 0.0 collective-permute-done.1.refs_1_
  34.3 0.5 advanced.1
  34.8 2.4 %collective-permute-start.4 = (f32[1,256]{1,0:T(1,128)S(1)}, f32[1,256]{1,0:T(1,128)S(1)}, u32[]{:S(2)}, u32[]{:S(2)}) collective-permute-start(f32[1,256]{1,0:T(1,128)S(1)} %advanced.1), channel_id=1, source_target_pairs={{0,8},{1,9},{2,10},{3,11},{4,12},{5,13},{6,14},{7,15},{8,0},{9,1},... | collective-permute-start | bytes 3080 | tf_op jit(solution)/shard_map/ppermute | solution.py:513
  37.2 1.0 %prefixed.1 = (bf16[256,1024]{1,0:T(8,128)(2,1)S(1)}, bf16[256,1024]{1,0:T(8,128)(2,1)S(1)}, f32[1,1024]{1,0:T(1,128)S(1)}) custom-call(s32[1]{0:T(128)} %bitcast.7.pair_ref, s32[1]{0:T(128)} %bitcast.1.upper_ref, bf16[272,256]{1,0:T(8,128)(2,1)S(1)} %combined.1.refs_0_, bf16[272,256]{1,0:T(8,128)(2,1)S(1)} %collective-permute-done.1.refs_1_, ...), custom_call_target="tpu_custom_call" | custom-call | flops 603979776 | bytes 3145728 | tf_op jit(solution)/shard_map/prefixed/pallas_call | solution.py:356
  38.2 1.1 %collective-permute-done.4 = f32[1,256]{1,0:T(1,128)S(1)} collective-permute-done((f32[1,256]{1,0:T(1,128)S(1)}, f32[1,256]{1,0:T(1,128)S(1)}, u32[]{:S(2)}, u32[]{:S(2)}) %collective-permute-start.4) | collective-permute-done | bytes 1056 | tf_op jit(solution)/shard_map/ppermute | solution.py:513
  39.3 0.2 filtered.1
  39.6 12.2 %all_to_all.10.gathered_ref = f32[16,4,256]{2,1,0:T(4,128)S(1)} all-to-all(f32[16,4,256]{2,1,0:T(4,128)S(1)} %broadcast_in_dim.24), channel_id=1, replica_groups=mesh['spec'=2,'tm'=16] {'tm'}, dimensions={0} | all-to-all | bytes 131072 | tf_op jit(solution)/shard_map/all_to_all | solution.py:543
  51.7 0.0 copy-done
  51.8 2.1 %finish.1 = (f32[4,256]{1,0:T(4,128)}, bf16[64,1024]{1,0:T(8,128)(2,1)}) custom-call(s32[1]{0:T(128)} %bitcast.index_ref, f32[16,4,256]{2,1,0:T(4,128)S(1)} %all_to_all.10.gathered_ref, bf16[5,256,256]{2,1,0:T(8,128)(2,1)S(1)} %get-tuple-element.38.high_ref, bf16[5,256,256]{2,1,0:T(8,128)(2,1)S(1)} %get-tuple-element.39.low_ref, ...), custom_call_target="tpu_custom_call" | custom-call | flops 33554432 | bytes 2097152 | tf_op jit(solution)/shard_map/finish/pallas_call | solution.py:487
  (3 shorter events, 0.0 us)
Async XLA Ops:
  0.6 9.6 %copy-start.4 = (s32[16384]{0:T(1024)S(1)}, s32[16384]{0:T(1024)}, u32[]{:S(2)}) copy-start(s32[16384]{0:T(1024)} %param.14) | copy-start | bytes 196612
  0.6 9.6 %copy-start.3 = (s32[16384]{0:T(1024)S(1)}, s32[16384]{0:T(1024)}, u32[]{:S(2)}) copy-start(s32[16384]{0:T(1024)} %param.13) | copy-start | bytes 196612
  0.7 9.6 %copy-start.2 = (s32[16384]{0:T(1024)S(1)}, s32[16384]{0:T(1024)}, u32[]{:S(2)}) copy-start(s32[16384]{0:T(1024)} %param.12) | copy-start | bytes 196612
  0.7 9.6 %copy-start.1 = (f32[16384]{0:T(1024)S(1)}, f32[16384]{0:T(1024)}, u32[]{:S(2)}) copy-start(f32[16384]{0:T(1024)} %param.11) | copy-start | bytes 196612
  0.7 9.6 %copy-start.6 = (f32[256]{0:T(256)S(1)}, f32[256]{0:T(256)}, u32[]{:S(2)}) copy-start(f32[256]{0:T(256)} %param.15) | copy-start | bytes 3076
  2.8 18.1 %all-to-all-start = ((f32[16,4,256]{2,1,0:T(4,128)}), f32[16,4,256]{2,1,0:T(4,128)S(1)}, u32[]{:S(2)}, u32[]{:S(2)}) async-start(f32[16,4,256]{2,1,0:T(4,128)} %partial_drive.1), calls=%async_computation | async-start | bytes 131072 | tf_op jit(solution)/shard_map/all_to_all | solution.py:517
  10.3 10.7 %copy-start.7 = (bf16[256,256]{1,0:T(8,128)(2,1)S(1)}, bf16[256,256]{1,0:T(8,128)(2,1)}, u32[]{:S(2)}) copy-start(bf16[256,256]{1,0:T(8,128)(2,1)} %gain_ref.1) | copy-start | bytes 393220
  10.3 17.4 %copy-start.5 = (f32[256,256]{1,0:T(8,128)S(1)}, f32[256,256]{1,0:T(8,128)}, u32[]{:S(2)}) copy-start(f32[256,256]{1,0:T(8,128)} %in_ref) | copy-start | bytes 786436
  21.0 30.8 %copy-start = (bf16[64,1024]{1,0:T(8,128)(2,1)S(1)}, bf16[64,1024]{1,0:T(8,128)(2,1)}, u32[]{:S(2)}) copy-start(bf16[64,1024]{1,0:T(8,128)(2,1)} %series_ref.1) | copy-start | bytes 393220
  22.4 1.5 %collective-permute-start = (bf16[272,256]{1,0:T(8,128)(2,1)S(1)}, bf16[272,256]{1,0:T(8,128)(2,1)S(1)}, u32[]{:S(2)}, u32[]{:S(2)}) collective-permute-start(bf16[272,256]{1,0:T(8,128)(2,1)S(1)} %get-tuple-element.26), channel_id=1, source_target_pairs={{0,1},{1,0},{2,3},{3,2},{4,5},{5,4},{6,7},{7,6},{8,9},{9,8},{10,11... | collective-permute-start | bytes 417800 | tf_op jit(solution)/shard_map/ppermute | solution.py:513
  24.1 7.4 %collective-permute-start.3 = (bf16[272,256]{1,0:T(8,128)(2,1)S(1)}, bf16[272,256]{1,0:T(8,128)(2,1)S(1)}, u32[]{:S(2)}, u32[]{:S(2)}) collective-permute-start(bf16[272,256]{1,0:T(8,128)(2,1)S(1)} %combined.1.refs_0_), channel_id=1, source_target_pairs={{0,6},{1,7},{2,4},{3,5},{4,2},{5,3},{6,0},{7,1},{8,14},{9,15},{10,... | collective-permute-start | bytes 417800 | tf_op jit(solution)/shard_map/ppermute | solution.py:513
  27.0 7.3 %collective-permute-start.2 = (bf16[272,256]{1,0:T(8,128)(2,1)S(1)}, bf16[272,256]{1,0:T(8,128)(2,1)S(1)}, u32[]{:S(2)}, u32[]{:S(2)}) collective-permute-start(bf16[272,256]{1,0:T(8,128)(2,1)S(1)} %combined.1.refs_0_), channel_id=1, source_target_pairs={{0,4},{1,5},{2,6},{3,7},{4,0},{5,1},{6,2},{7,3},{8,12},{9,13},{10,... | collective-permute-start | bytes 417800 | tf_op jit(solution)/shard_map/ppermute | solution.py:513
  27.5 6.8 %collective-permute-start.1 = (bf16[272,256]{1,0:T(8,128)(2,1)S(1)}, bf16[272,256]{1,0:T(8,128)(2,1)S(1)}, u32[]{:S(2)}, u32[]{:S(2)}) collective-permute-start(bf16[272,256]{1,0:T(8,128)(2,1)S(1)} %combined.1.refs_0_), channel_id=1, source_target_pairs={{0,2},{1,3},{2,0},{3,1},{4,6},{5,7},{6,4},{7,5},{8,10},{9,11},{10,... | collective-permute-start | bytes 417800 | tf_op jit(solution)/shard_map/ppermute | solution.py:513
  34.8 4.5 %collective-permute-start.4 = (f32[1,256]{1,0:T(1,128)S(1)}, f32[1,256]{1,0:T(1,128)S(1)}, u32[]{:S(2)}, u32[]{:S(2)}) collective-permute-start(f32[1,256]{1,0:T(1,128)S(1)} %advanced.1), channel_id=1, source_target_pairs={{0,8},{1,9},{2,10},{3,11},{4,12},{5,13},{6,14},{7,15},{8,0},{9,1},... | collective-permute-start | bytes 3080 | tf_op jit(solution)/shard_map/ppermute | solution.py:513

commit v7 on v6

--- a/solution.py
+++ b/solution.py
@@ -1,3 +1,5 @@
+import itertools
+
 import jax
 import jax.numpy as jnp
 from jax import lax
@@ -190,23 +192,37 @@
 def unpacked(packed_ref):
     factors = packed_ref.shape[1]
     rows = packed_ref[factors:].astype(F32)
-    return packed_ref[:factors], rows[2:3] + rows[3:4], rows[0:1] + rows[1:2]
-
-
-def pack(packed_ref, total, tail, same):
+    return (packed_ref[:factors],), rows[2:3] + rows[3:4], rows[0:1] + rows[1:2]
+
+
+def joined(top_ref, bottom_ref):
+    half = top_ref.shape[0] - PACKED
+    rows = top_ref[half:].astype(F32)
+    return (top_ref[:half], bottom_ref[:half]), rows[2:3] + rows[3:4], rows[0:1] + rows[1:2]
+
+
+def pack(refs, total, tail, same):
     factors = total.shape[0]
-    packed_ref[:factors] = jnp.where(same, 0.0, total).astype(BF16)
+    half = factors // len(refs)
+    rest = jnp.where(same, 0.0, total).astype(BF16)
     diag = jnp.sum(jnp.where(same, total, 0.0), axis=0, keepdims=True)
     rows = [*split(tail), *split(diag), jnp.zeros((PACKED - 4, factors), BF16)]
-    packed_ref[factors:] = jnp.concatenate(rows, 0)
-
-
-def through(a, rest, diag):
+    for n, ref in enumerate(refs):
+        ref[:half] = rest[n * half : (n + 1) * half]
+        ref[half:] = jnp.concatenate(rows, 0)
+
+
+def through(a, rests, diag):
     rows = a.shape[0]
     high, low = split(a)
+    depth = a.shape[1] // len(rests)
+
+    def times(x):
+        return sum(mul(x[:, n * depth : (n + 1) * depth], r) for n, r in enumerate(rests))
+
     if rows > 64:
-        return mul(high, rest) + mul(low, rest) + a * diag
-    both = mul(jnp.concatenate([high, low], 0), rest)
+        return times(high) + times(low) + a * diag
+    both = times(jnp.concatenate([high, low], 0))
     return both[:rows] + both[rows:] + a * diag
 
 
@@ -243,7 +259,7 @@
             states_ref[d : d + 1] = state
         last_ref[...] = running
         tail_ref[...] = state
-        pack(packed_ref, running, state, same)
+        pack([packed_ref], running, state, same)
 
     return pl.pallas_call(
         kernel,
@@ -265,46 +281,47 @@
 def combined(upper, matrix, tail, other):
     factors = matrix.shape[0]
 
-    def kernel(upper_ref, mine_ref, tail_ref, other_ref, packed_ref):
+    def kernel(upper_ref, mine_ref, tail_ref, other_ref, sent_ref, kept_ref):
         same = eye(factors)
         rest, diag, other_tail = unpacked(other_ref)
 
         @pl.when(upper_ref[0] == 1)
         def _():
             mine = split(mine_ref[...])
-            theirs = rest.astype(F32) + jnp.where(same, diag, 0.0)
+            theirs = rest[0].astype(F32) + jnp.where(same, diag, 0.0)
             total = product(theirs, mine)
-            pack(packed_ref, total, product(other_tail, mine) + tail_ref[...], same)
+            pack([kept_ref, sent_ref], total, product(other_tail, mine) + tail_ref[...], same)
 
         @pl.when(upper_ref[0] == 0)
         def _():
             total = through(mine_ref[...], rest, diag)
-            pack(packed_ref, total, through(tail_ref[...], rest, diag) + other_tail, same)
+            tail = through(tail_ref[...], rest, diag) + other_tail
+            pack([sent_ref, kept_ref], total, tail, same)
 
     return pl.pallas_call(
         kernel,
         in_specs=[smem()] + vmem(3),
-        out_specs=pl.BlockSpec(memory_space=VMEM),
-        out_shape=shape(factors + PACKED, factors, dtype=BF16),
+        out_specs=vmem(2),
+        out_shape=[shape(factors // 2 + PACKED, factors, dtype=BF16)] * 2,
         compiler_params=params(),
         cost_estimate=cost(6 * factors**3, 1 << 20),
         name="combined",
     )(upper, matrix, tail, other)
 
 
-def advanced(pair, state, pieces, nothing=False):
+def advanced(pair, upper, state, pieces, nothing=False):
     count = len(pieces)
-    factors = pieces[0].shape[1]
-
-    def kernel(pair_ref, state_ref, *refs):
+    factors = state.shape[1]
+
+    def kernel(pair_ref, upper_ref, state_ref, *refs):
         out_ref = refs[-1]
         out_ref[...] = state_ref[...]
         for turn in range(count):
-            for m in range(count):
-
-                @pl.when((pair_ref[0] ^ m) == turn)
+            for m, core in itertools.product(range(count), range(2)):
+
+                @pl.when(((pair_ref[0] ^ m) == turn) & (upper_ref[0] == core))
                 def _():
-                    rest, diag, tail = unpacked(refs[m])
+                    rest, diag, tail = joined(refs[2 * m + core], refs[2 * m + 1 - core])
                     if nothing and turn == 0:
                         out_ref[...] = tail
                     else:
@@ -312,13 +329,13 @@
 
     return pl.pallas_call(
         kernel,
-        in_specs=[smem()] + vmem(count + 1),
+        in_specs=[smem()] * 2 + vmem(2 * count + 1),
         out_specs=pl.BlockSpec(memory_space=VMEM),
         out_shape=shape(1, factors),
         compiler_params=params(),
         cost_estimate=cost(12 * factors**2, 1 << 18),
         name="advanced",
-    )(pair, state, *pieces)
+    )(pair, upper, state, *[a for piece in pieces for a in piece])
 
 
 def prefixed(pair, upper, pieces, other, running, last, states):
@@ -326,8 +343,8 @@
     count = len(pieces)
 
     def kernel(pair_ref, upper_ref, *refs):
-        other_ref, run_ref, last_ref, states_ref = refs[count : count + 4]
-        high_ref, low_ref, add_ref, work, tail = refs[count + 4 :]
+        other_ref, run_ref, last_ref, states_ref = refs[2 * count : 2 * count + 4]
+        high_ref, low_ref, add_ref, work, tail = refs[2 * count + 4 :]
         work[...] = jnp.where(eye(factors), 1.0, 0.0)
         tail[...] = jnp.zeros_like(tail)
 
@@ -336,11 +353,12 @@
             tail[...] = through(tail[...], rest, diag) + add
 
         for turn in range(count - 1):
-            for m in range(1, count):
-
-                @pl.when(((pair_ref[0] ^ m) == turn) & (pair_ref[0] > turn))
+            for m, core in itertools.product(range(1, count), range(2)):
+                now = ((pair_ref[0] ^ m) == turn) & (pair_ref[0] > turn)
+
+                @pl.when(now & (upper_ref[0] == core))
                 def _():
-                    follow(*unpacked(refs[m]))
+                    follow(*joined(refs[2 * m + core], refs[2 * m + 1 - core]))
 
         @pl.when(upper_ref[0] == 1)
         def _():
@@ -355,7 +373,7 @@
     wide = day_count * factors
     return pl.pallas_call(
         kernel,
-        in_specs=[smem()] * 2 + vmem(count + 4),
+        in_specs=[smem()] * 2 + vmem(2 * count + 4),
         out_specs=vmem(3),
         out_shape=[
             shape(factors, wide, dtype=BF16),
@@ -366,7 +384,7 @@
         compiler_params=params(),
         cost_estimate=cost(36 * factors**3, 3 << 20),
         name="prefixed",
-    )(pair, upper, *pieces, other, running, last, states)
+    )(pair, upper, *[a for piece in pieces for a in piece], other, running, last, states)
 
 
 def filtered_of(state, arrived, high, low, add):
@@ -520,22 +538,23 @@
 
     upper = (place & 1)[None]
     other = swapped(packed, 1)
-    packed = combined(upper, last, tail, other)
+    sent, kept = combined(upper, last, tail, other)
     group = min(8, devices)
     pair = ((place % group) >> 1)[None]
-    pieces = [packed] + [swapped(packed, 2 * m) for m in range(1, group // 2)]
-    smoother, packed = lax.optimization_barrier((smoother, packed))
+    came = [swapped(sent, 2 * m) for m in range(1, group // 2)]
+    pieces = [(sent, kept)] + [(half, swapped(half, 1)) for half in came]
+    smoother, sent = lax.optimization_barrier((smoother, sent))
     ready = prepared(index, days, series.shape[1], smoother, loadings, tables)
     nothing = jnp.zeros((1, factors), F32)
     nothing, ready = lax.optimization_barrier((nothing, ready))
-    tail = advanced(pair, nothing, pieces, True)
+    tail = advanced(pair, upper, nothing, pieces, True)
     ahead = prefixed(pair, upper, pieces, other, running, last, states)
 
     state = nothing
     arrived = jnp.where(place // group == 1, swapped(tail, group), 0.0)
     for g in range(1, devices // group - 1):
         state = state + arrived
-        moved = advanced(pair, state, pieces)
+        moved = advanced(pair, upper, state, pieces)
         pairs = [(g * group + j, (g + 1) * group + j) for j in range(group)]
         arrived = lax.ppermute(moved, "tm", pairs)
 

time: 54.1 us -> 52.9 us (0.978)
  waiting for transfers between devices: 7.15 us -> 6.18 us
    ppermute x5 -> x8, waiting for transfers between devices: 7.15 us -> 6.18 us  [swapped(): lax.ppermute(array, 'tm', [(i, i ^ distance) for i in range(devices)])]
    ppermute x5 -> x8, starting transfers between devices: 6.42 us -> 6.53 us  [swapped(): lax.ppermute(array, 'tm', [(i, i ^ distance) for i in range(devices)])]
  transfers between devices with their start and end apart: 6 -> 9, of which waited for: 4 -> 5; matrix products, arithmetic and copies ran while one was open for 0% -> 0% of each run, Pallas kernels for 25% -> 25%
where the time goes in v7:
time: 52.9 us; the launch traced here: 52.7 us
  Pallas kernels  19.9 us (38%)
  starting transfers between devices  13.9 us (26%)
  blocking collectives  11.8 us (22%)
  waiting for transfers between devices  6.18 us (12%)
  between operations  0.85 us (2%)
    all_to_all x1, blocking collectives, local(): lax.all_to_all(jnp.broadcast_to(own, (devices, day_count, factors)), 'tm'...  11.8 us
    pallas_call x1, Pallas kernels, damped_of(): pl.pallas_call(kernel, in_specs=[smem()] + vmem(1) + hbm(5), out_specs=pl...  10.6 us
    all_to_all x1, starting transfers between devices, local(): terms = lax.all_to_all(partial, 'tm', 0, 0, tiled=True)  7.4 us
    ppermute x8, starting transfers between devices, swapped(): lax.ppermute(array, 'tm', [(i, i ^ distance) for i in range(devices)])  6.53 us
    ppermute x8, waiting for transfers between devices, swapped(): lax.ppermute(array, 'tm', [(i, i ^ distance) for i in range(devices)])  6.18 us
    pallas_call x1, Pallas kernels, partial_drive(): pl.pallas_call(kernel, in_specs=[smem()] + hbm(6), out_specs=pl.BlockSpec...  2.15 us
    pallas_call x1, Pallas kernels, finish(): pl.pallas_call(kernel, in_specs=[smem()] + vmem(7), out_specs=vmem(2), ou...  2.07 us
    pallas_call x1, Pallas kernels, prepared(): pl.pallas_call(kernel, in_specs=[smem()] + vmem(1) + hbm(5), out_specs=vm...  1.55 us
  transfers between devices with their start and end apart: 9, of which 5 were waited for; matrix products, arithmetic and copies ran while one was open for 0% of the time, Pallas kernels for 25%

profile of v7, /device:TPU:0, one launch (start us, length us, event | category | flops | bytes accessed | tf_op | source)
XLA Modules:
  0.0 52.7 jit_solution(17663650636590547758)
XLA Ops:
  0.6 0.0 copy-start.4
  0.6 0.0 copy-start.3
  0.7 0.0 copy-start.2
  0.7 0.0 copy-start.1
  0.7 0.0 copy-start.6
  0.7 2.1 %partial_drive.1 = f32[16,4,256]{2,1,0:T(4,128)} custom-call(s32[1]{0:T(128)} %bitcast.index_ref, bf16[64,1024]{1,0:T(8,128)(2,1)} %series_ref.1, bf16[16384,256]{1,0:T(8,128)(2,1)} %load_hbm.5, f32[1,16384]{1,0:T(1,128)} %bitcast.8, s32[1,16384]{1,0:T(1,128)} %bitcast.11, s32[1,16384]{1,0:T(1,128)} %bitcast.14, s32[1,16384]{1,0:T(1,128)} %bitcast.17), custom_call_target="tpu_custom_call" | custom-call | flops 33554432 | bytes 1048576 | tf_op jit(solution)/shard_map/partial_drive/pallas_call | solution.py:106
  2.8 7.4 %all-to-all-start = ((f32[16,4,256]{2,1,0:T(4,128)}), f32[16,4,256]{2,1,0:T(4,128)S(1)}, u32[]{:S(2)}, u32[]{:S(2)}) async-start(f32[16,4,256]{2,1,0:T(4,128)} %partial_drive.1), calls=%async_computation | async-start | bytes 131072 | tf_op jit(solution)/shard_map/all_to_all | solution.py:535
  10.2 0.0 copy-done.4
  10.3 0.0 copy-done.3
  10.3 0.0 copy-done.2
  10.3 0.0 copy-done.1
  10.3 0.0 copy-done.6
  10.3 0.0 copy-start.7
  10.3 0.0 copy-start.5
  10.3 10.6 %damped.1.damped_ref = bf16[4,256,256]{2,1,0:T(8,128)(2,1)S(1)} custom-call(s32[1]{0:T(128)S(6)} %mul.3.day_ref, f32[1,256]{1,0:T(1,128)S(1)} %bitcast.20, bf16[16384,256]{1,0:T(8,128)(2,1)} %load_hbm.5, f32[1,16384]{1,0:T(1,128)S(1)} %bitcast.9, s32[1,16384]{1,0:T(1,128)S(1)} %bitcast.12, s32[1,16384]{1,0:T(1,128)S(1)} %bitcast.15, s32[1,16384]{1,0:T(1,128)S(1)} %bitcast.18), custom_call_target="tpu_custom_call" | custom-call | flops 8589934592 | bytes 10485760 | tf_op jit(solution)/shard_map/damped/pallas_call | solution.py:169
  21.0 0.0 copy-start
  21.0 0.0 all-to-all-done.terms_ref
  21.0 0.0 copy-done.7
  21.0 1.3 %block.1 = (f32[3,256,256]{2,1,0:T(8,128)S(1)}, f32[256,256]{1,0:T(8,128)S(1)}, f32[4,256]{1,0:T(4,128)S(1)}, f32[1,256]{1,0:T(1,128)S(1)}, bf16[272,256]{1,0:T(8,128)(2,1)S(1)}) custom-call(bf16[4,256,256]{2,1,0:T(8,128)(2,1)S(1)} %damped.1.damped_ref, f32[16,4,256]{2,1,0:T(4,128)S(1)} %all-to-all-done.terms_ref, f32[1,256]{1,0:T(1,128)S(1)} %bitcast.21, ...), custom_call_target="tpu_custom_call" | custom-call | flops 838860800 | bytes 3145728 | tf_op jit(solution)/shard_map/block/pallas_call | solution.py:264
  22.3 0.5 collective-permute-start
  22.8 1.0 %collective-permute-done.other_ref.refs_8_ = bf16[272,256]{1,0:T(8,128)(2,1)S(1)} collective-permute-done((bf16[272,256]{1,0:T(8,128)(2,1)S(1)}, bf16[272,256]{1,0:T(8,128)(2,1)S(1)}, u32[]{:S(2)}, u32[]{:S(2)}) %collective-permute-start) | collective-permute-done | bytes 139296 | tf_op jit(solution)/shard_map/ppermute | solution.py:531
  23.8 0.3 combined.1
  24.1 2.8 %collective-permute-start.5 = (bf16[144,256]{1,0:T(8,128)(2,1)S(1)}, bf16[144,256]{1,0:T(8,128)(2,1)S(1)}, u32[]{:S(2)}, u32[]{:S(2)}) collective-permute-start(bf16[144,256]{1,0:T(8,128)(2,1)S(1)} %get-tuple-element.29.refs_0_), channel_id=1, source_target_pairs={{0,6},{1,7},{2,4},{3,5},{4,2},{5,3},{6,0},{7,1},{8,14},{9,15},{10,... | collective-permute-start | bytes 221192 | tf_op jit(solution)/shard_map/ppermute | solution.py:531
  27.0 0.5 %collective-permute-start.3 = (bf16[144,256]{1,0:T(8,128)(2,1)S(1)}, bf16[144,256]{1,0:T(8,128)(2,1)S(1)}, u32[]{:S(2)}, u32[]{:S(2)}) collective-permute-start(bf16[144,256]{1,0:T(8,128)(2,1)S(1)} %get-tuple-element.29.refs_0_), channel_id=1, source_target_pairs={{0,4},{1,5},{2,6},{3,7},{4,0},{5,1},{6,2},{7,3},{8,12},{9,13},{10,... | collective-permute-start | bytes 221192 | tf_op jit(solution)/shard_map/ppermute | solution.py:531
  27.5 0.2 collective-permute-start.1
  27.7 2.2 %collective-permute-done.5.refs_6_ = bf16[144,256]{1,0:T(8,128)(2,1)S(1)} collective-permute-done((bf16[144,256]{1,0:T(8,128)(2,1)S(1)}, bf16[144,256]{1,0:T(8,128)(2,1)S(1)}, u32[]{:S(2)}, u32[]{:S(2)}) %collective-permute-start.5) | collective-permute-done | bytes 73760 | tf_op jit(solution)/shard_map/ppermute | solution.py:531
  29.9 0.0 collective-permute-start.6
  29.9 1.5 %collective-permute-done.3.refs_4_ = bf16[144,256]{1,0:T(8,128)(2,1)S(1)} collective-permute-done((bf16[144,256]{1,0:T(8,128)(2,1)S(1)}, bf16[144,256]{1,0:T(8,128)(2,1)S(1)}, u32[]{:S(2)}, u32[]{:S(2)}) %collective-permute-start.3) | collective-permute-done | bytes 73760 | tf_op jit(solution)/shard_map/ppermute | solution.py:531
  31.4 0.0 collective-permute-start.4
  31.5 0.4 collective-permute-done.1.refs_2_
  31.9 0.1 collective-permute-start.2
  32.0 0.0 copy-done.5
  32.0 1.6 %prepared.1 = (bf16[5,256,256]{2,1,0:T(8,128)(2,1)S(1)}, bf16[5,256,256]{2,1,0:T(8,128)(2,1)S(1)}, bf16[1024,256]{1,0:T(8,128)(2,1)S(1)}, f32[64,1024]{1,0:T(8,128)S(1)}) custom-call(s32[1]{0:T(128)} %bitcast.index_ref, f32[256,256]{1,0:T(8,128)S(1)} %copy-done.5, bf16[16384,256]{1,0:T(8,128)(2,1)} %load_hbm.5, f32[1,16384]{1,0:T(1,128)S(1)} %bitcast.10, ...), custom_call_target="tpu_custom_call" | custom-call | flops 402653184 | bytes 3145728 | tf_op jit(solution)/shard_map/prepared/pallas_call | solution.py:445
  33.5 0.0 collective-permute-done.6.refs_7_
  33.5 0.0 collective-permute-done.4.refs_5_
  33.5 0.0 collective-permute-done.2.refs_3_
  33.6 0.5 advanced.1
  34.1 2.4 %collective-permute-start.7 = (f32[1,256]{1,0:T(1,128)S(1)}, f32[1,256]{1,0:T(1,128)S(1)}, u32[]{:S(2)}, u32[]{:S(2)}) collective-permute-start(f32[1,256]{1,0:T(1,128)S(1)} %advanced.1), channel_id=1, source_target_pairs={{0,8},{1,9},{2,10},{3,11},{4,12},{5,13},{6,14},{7,15},{8,0},{9,1},... | collective-permute-start | bytes 3080 | tf_op jit(solution)/shard_map/ppermute | solution.py:531
  36.5 1.1 %prefixed.1 = (bf16[256,1024]{1,0:T(8,128)(2,1)S(1)}, bf16[256,1024]{1,0:T(8,128)(2,1)S(1)}, f32[1,1024]{1,0:T(1,128)S(1)}) custom-call(s32[1]{0:T(128)} %bitcast.7.pair_ref, s32[1]{0:T(128)} %bitcast.1.upper_ref, bf16[144,256]{1,0:T(8,128)(2,1)S(1)} %get-tuple-element.29.refs_0_, bf16[144,256]{1,0:T(8,128)(2,1)S(1)} %get-tuple-element.36.refs_1_, ...), custom_call_target="tpu_custom_call" | custom-call | flops 603979776 | bytes 3145728 | tf_op jit(solution)/shard_map/prefixed/pallas_call | solution.py:374
  37.6 1.0 %collective-permute-done.7 = f32[1,256]{1,0:T(1,128)S(1)} collective-permute-done((f32[1,256]{1,0:T(1,128)S(1)}, f32[1,256]{1,0:T(1,128)S(1)}, u32[]{:S(2)}, u32[]{:S(2)}) %collective-permute-start.7) | collective-permute-done | bytes 1056 | tf_op jit(solution)/shard_map/ppermute | solution.py:531
  38.6 0.2 filtered.1
  38.8 11.8 %all_to_all.10.gathered_ref = f32[16,4,256]{2,1,0:T(4,128)S(1)} all-to-all(f32[16,4,256]{2,1,0:T(4,128)S(1)} %broadcast_in_dim.24), channel_id=1, replica_groups=mesh['spec'=2,'tm'=16] {'tm'}, dimensions={0} | all-to-all | bytes 131072 | tf_op jit(solution)/shard_map/all_to_all | solution.py:562
  50.6 0.0 copy-done
  50.6 2.1 %finish.1 = (f32[4,256]{1,0:T(4,128)}, bf16[64,1024]{1,0:T(8,128)(2,1)}) custom-call(s32[1]{0:T(128)} %bitcast.index_ref, f32[16,4,256]{2,1,0:T(4,128)S(1)} %all_to_all.10.gathered_ref, bf16[5,256,256]{2,1,0:T(8,128)(2,1)S(1)} %get-tuple-element.42.high_ref, bf16[5,256,256]{2,1,0:T(8,128)(2,1)S(1)} %get-tuple-element.43.low_ref, ...), custom_call_target="tpu_custom_call" | custom-call | flops 33554432 | bytes 2097152 | tf_op jit(solution)/shard_map/finish/pallas_call | solution.py:505
  (3 shorter events, 0.0 us)
Async XLA Ops:
  0.6 9.6 %copy-start.4 = (s32[16384]{0:T(1024)S(1)}, s32[16384]{0:T(1024)}, u32[]{:S(2)}) copy-start(s32[16384]{0:T(1024)} %param.14) | copy-start | bytes 196612
  0.6 9.6 %copy-start.3 = (s32[16384]{0:T(1024)S(1)}, s32[16384]{0:T(1024)}, u32[]{:S(2)}) copy-start(s32[16384]{0:T(1024)} %param.13) | copy-start | bytes 196612
  0.7 9.6 %copy-start.2 = (s32[16384]{0:T(1024)S(1)}, s32[16384]{0:T(1024)}, u32[]{:S(2)}) copy-start(s32[16384]{0:T(1024)} %param.12) | copy-start | bytes 196612
  0.7 9.6 %copy-start.1 = (f32[16384]{0:T(1024)S(1)}, f32[16384]{0:T(1024)}, u32[]{:S(2)}) copy-start(f32[16384]{0:T(1024)} %param.11) | copy-start | bytes 196612
  0.7 9.6 %copy-start.6 = (f32[256]{0:T(256)S(1)}, f32[256]{0:T(256)}, u32[]{:S(2)}) copy-start(f32[256]{0:T(256)} %param.15) | copy-start | bytes 3076
  2.8 18.1 %all-to-all-start = ((f32[16,4,256]{2,1,0:T(4,128)}), f32[16,4,256]{2,1,0:T(4,128)S(1)}, u32[]{:S(2)}, u32[]{:S(2)}) async-start(f32[16,4,256]{2,1,0:T(4,128)} %partial_drive.1), calls=%async_computation | async-start | bytes 131072 | tf_op jit(solution)/shard_map/all_to_all | solution.py:535
  10.3 10.7 %copy-start.7 = (bf16[256,256]{1,0:T(8,128)(2,1)S(1)}, bf16[256,256]{1,0:T(8,128)(2,1)}, u32[]{:S(2)}) copy-start(bf16[256,256]{1,0:T(8,128)(2,1)} %gain_ref.1) | copy-start | bytes 393220
  10.3 21.7 %copy-start.5 = (f32[256,256]{1,0:T(8,128)S(1)}, f32[256,256]{1,0:T(8,128)}, u32[]{:S(2)}) copy-start(f32[256,256]{1,0:T(8,128)} %in_ref) | copy-start | bytes 786436
  21.0 29.6 %copy-start = (bf16[64,1024]{1,0:T(8,128)(2,1)S(1)}, bf16[64,1024]{1,0:T(8,128)(2,1)}, u32[]{:S(2)}) copy-start(bf16[64,1024]{1,0:T(8,128)(2,1)} %series_ref.1) | copy-start | bytes 393220
  22.3 1.5 %collective-permute-start = (bf16[272,256]{1,0:T(8,128)(2,1)S(1)}, bf16[272,256]{1,0:T(8,128)(2,1)S(1)}, u32[]{:S(2)}, u32[]{:S(2)}) collective-permute-start(bf16[272,256]{1,0:T(8,128)(2,1)S(1)} %get-tuple-element.28), channel_id=1, source_target_pairs={{0,1},{1,0},{2,3},{3,2},{4,5},{5,4},{6,7},{7,6},{8,9},{9,8},{10,11... | collective-permute-start | bytes 417800 | tf_op jit(solution)/shard_map/ppermute | solution.py:531
  24.1 5.8 %collective-permute-start.5 = (bf16[144,256]{1,0:T(8,128)(2,1)S(1)}, bf16[144,256]{1,0:T(8,128)(2,1)S(1)}, u32[]{:S(2)}, u32[]{:S(2)}) collective-permute-start(bf16[144,256]{1,0:T(8,128)(2,1)S(1)} %get-tuple-element.29.refs_0_), channel_id=1, source_target_pairs={{0,6},{1,7},{2,4},{3,5},{4,2},{5,3},{6,0},{7,1},{8,14},{9,15},{10,... | collective-permute-start | bytes 221192 | tf_op jit(solution)/shard_map/ppermute | solution.py:531
  27.0 4.5 %collective-permute-start.3 = (bf16[144,256]{1,0:T(8,128)(2,1)S(1)}, bf16[144,256]{1,0:T(8,128)(2,1)S(1)}, u32[]{:S(2)}, u32[]{:S(2)}) collective-permute-start(bf16[144,256]{1,0:T(8,128)(2,1)S(1)} %get-tuple-element.29.refs_0_), channel_id=1, source_target_pairs={{0,4},{1,5},{2,6},{3,7},{4,0},{5,1},{6,2},{7,3},{8,12},{9,13},{10,... | collective-permute-start | bytes 221192 | tf_op jit(solution)/shard_map/ppermute | solution.py:531
  27.5 4.4 %collective-permute-start.1 = (bf16[144,256]{1,0:T(8,128)(2,1)S(1)}, bf16[144,256]{1,0:T(8,128)(2,1)S(1)}, u32[]{:S(2)}, u32[]{:S(2)}) collective-permute-start(bf16[144,256]{1,0:T(8,128)(2,1)S(1)} %get-tuple-element.29.refs_0_), channel_id=1, source_target_pairs={{0,2},{1,3},{2,0},{3,1},{4,6},{5,7},{6,4},{7,5},{8,10},{9,11},{10,... | collective-permute-start | bytes 221192 | tf_op jit(solution)/shard_map/ppermute | solution.py:531
  29.9 3.6 %collective-permute-start.6 = (bf16[144,256]{1,0:T(8,128)(2,1)S(1)}, bf16[144,256]{1,0:T(8,128)(2,1)S(1)}, u32[]{:S(2)}, u32[]{:S(2)}) collective-permute-start(bf16[144,256]{1,0:T(8,128)(2,1)S(1)} %collective-permute-done.5.refs_6_), channel_id=1, source_target_pairs={{0,1},{1,0},{2,3},{3,2},{4,5},{5,4},{6,7},{7,6},{8,9},{9,8},{10,11... | collective-permute-start | bytes 221192 | tf_op jit(solution)/shard_map/ppermute | solution.py:531
  31.4 2.1 %collective-permute-start.4 = (bf16[144,256]{1,0:T(8,128)(2,1)S(1)}, bf16[144,256]{1,0:T(8,128)(2,1)S(1)}, u32[]{:S(2)}, u32[]{:S(2)}) collective-permute-start(bf16[144,256]{1,0:T(8,128)(2,1)S(1)} %collective-permute-done.3.refs_4_), channel_id=1, source_target_pairs={{0,1},{1,0},{2,3},{3,2},{4,5},{5,4},{6,7},{7,6},{8,9},{9,8},{10,11... | collective-permute-start | bytes 221192 | tf_op jit(solution)/shard_map/ppermute | solution.py:531
  31.9 1.7 %collective-permute-start.2 = (bf16[144,256]{1,0:T(8,128)(2,1)S(1)}, bf16[144,256]{1,0:T(8,128)(2,1)S(1)}, u32[]{:S(2)}, u32[]{:S(2)}) collective-permute-start(bf16[144,256]{1,0:T(8,128)(2,1)S(1)} %collective-permute-done.1.refs_2_), channel_id=1, source_target_pairs={{0,1},{1,0},{2,3},{3,2},{4,5},{5,4},{6,7},{7,6},{8,9},{9,8},{10,11... | collective-permute-start | bytes 221192 | tf_op jit(solution)/shard_map/ppermute | solution.py:531
  34.1 4.5 %collective-permute-start.7 = (f32[1,256]{1,0:T(1,128)S(1)}, f32[1,256]{1,0:T(1,128)S(1)}, u32[]{:S(2)}, u32[]{:S(2)}) collective-permute-start(f32[1,256]{1,0:T(1,128)S(1)} %advanced.1), channel_id=1, source_target_pairs={{0,8},{1,9},{2,10},{3,11},{4,12},{5,13},{6,14},{7,15},{8,0},{9,1},... | collective-permute-start | bytes 3080 | tf_op jit(solution)/shard_map/ppermute | solution.py:531

commit v8 on v7

--- a/solution.py
+++ b/solution.py
@@ -543,11 +543,10 @@
     pair = ((place % group) >> 1)[None]
     came = [swapped(sent, 2 * m) for m in range(1, group // 2)]
     pieces = [(sent, kept)] + [(half, swapped(half, 1)) for half in came]
-    smoother, sent = lax.optimization_barrier((smoother, sent))
+    nothing = jnp.zeros((1, factors), F32)
+    tail = advanced(pair, upper, nothing, pieces, True)
+    smoother, tail = lax.optimization_barrier((smoother, tail))
     ready = prepared(index, days, series.shape[1], smoother, loadings, tables)
-    nothing = jnp.zeros((1, factors), F32)
-    nothing, ready = lax.optimization_barrier((nothing, ready))
-    tail = advanced(pair, upper, nothing, pieces, True)
     ahead = prefixed(pair, upper, pieces, other, running, last, states)
 
     state = nothing
@@ -558,6 +557,7 @@
         pairs = [(g * group + j, (g + 1) * group + j) for j in range(group)]
         arrived = lax.ppermute(moved, "tm", pairs)
 
+    ahead, ready = lax.optimization_barrier((ahead, ready))
     own = filtered_of(state, arrived, *ahead)[None]
     gathered = lax.all_to_all(
         jnp.broadcast_to(own, (devices, day_count, factors)), "tm", 0, 0, tiled=True

time: 52.9 us -> 52.5 us (level)
  blocking collectives: 11.8 us -> 11.2 us
    all_to_all x1, blocking collectives: 11.8 us -> 11.2 us  [local(): lax.all_to_all(jnp.broadcast_to(own, (devices, day_count, factors)), 'tm'...]
  transfers between devices with their start and end apart: 9 -> 9, of which waited for: 5 -> 6; matrix products, arithmetic and copies ran while one was open for 0% -> 0% of each run, Pallas kernels for 25% -> 25%
where the time goes in v8:
time: 52.5 us; the launch traced here: 52.3 us
  Pallas kernels  19.9 us (38%)
  starting transfers between devices  13.9 us (26%)
  blocking collectives  11.2 us (21%)
  waiting for transfers between devices  6.34 us (12%)
  between operations  0.84 us (2%)
    all_to_all x1, blocking collectives, local(): lax.all_to_all(jnp.broadcast_to(own, (devices, day_count, factors)), 'tm'...  11.2 us
    pallas_call x1, Pallas kernels, damped_of(): pl.pallas_call(kernel, in_specs=[smem()] + vmem(1) + hbm(5), out_specs=pl...  10.6 us
    all_to_all x1, starting transfers between devices, local(): terms = lax.all_to_all(partial, 'tm', 0, 0, tiled=True)  7.4 us
    ppermute x8, starting transfers between devices, swapped(): lax.ppermute(array, 'tm', [(i, i ^ distance) for i in range(devices)])  6.53 us
    ppermute x8, waiting for transfers between devices, swapped(): lax.ppermute(array, 'tm', [(i, i ^ distance) for i in range(devices)])  6.34 us
    pallas_call x1, Pallas kernels, partial_drive(): pl.pallas_call(kernel, in_specs=[smem()] + hbm(6), out_specs=pl.BlockSpec...  2.15 us
    pallas_call x1, Pallas kernels, finish(): pl.pallas_call(kernel, in_specs=[smem()] + vmem(7), out_specs=vmem(2), ou...  2.07 us
    pallas_call x1, Pallas kernels, prepared(): pl.pallas_call(kernel, in_specs=[smem()] + vmem(1) + hbm(5), out_specs=vm...  1.57 us
  transfers between devices with their start and end apart: 9, of which 6 were waited for; matrix products, arithmetic and copies ran while one was open for 0% of the time, Pallas kernels for 25%

profile of v8, /device:TPU:0, one launch (start us, length us, event | category | flops | bytes accessed | tf_op | source)
XLA Modules:
  0.0 52.3 jit_solution(4397044356254738066)
XLA Ops:
  0.6 0.0 copy-start.4
  0.6 0.0 copy-start.3
  0.7 0.0 copy-start.2
  0.7 0.0 copy-start.1
  0.7 0.0 copy-start.6
  0.7 2.1 %partial_drive.1 = f32[16,4,256]{2,1,0:T(4,128)} custom-call(s32[1]{0:T(128)} %bitcast.index_ref, bf16[64,1024]{1,0:T(8,128)(2,1)} %series_ref.1, bf16[16384,256]{1,0:T(8,128)(2,1)} %load_hbm.5, f32[1,16384]{1,0:T(1,128)} %bitcast.8, s32[1,16384]{1,0:T(1,128)} %bitcast.11, s32[1,16384]{1,0:T(1,128)} %bitcast.14, s32[1,16384]{1,0:T(1,128)} %bitcast.17), custom_call_target="tpu_custom_call" | custom-call | flops 33554432 | bytes 1048576 | tf_op jit(solution)/shard_map/partial_drive/pallas_call | solution.py:106
  2.8 7.4 %all-to-all-start = ((f32[16,4,256]{2,1,0:T(4,128)}), f32[16,4,256]{2,1,0:T(4,128)S(1)}, u32[]{:S(2)}, u32[]{:S(2)}) async-start(f32[16,4,256]{2,1,0:T(4,128)} %partial_drive.1), calls=%async_computation | async-start | bytes 131072 | tf_op jit(solution)/shard_map/all_to_all | solution.py:535
  10.2 0.0 copy-done.4
  10.3 0.0 copy-done.3
  10.3 0.0 copy-done.2
  10.3 0.0 copy-done.1
  10.3 0.0 copy-done.6
  10.3 0.0 copy-start.7
  10.3 0.0 copy-start.5
  10.3 10.6 %damped.1.damped_ref = bf16[4,256,256]{2,1,0:T(8,128)(2,1)S(1)} custom-call(s32[1]{0:T(128)S(6)} %mul.3.day_ref, f32[1,256]{1,0:T(1,128)S(1)} %bitcast.20, bf16[16384,256]{1,0:T(8,128)(2,1)} %load_hbm.5, f32[1,16384]{1,0:T(1,128)S(1)} %bitcast.9, s32[1,16384]{1,0:T(1,128)S(1)} %bitcast.12, s32[1,16384]{1,0:T(1,128)S(1)} %bitcast.15, s32[1,16384]{1,0:T(1,128)S(1)} %bitcast.18), custom_call_target="tpu_custom_call" | custom-call | flops 8589934592 | bytes 10485760 | tf_op jit(solution)/shard_map/damped/pallas_call | solution.py:169
  21.0 0.0 copy-start
  21.0 0.0 all-to-all-done.terms_ref
  21.0 0.0 copy-done.7
  21.0 1.3 %block.1 = (f32[3,256,256]{2,1,0:T(8,128)S(1)}, f32[256,256]{1,0:T(8,128)S(1)}, f32[4,256]{1,0:T(4,128)S(1)}, f32[1,256]{1,0:T(1,128)S(1)}, bf16[272,256]{1,0:T(8,128)(2,1)S(1)}) custom-call(bf16[4,256,256]{2,1,0:T(8,128)(2,1)S(1)} %damped.1.damped_ref, f32[16,4,256]{2,1,0:T(4,128)S(1)} %all-to-all-done.terms_ref, f32[1,256]{1,0:T(1,128)S(1)} %bitcast.21, ...), custom_call_target="tpu_custom_call" | custom-call | flops 838860800 | bytes 3145728 | tf_op jit(solution)/shard_map/block/pallas_call | solution.py:264
  22.3 0.5 collective-permute-start
  22.8 1.0 %collective-permute-done.other_ref.refs_8_ = bf16[272,256]{1,0:T(8,128)(2,1)S(1)} collective-permute-done((bf16[272,256]{1,0:T(8,128)(2,1)S(1)}, bf16[272,256]{1,0:T(8,128)(2,1)S(1)}, u32[]{:S(2)}, u32[]{:S(2)}) %collective-permute-start) | collective-permute-done | bytes 139296 | tf_op jit(solution)/shard_map/ppermute | solution.py:531
  23.8 0.3 combined.1
  24.1 2.8 %collective-permute-start.5 = (bf16[144,256]{1,0:T(8,128)(2,1)S(1)}, bf16[144,256]{1,0:T(8,128)(2,1)S(1)}, u32[]{:S(2)}, u32[]{:S(2)}) collective-permute-start(bf16[144,256]{1,0:T(8,128)(2,1)S(1)} %get-tuple-element.32.refs_0_), channel_id=1, source_target_pairs={{0,6},{1,7},{2,4},{3,5},{4,2},{5,3},{6,0},{7,1},{8,14},{9,15},{10,... | collective-permute-start | bytes 221192 | tf_op jit(solution)/shard_map/ppermute | solution.py:531
  27.0 0.5 %collective-permute-start.3 = (bf16[144,256]{1,0:T(8,128)(2,1)S(1)}, bf16[144,256]{1,0:T(8,128)(2,1)S(1)}, u32[]{:S(2)}, u32[]{:S(2)}) collective-permute-start(bf16[144,256]{1,0:T(8,128)(2,1)S(1)} %get-tuple-element.32.refs_0_), channel_id=1, source_target_pairs={{0,4},{1,5},{2,6},{3,7},{4,0},{5,1},{6,2},{7,3},{8,12},{9,13},{10,... | collective-permute-start | bytes 221192 | tf_op jit(solution)/shard_map/ppermute | solution.py:531
  27.5 0.2 collective-permute-start.1
  27.7 2.3 %collective-permute-done.5.refs_6_ = bf16[144,256]{1,0:T(8,128)(2,1)S(1)} collective-permute-done((bf16[144,256]{1,0:T(8,128)(2,1)S(1)}, bf16[144,256]{1,0:T(8,128)(2,1)S(1)}, u32[]{:S(2)}, u32[]{:S(2)}) %collective-permute-start.5) | collective-permute-done | bytes 73760 | tf_op jit(solution)/shard_map/ppermute | solution.py:531
  29.9 0.0 collective-permute-start.6
  29.9 1.5 %collective-permute-done.3.refs_4_ = bf16[144,256]{1,0:T(8,128)(2,1)S(1)} collective-permute-done((bf16[144,256]{1,0:T(8,128)(2,1)S(1)}, bf16[144,256]{1,0:T(8,128)(2,1)S(1)}, u32[]{:S(2)}, u32[]{:S(2)}) %collective-permute-start.3) | collective-permute-done | bytes 73760 | tf_op jit(solution)/shard_map/ppermute | solution.py:531
  31.5 0.0 collective-permute-start.4
  31.5 0.4 collective-permute-done.1.refs_2_
  31.9 0.1 collective-permute-start.2
  32.0 0.0 collective-permute-done.6.refs_7_
  32.0 0.7 %collective-permute-done.4.refs_5_ = bf16[144,256]{1,0:T(8,128)(2,1)S(1)} collective-permute-done((bf16[144,256]{1,0:T(8,128)(2,1)S(1)}, bf16[144,256]{1,0:T(8,128)(2,1)S(1)}, u32[]{:S(2)}, u32[]{:S(2)}) %collective-permute-start.4) | collective-permute-done | bytes 73760 | tf_op jit(solution)/shard_map/ppermute | solution.py:531
  32.7 0.4 collective-permute-done.2.refs_3_
  33.1 0.5 advanced.1
  33.6 2.4 %collective-permute-start.7 = (f32[1,256]{1,0:T(1,128)S(1)}, f32[1,256]{1,0:T(1,128)S(1)}, u32[]{:S(2)}, u32[]{:S(2)}) collective-permute-start(f32[1,256]{1,0:T(1,128)S(1)} %advanced.1), channel_id=1, source_target_pairs={{0,8},{1,9},{2,10},{3,11},{4,12},{5,13},{6,14},{7,15},{8,0},{9,1},... | collective-permute-start | bytes 3080 | tf_op jit(solution)/shard_map/ppermute | solution.py:531
  36.0 1.1 %prefixed.1 = (bf16[256,1024]{1,0:T(8,128)(2,1)S(1)}, bf16[256,1024]{1,0:T(8,128)(2,1)S(1)}, f32[1,1024]{1,0:T(1,128)S(1)}) custom-call(s32[1]{0:T(128)} %bitcast.1.pair_ref, s32[1]{0:T(128)} %bitcast.2.upper_ref, bf16[144,256]{1,0:T(8,128)(2,1)S(1)} %get-tuple-element.32.refs_0_, bf16[144,256]{1,0:T(8,128)(2,1)S(1)} %get-tuple-element.33.refs_1_, ...), custom_call_target="tpu_custom_call" | custom-call | flops 603979776 | bytes 3145728 | tf_op jit(solution)/shard_map/prefixed/pallas_call | solution.py:374
  37.1 0.0 copy-done.5
  37.1 1.6 %prepared.1 = (bf16[5,256,256]{2,1,0:T(8,128)(2,1)S(1)}, bf16[5,256,256]{2,1,0:T(8,128)(2,1)S(1)}, bf16[1024,256]{1,0:T(8,128)(2,1)S(1)}, f32[64,1024]{1,0:T(8,128)S(1)}) custom-call(s32[1]{0:T(128)} %bitcast.index_ref, f32[256,256]{1,0:T(8,128)S(1)} %copy-done.5, bf16[16384,256]{1,0:T(8,128)(2,1)} %load_hbm.5, f32[1,16384]{1,0:T(1,128)S(1)} %bitcast.10, ...), custom_call_target="tpu_custom_call" | custom-call | flops 402653184 | bytes 3145728 | tf_op jit(solution)/shard_map/prepared/pallas_call | solution.py:445
  38.7 0.0 collective-permute-done.7
  38.7 0.2 filtered.1
  39.0 11.2 %all_to_all.10.gathered_ref = f32[16,4,256]{2,1,0:T(4,128)S(1)} all-to-all(f32[16,4,256]{2,1,0:T(4,128)S(1)} %broadcast_in_dim.24), channel_id=1, replica_groups=mesh['spec'=2,'tm'=16] {'tm'}, dimensions={0} | all-to-all | bytes 131072 | tf_op jit(solution)/shard_map/all_to_all | solution.py:562
  50.2 0.0 copy-done
  50.2 2.1 %finish.1 = (f32[4,256]{1,0:T(4,128)}, bf16[64,1024]{1,0:T(8,128)(2,1)}) custom-call(s32[1]{0:T(128)} %bitcast.index_ref, f32[16,4,256]{2,1,0:T(4,128)S(1)} %all_to_all.10.gathered_ref, bf16[5,256,256]{2,1,0:T(8,128)(2,1)S(1)} %get-tuple-element.48.high_ref, bf16[5,256,256]{2,1,0:T(8,128)(2,1)S(1)} %get-tuple-element.49.low_ref, ...), custom_call_target="tpu_custom_call" | custom-call | flops 33554432 | bytes 2097152 | tf_op jit(solution)/shard_map/finish/pallas_call | solution.py:505
  (3 shorter events, 0.0 us)
Async XLA Ops:
  0.6 9.6 %copy-start.4 = (s32[16384]{0:T(1024)S(1)}, s32[16384]{0:T(1024)}, u32[]{:S(2)}) copy-start(s32[16384]{0:T(1024)} %param.14) | copy-start | bytes 196612
  0.6 9.6 %copy-start.3 = (s32[16384]{0:T(1024)S(1)}, s32[16384]{0:T(1024)}, u32[]{:S(2)}) copy-start(s32[16384]{0:T(1024)} %param.13) | copy-start | bytes 196612
  0.7 9.6 %copy-start.2 = (s32[16384]{0:T(1024)S(1)}, s32[16384]{0:T(1024)}, u32[]{:S(2)}) copy-start(s32[16384]{0:T(1024)} %param.12) | copy-start | bytes 196612
  0.7 9.6 %copy-start.1 = (f32[16384]{0:T(1024)S(1)}, f32[16384]{0:T(1024)}, u32[]{:S(2)}) copy-start(f32[16384]{0:T(1024)} %param.11) | copy-start | bytes 196612
  0.7 9.6 %copy-start.6 = (f32[256]{0:T(256)S(1)}, f32[256]{0:T(256)}, u32[]{:S(2)}) copy-start(f32[256]{0:T(256)} %param.15) | copy-start | bytes 3076
  2.8 18.1 %all-to-all-start = ((f32[16,4,256]{2,1,0:T(4,128)}), f32[16,4,256]{2,1,0:T(4,128)S(1)}, u32[]{:S(2)}, u32[]{:S(2)}) async-start(f32[16,4,256]{2,1,0:T(4,128)} %partial_drive.1), calls=%async_computation | async-start | bytes 131072 | tf_op jit(solution)/shard_map/all_to_all | solution.py:535
  10.3 10.7 %copy-start.7 = (bf16[256,256]{1,0:T(8,128)(2,1)S(1)}, bf16[256,256]{1,0:T(8,128)(2,1)}, u32[]{:S(2)}) copy-start(bf16[256,256]{1,0:T(8,128)(2,1)} %gain_ref.1) | copy-start | bytes 393220
  10.3 26.8 %copy-start.5 = (f32[256,256]{1,0:T(8,128)S(1)}, f32[256,256]{1,0:T(8,128)}, u32[]{:S(2)}) copy-start(f32[256,256]{1,0:T(8,128)} %in_ref) | copy-start | bytes 786436
  21.0 29.2 %copy-start = (bf16[64,1024]{1,0:T(8,128)(2,1)S(1)}, bf16[64,1024]{1,0:T(8,128)(2,1)}, u32[]{:S(2)}) copy-start(bf16[64,1024]{1,0:T(8,128)(2,1)} %series_ref.1) | copy-start | bytes 393220
  22.3 1.5 %collective-permute-start = (bf16[272,256]{1,0:T(8,128)(2,1)S(1)}, bf16[272,256]{1,0:T(8,128)(2,1)S(1)}, u32[]{:S(2)}, u32[]{:S(2)}) collective-permute-start(bf16[272,256]{1,0:T(8,128)(2,1)S(1)} %get-tuple-element.31), channel_id=1, source_target_pairs={{0,1},{1,0},{2,3},{3,2},{4,5},{5,4},{6,7},{7,6},{8,9},{9,8},{10,11... | collective-permute-start | bytes 417800 | tf_op jit(solution)/shard_map/ppermute | solution.py:531
  24.1 5.8 %collective-permute-start.5 = (bf16[144,256]{1,0:T(8,128)(2,1)S(1)}, bf16[144,256]{1,0:T(8,128)(2,1)S(1)}, u32[]{:S(2)}, u32[]{:S(2)}) collective-permute-start(bf16[144,256]{1,0:T(8,128)(2,1)S(1)} %get-tuple-element.32.refs_0_), channel_id=1, source_target_pairs={{0,6},{1,7},{2,4},{3,5},{4,2},{5,3},{6,0},{7,1},{8,14},{9,15},{10,... | collective-permute-start | bytes 221192 | tf_op jit(solution)/shard_map/ppermute | solution.py:531
  27.0 4.5 %collective-permute-start.3 = (bf16[144,256]{1,0:T(8,128)(2,1)S(1)}, bf16[144,256]{1,0:T(8,128)(2,1)S(1)}, u32[]{:S(2)}, u32[]{:S(2)}) collective-permute-start(bf16[144,256]{1,0:T(8,128)(2,1)S(1)} %get-tuple-element.32.refs_0_), channel_id=1, source_target_pairs={{0,4},{1,5},{2,6},{3,7},{4,0},{5,1},{6,2},{7,3},{8,12},{9,13},{10,... | collective-permute-start | bytes 221192 | tf_op jit(solution)/shard_map/ppermute | solution.py:531
  27.5 4.4 %collective-permute-start.1 = (bf16[144,256]{1,0:T(8,128)(2,1)S(1)}, bf16[144,256]{1,0:T(8,128)(2,1)S(1)}, u32[]{:S(2)}, u32[]{:S(2)}) collective-permute-start(bf16[144,256]{1,0:T(8,128)(2,1)S(1)} %get-tuple-element.32.refs_0_), channel_id=1, source_target_pairs={{0,2},{1,3},{2,0},{3,1},{4,6},{5,7},{6,4},{7,5},{8,10},{9,11},{10,... | collective-permute-start | bytes 221192 | tf_op jit(solution)/shard_map/ppermute | solution.py:531
  29.9 2.0 %collective-permute-start.6 = (bf16[144,256]{1,0:T(8,128)(2,1)S(1)}, bf16[144,256]{1,0:T(8,128)(2,1)S(1)}, u32[]{:S(2)}, u32[]{:S(2)}) collective-permute-start(bf16[144,256]{1,0:T(8,128)(2,1)S(1)} %collective-permute-done.5.refs_6_), channel_id=1, source_target_pairs={{0,1},{1,0},{2,3},{3,2},{4,5},{5,4},{6,7},{7,6},{8,9},{9,8},{10,11... | collective-permute-start | bytes 221192 | tf_op jit(solution)/shard_map/ppermute | solution.py:531
  31.5 1.3 %collective-permute-start.4 = (bf16[144,256]{1,0:T(8,128)(2,1)S(1)}, bf16[144,256]{1,0:T(8,128)(2,1)S(1)}, u32[]{:S(2)}, u32[]{:S(2)}) collective-permute-start(bf16[144,256]{1,0:T(8,128)(2,1)S(1)} %collective-permute-done.3.refs_4_), channel_id=1, source_target_pairs={{0,1},{1,0},{2,3},{3,2},{4,5},{5,4},{6,7},{7,6},{8,9},{9,8},{10,11... | collective-permute-start | bytes 221192 | tf_op jit(solution)/shard_map/ppermute | solution.py:531
  31.9 1.3 %collective-permute-start.2 = (bf16[144,256]{1,0:T(8,128)(2,1)S(1)}, bf16[144,256]{1,0:T(8,128)(2,1)S(1)}, u32[]{:S(2)}, u32[]{:S(2)}) collective-permute-start(bf16[144,256]{1,0:T(8,128)(2,1)S(1)} %collective-permute-done.1.refs_2_), channel_id=1, source_target_pairs={{0,1},{1,0},{2,3},{3,2},{4,5},{5,4},{6,7},{7,6},{8,9},{9,8},{10,11... | collective-permute-start | bytes 221192 | tf_op jit(solution)/shard_map/ppermute | solution.py:531
  33.6 5.1 %collective-permute-start.7 = (f32[1,256]{1,0:T(1,128)S(1)}, f32[1,256]{1,0:T(1,128)S(1)}, u32[]{:S(2)}, u32[]{:S(2)}) collective-permute-start(f32[1,256]{1,0:T(1,128)S(1)} %advanced.1), channel_id=1, source_target_pairs={{0,8},{1,9},{2,10},{3,11},{4,12},{5,13},{6,14},{7,15},{8,0},{9,1},... | collective-permute-start | bytes 3080 | tf_op jit(solution)/shard_map/ppermute | solution.py:531

commit v9 on v8

--- a/solution.py
+++ b/solution.py
@@ -126,7 +126,7 @@
 def damped_of(first_day, day_count, loadings, tables, decay):
     providers, factors = loadings.shape
     unit = providers // 16
-    sizes = [unit, unit, 2 * unit, 4 * unit, 8 * unit]
+    sizes = [unit, unit, 2 * unit, 6 * unit, 6 * unit]
     parts = [slice(sum(sizes[:n]), sum(sizes[: n + 1])) for n in range(len(sizes))]
 
     def kernel(

time: 52.5 us -> 52.5 us (level)
  no operation moved by 1% of the time
where the time goes in v9:
time: 52.5 us; the launch traced here: 52.3 us
  Pallas kernels  19.9 us (38%)
  starting transfers between devices  13.9 us (26%)
  blocking collectives  11.2 us (21%)
  waiting for transfers between devices  6.34 us (12%)
  between operations  0.84 us (2%)
    all_to_all x1, blocking collectives, local(): lax.all_to_all(jnp.broadcast_to(own, (devices, day_count, factors)), 'tm'...  11.2 us
    pallas_call x1, Pallas kernels, damped_of(): pl.pallas_call(kernel, in_specs=[smem()] + vmem(1) + hbm(5), out_specs=pl...  10.6 us
    all_to_all x1, starting transfers between devices, local(): terms = lax.all_to_all(partial, 'tm', 0, 0, tiled=True)  7.4 us
    ppermute x8, starting transfers between devices, swapped(): lax.ppermute(array, 'tm', [(i, i ^ distance) for i in range(devices)])  6.53 us
    ppermute x8, waiting for transfers between devices, swapped(): lax.ppermute(array, 'tm', [(i, i ^ distance) for i in range(devices)])  6.34 us
    pallas_call x1, Pallas kernels, partial_drive(): pl.pallas_call(kernel, in_specs=[smem()] + hbm(6), out_specs=pl.BlockSpec...  2.15 us
    pallas_call x1, Pallas kernels, finish(): pl.pallas_call(kernel, in_specs=[smem()] + vmem(7), out_specs=vmem(2), ou...  2.07 us
    pallas_call x1, Pallas kernels, prepared(): pl.pallas_call(kernel, in_specs=[smem()] + vmem(1) + hbm(5), out_specs=vm...  1.57 us
  transfers between devices with their start and end apart: 9, of which 6 were waited for; matrix products, arithmetic and copies ran while one was open for 0% of the time, Pallas kernels for 25%

profile of v9, /device:TPU:0, one launch (start us, length us, event | category | flops | bytes accessed | tf_op | source)
XLA Modules:
  0.0 52.3 jit_solution(9351921116453667899)
XLA Ops:
  0.6 0.0 copy-start.4
  0.6 0.0 copy-start.3
  0.7 0.0 copy-start.2
  0.7 0.0 copy-start.1
  0.7 0.0 copy-start.6
  0.7 2.1 %partial_drive.1 = f32[16,4,256]{2,1,0:T(4,128)} custom-call(s32[1]{0:T(128)} %bitcast.index_ref, bf16[64,1024]{1,0:T(8,128)(2,1)} %series_ref.1, bf16[16384,256]{1,0:T(8,128)(2,1)} %load_hbm.5, f32[1,16384]{1,0:T(1,128)} %bitcast.8, s32[1,16384]{1,0:T(1,128)} %bitcast.11, s32[1,16384]{1,0:T(1,128)} %bitcast.14, s32[1,16384]{1,0:T(1,128)} %bitcast.17), custom_call_target="tpu_custom_call" | custom-call | flops 33554432 | bytes 1048576 | tf_op jit(solution)/shard_map/partial_drive/pallas_call | solution.py:106
  2.8 7.4 %all-to-all-start = ((f32[16,4,256]{2,1,0:T(4,128)}), f32[16,4,256]{2,1,0:T(4,128)S(1)}, u32[]{:S(2)}, u32[]{:S(2)}) async-start(f32[16,4,256]{2,1,0:T(4,128)} %partial_drive.1), calls=%async_computation | async-start | bytes 131072 | tf_op jit(solution)/shard_map/all_to_all | solution.py:535
  10.2 0.0 copy-done.4
  10.3 0.0 copy-done.3
  10.3 0.0 copy-done.2
  10.3 0.0 copy-done.1
  10.3 0.0 copy-done.6
  10.3 0.0 copy-start.7
  10.3 0.0 copy-start.5
  10.3 10.6 %damped.1.damped_ref = bf16[4,256,256]{2,1,0:T(8,128)(2,1)S(1)} custom-call(s32[1]{0:T(128)S(6)} %mul.3.day_ref, f32[1,256]{1,0:T(1,128)S(1)} %bitcast.20, bf16[16384,256]{1,0:T(8,128)(2,1)} %load_hbm.5, f32[1,16384]{1,0:T(1,128)S(1)} %bitcast.9, s32[1,16384]{1,0:T(1,128)S(1)} %bitcast.12, s32[1,16384]{1,0:T(1,128)S(1)} %bitcast.15, s32[1,16384]{1,0:T(1,128)S(1)} %bitcast.18), custom_call_target="tpu_custom_call" | custom-call | flops 8589934592 | bytes 10485760 | tf_op jit(solution)/shard_map/damped/pallas_call | solution.py:169
  21.0 0.0 copy-start
  21.0 0.0 all-to-all-done.terms_ref
  21.0 0.0 copy-done.7
  21.0 1.4 %block.1 = (f32[3,256,256]{2,1,0:T(8,128)S(1)}, f32[256,256]{1,0:T(8,128)S(1)}, f32[4,256]{1,0:T(4,128)S(1)}, f32[1,256]{1,0:T(1,128)S(1)}, bf16[272,256]{1,0:T(8,128)(2,1)S(1)}) custom-call(bf16[4,256,256]{2,1,0:T(8,128)(2,1)S(1)} %damped.1.damped_ref, f32[16,4,256]{2,1,0:T(4,128)S(1)} %all-to-all-done.terms_ref, f32[1,256]{1,0:T(1,128)S(1)} %bitcast.21, ...), custom_call_target="tpu_custom_call" | custom-call | flops 838860800 | bytes 3145728 | tf_op jit(solution)/shard_map/block/pallas_call | solution.py:264
  22.4 0.5 collective-permute-start
  22.8 1.0 %collective-permute-done.other_ref.refs_8_ = bf16[272,256]{1,0:T(8,128)(2,1)S(1)} collective-permute-done((bf16[272,256]{1,0:T(8,128)(2,1)S(1)}, bf16[272,256]{1,0:T(8,128)(2,1)S(1)}, u32[]{:S(2)}, u32[]{:S(2)}) %collective-permute-start) | collective-permute-done | bytes 139296 | tf_op jit(solution)/shard_map/ppermute | solution.py:531
  23.8 0.3 combined.1
  24.1 2.8 %collective-permute-start.5 = (bf16[144,256]{1,0:T(8,128)(2,1)S(1)}, bf16[144,256]{1,0:T(8,128)(2,1)S(1)}, u32[]{:S(2)}, u32[]{:S(2)}) collective-permute-start(bf16[144,256]{1,0:T(8,128)(2,1)S(1)} %get-tuple-element.32.refs_0_), channel_id=1, source_target_pairs={{0,6},{1,7},{2,4},{3,5},{4,2},{5,3},{6,0},{7,1},{8,14},{9,15},{10,... | collective-permute-start | bytes 221192 | tf_op jit(solution)/shard_map/ppermute | solution.py:531
  27.0 0.5 %collective-permute-start.3 = (bf16[144,256]{1,0:T(8,128)(2,1)S(1)}, bf16[144,256]{1,0:T(8,128)(2,1)S(1)}, u32[]{:S(2)}, u32[]{:S(2)}) collective-permute-start(bf16[144,256]{1,0:T(8,128)(2,1)S(1)} %get-tuple-element.32.refs_0_), channel_id=1, source_target_pairs={{0,4},{1,5},{2,6},{3,7},{4,0},{5,1},{6,2},{7,3},{8,12},{9,13},{10,... | collective-permute-start | bytes 221192 | tf_op jit(solution)/shard_map/ppermute | solution.py:531
  27.5 0.2 collective-permute-start.1
  27.7 2.2 %collective-permute-done.5.refs_6_ = bf16[144,256]{1,0:T(8,128)(2,1)S(1)} collective-permute-done((bf16[144,256]{1,0:T(8,128)(2,1)S(1)}, bf16[144,256]{1,0:T(8,128)(2,1)S(1)}, u32[]{:S(2)}, u32[]{:S(2)}) %collective-permute-start.5) | collective-permute-done | bytes 73760 | tf_op jit(solution)/shard_map/ppermute | solution.py:531
  29.9 0.0 collective-permute-start.6
  29.9 1.5 %collective-permute-done.3.refs_4_ = bf16[144,256]{1,0:T(8,128)(2,1)S(1)} collective-permute-done((bf16[144,256]{1,0:T(8,128)(2,1)S(1)}, bf16[144,256]{1,0:T(8,128)(2,1)S(1)}, u32[]{:S(2)}, u32[]{:S(2)}) %collective-permute-start.3) | collective-permute-done | bytes 73760 | tf_op jit(solution)/shard_map/ppermute | solution.py:531
  31.5 0.0 collective-permute-start.4
  31.5 0.4 collective-permute-done.1.refs_2_
  31.9 0.1 collective-permute-start.2
  32.0 0.0 collective-permute-done.6.refs_7_
  32.0 0.7 %collective-permute-done.4.refs_5_ = bf16[144,256]{1,0:T(8,128)(2,1)S(1)} collective-permute-done((bf16[144,256]{1,0:T(8,128)(2,1)S(1)}, bf16[144,256]{1,0:T(8,128)(2,1)S(1)}, u32[]{:S(2)}, u32[]{:S(2)}) %collective-permute-start.4) | collective-permute-done | bytes 73760 | tf_op jit(solution)/shard_map/ppermute | solution.py:531
  32.7 0.4 collective-permute-done.2.refs_3_
  33.1 0.5 advanced.1
  33.6 2.4 %collective-permute-start.7 = (f32[1,256]{1,0:T(1,128)S(1)}, f32[1,256]{1,0:T(1,128)S(1)}, u32[]{:S(2)}, u32[]{:S(2)}) collective-permute-start(f32[1,256]{1,0:T(1,128)S(1)} %advanced.1), channel_id=1, source_target_pairs={{0,8},{1,9},{2,10},{3,11},{4,12},{5,13},{6,14},{7,15},{8,0},{9,1},... | collective-permute-start | bytes 3080 | tf_op jit(solution)/shard_map/ppermute | solution.py:531
  36.0 1.1 %prefixed.1 = (bf16[256,1024]{1,0:T(8,128)(2,1)S(1)}, bf16[256,1024]{1,0:T(8,128)(2,1)S(1)}, f32[1,1024]{1,0:T(1,128)S(1)}) custom-call(s32[1]{0:T(128)} %bitcast.1.pair_ref, s32[1]{0:T(128)} %bitcast.2.upper_ref, bf16[144,256]{1,0:T(8,128)(2,1)S(1)} %get-tuple-element.32.refs_0_, bf16[144,256]{1,0:T(8,128)(2,1)S(1)} %get-tuple-element.33.refs_1_, ...), custom_call_target="tpu_custom_call" | custom-call | flops 603979776 | bytes 3145728 | tf_op jit(solution)/shard_map/prefixed/pallas_call | solution.py:374
  37.1 0.0 copy-done.5
  37.1 1.6 %prepared.1 = (bf16[5,256,256]{2,1,0:T(8,128)(2,1)S(1)}, bf16[5,256,256]{2,1,0:T(8,128)(2,1)S(1)}, bf16[1024,256]{1,0:T(8,128)(2,1)S(1)}, f32[64,1024]{1,0:T(8,128)S(1)}) custom-call(s32[1]{0:T(128)} %bitcast.index_ref, f32[256,256]{1,0:T(8,128)S(1)} %copy-done.5, bf16[16384,256]{1,0:T(8,128)(2,1)} %load_hbm.5, f32[1,16384]{1,0:T(1,128)S(1)} %bitcast.10, ...), custom_call_target="tpu_custom_call" | custom-call | flops 402653184 | bytes 3145728 | tf_op jit(solution)/shard_map/prepared/pallas_call | solution.py:445
  38.7 0.0 collective-permute-done.7
  38.7 0.2 filtered.1
  39.0 11.2 %all_to_all.10.gathered_ref = f32[16,4,256]{2,1,0:T(4,128)S(1)} all-to-all(f32[16,4,256]{2,1,0:T(4,128)S(1)} %broadcast_in_dim.24), channel_id=1, replica_groups=mesh['spec'=2,'tm'=16] {'tm'}, dimensions={0} | all-to-all | bytes 131072 | tf_op jit(solution)/shard_map/all_to_all | solution.py:562
  50.2 0.0 copy-done
  50.2 2.1 %finish.1 = (f32[4,256]{1,0:T(4,128)}, bf16[64,1024]{1,0:T(8,128)(2,1)}) custom-call(s32[1]{0:T(128)} %bitcast.index_ref, f32[16,4,256]{2,1,0:T(4,128)S(1)} %all_to_all.10.gathered_ref, bf16[5,256,256]{2,1,0:T(8,128)(2,1)S(1)} %get-tuple-element.48.high_ref, bf16[5,256,256]{2,1,0:T(8,128)(2,1)S(1)} %get-tuple-element.49.low_ref, ...), custom_call_target="tpu_custom_call" | custom-call | flops 33554432 | bytes 2097152 | tf_op jit(solution)/shard_map/finish/pallas_call | solution.py:505
  (3 shorter events, 0.0 us)
Async XLA Ops:
  0.6 9.6 %copy-start.4 = (s32[16384]{0:T(1024)S(1)}, s32[16384]{0:T(1024)}, u32[]{:S(2)}) copy-start(s32[16384]{0:T(1024)} %param.14) | copy-start | bytes 196612
  0.6 9.6 %copy-start.3 = (s32[16384]{0:T(1024)S(1)}, s32[16384]{0:T(1024)}, u32[]{:S(2)}) copy-start(s32[16384]{0:T(1024)} %param.13) | copy-start | bytes 196612
  0.7 9.6 %copy-start.2 = (s32[16384]{0:T(1024)S(1)}, s32[16384]{0:T(1024)}, u32[]{:S(2)}) copy-start(s32[16384]{0:T(1024)} %param.12) | copy-start | bytes 196612
  0.7 9.6 %copy-start.1 = (f32[16384]{0:T(1024)S(1)}, f32[16384]{0:T(1024)}, u32[]{:S(2)}) copy-start(f32[16384]{0:T(1024)} %param.11) | copy-start | bytes 196612
  0.7 9.6 %copy-start.6 = (f32[256]{0:T(256)S(1)}, f32[256]{0:T(256)}, u32[]{:S(2)}) copy-start(f32[256]{0:T(256)} %param.15) | copy-start | bytes 3076
  2.8 18.1 %all-to-all-start = ((f32[16,4,256]{2,1,0:T(4,128)}), f32[16,4,256]{2,1,0:T(4,128)S(1)}, u32[]{:S(2)}, u32[]{:S(2)}) async-start(f32[16,4,256]{2,1,0:T(4,128)} %partial_drive.1), calls=%async_computation | async-start | bytes 131072 | tf_op jit(solution)/shard_map/all_to_all | solution.py:535
  10.3 10.7 %copy-start.7 = (bf16[256,256]{1,0:T(8,128)(2,1)S(1)}, bf16[256,256]{1,0:T(8,128)(2,1)}, u32[]{:S(2)}) copy-start(bf16[256,256]{1,0:T(8,128)(2,1)} %gain_ref.1) | copy-start | bytes 393220
  10.3 26.8 %copy-start.5 = (f32[256,256]{1,0:T(8,128)S(1)}, f32[256,256]{1,0:T(8,128)}, u32[]{:S(2)}) copy-start(f32[256,256]{1,0:T(8,128)} %in_ref) | copy-start | bytes 786436
  21.0 29.2 %copy-start = (bf16[64,1024]{1,0:T(8,128)(2,1)S(1)}, bf16[64,1024]{1,0:T(8,128)(2,1)}, u32[]{:S(2)}) copy-start(bf16[64,1024]{1,0:T(8,128)(2,1)} %series_ref.1) | copy-start | bytes 393220
  22.4 1.5 %collective-permute-start = (bf16[272,256]{1,0:T(8,128)(2,1)S(1)}, bf16[272,256]{1,0:T(8,128)(2,1)S(1)}, u32[]{:S(2)}, u32[]{:S(2)}) collective-permute-start(bf16[272,256]{1,0:T(8,128)(2,1)S(1)} %get-tuple-element.31), channel_id=1, source_target_pairs={{0,1},{1,0},{2,3},{3,2},{4,5},{5,4},{6,7},{7,6},{8,9},{9,8},{10,11... | collective-permute-start | bytes 417800 | tf_op jit(solution)/shard_map/ppermute | solution.py:531
  24.1 5.8 %collective-permute-start.5 = (bf16[144,256]{1,0:T(8,128)(2,1)S(1)}, bf16[144,256]{1,0:T(8,128)(2,1)S(1)}, u32[]{:S(2)}, u32[]{:S(2)}) collective-permute-start(bf16[144,256]{1,0:T(8,128)(2,1)S(1)} %get-tuple-element.32.refs_0_), channel_id=1, source_target_pairs={{0,6},{1,7},{2,4},{3,5},{4,2},{5,3},{6,0},{7,1},{8,14},{9,15},{10,... | collective-permute-start | bytes 221192 | tf_op jit(solution)/shard_map/ppermute | solution.py:531
  27.0 4.5 %collective-permute-start.3 = (bf16[144,256]{1,0:T(8,128)(2,1)S(1)}, bf16[144,256]{1,0:T(8,128)(2,1)S(1)}, u32[]{:S(2)}, u32[]{:S(2)}) collective-permute-start(bf16[144,256]{1,0:T(8,128)(2,1)S(1)} %get-tuple-element.32.refs_0_), channel_id=1, source_target_pairs={{0,4},{1,5},{2,6},{3,7},{4,0},{5,1},{6,2},{7,3},{8,12},{9,13},{10,... | collective-permute-start | bytes 221192 | tf_op jit(solution)/shard_map/ppermute | solution.py:531
  27.5 4.4 %collective-permute-start.1 = (bf16[144,256]{1,0:T(8,128)(2,1)S(1)}, bf16[144,256]{1,0:T(8,128)(2,1)S(1)}, u32[]{:S(2)}, u32[]{:S(2)}) collective-permute-start(bf16[144,256]{1,0:T(8,128)(2,1)S(1)} %get-tuple-element.32.refs_0_), channel_id=1, source_target_pairs={{0,2},{1,3},{2,0},{3,1},{4,6},{5,7},{6,4},{7,5},{8,10},{9,11},{10,... | collective-permute-start | bytes 221192 | tf_op jit(solution)/shard_map/ppermute | solution.py:531
  29.9 2.1 %collective-permute-start.6 = (bf16[144,256]{1,0:T(8,128)(2,1)S(1)}, bf16[144,256]{1,0:T(8,128)(2,1)S(1)}, u32[]{:S(2)}, u32[]{:S(2)}) collective-permute-start(bf16[144,256]{1,0:T(8,128)(2,1)S(1)} %collective-permute-done.5.refs_6_), channel_id=1, source_target_pairs={{0,1},{1,0},{2,3},{3,2},{4,5},{5,4},{6,7},{7,6},{8,9},{9,8},{10,11... | collective-permute-start | bytes 221192 | tf_op jit(solution)/shard_map/ppermute | solution.py:531
  31.5 1.3 %collective-permute-start.4 = (bf16[144,256]{1,0:T(8,128)(2,1)S(1)}, bf16[144,256]{1,0:T(8,128)(2,1)S(1)}, u32[]{:S(2)}, u32[]{:S(2)}) collective-permute-start(bf16[144,256]{1,0:T(8,128)(2,1)S(1)} %collective-permute-done.3.refs_4_), channel_id=1, source_target_pairs={{0,1},{1,0},{2,3},{3,2},{4,5},{5,4},{6,7},{7,6},{8,9},{9,8},{10,11... | collective-permute-start | bytes 221192 | tf_op jit(solution)/shard_map/ppermute | solution.py:531
  31.9 1.3 %collective-permute-start.2 = (bf16[144,256]{1,0:T(8,128)(2,1)S(1)}, bf16[144,256]{1,0:T(8,128)(2,1)S(1)}, u32[]{:S(2)}, u32[]{:S(2)}) collective-permute-start(bf16[144,256]{1,0:T(8,128)(2,1)S(1)} %collective-permute-done.1.refs_2_), channel_id=1, source_target_pairs={{0,1},{1,0},{2,3},{3,2},{4,5},{5,4},{6,7},{7,6},{8,9},{9,8},{10,11... | collective-permute-start | bytes 221192 | tf_op jit(solution)/shard_map/ppermute | solution.py:531
  33.6 5.1 %collective-permute-start.7 = (f32[1,256]{1,0:T(1,128)S(1)}, f32[1,256]{1,0:T(1,128)S(1)}, u32[]{:S(2)}, u32[]{:S(2)}) collective-permute-start(f32[1,256]{1,0:T(1,128)S(1)} %advanced.1), channel_id=1, source_target_pairs={{0,8},{1,9},{2,10},{3,11},{4,12},{5,13},{6,14},{7,15},{8,0},{9,1},... | collective-permute-start | bytes 3080 | tf_op jit(solution)/shard_map/ppermute | solution.py:531

commit v10 on v9

--- a/solution.py
+++ b/solution.py
@@ -126,7 +126,7 @@
 def damped_of(first_day, day_count, loadings, tables, decay):
     providers, factors = loadings.shape
     unit = providers // 16
-    sizes = [unit, unit, 2 * unit, 6 * unit, 6 * unit]
+    sizes = [unit, 3 * unit, 6 * unit, 6 * unit]
     parts = [slice(sum(sizes[:n]), sum(sizes[: n + 1])) for n in range(len(sizes))]
 
     def kernel(

time: 52.5 us -> 52.4 us (level)
  no operation moved by 1% of the time
where the time goes in v10:
time: 52.4 us; the launch traced here: 52.2 us
  Pallas kernels  19.8 us (38%)
  starting transfers between devices  13.9 us (27%)
  blocking collectives  11.2 us (21%)
  waiting for transfers between devices  6.34 us (12%)
  between operations  0.84 us (2%)
    all_to_all x1, blocking collectives, local(): lax.all_to_all(jnp.broadcast_to(own, (devices, day_count, factors)), 'tm'...  11.2 us
    pallas_call x1, Pallas kernels, damped_of(): pl.pallas_call(kernel, in_specs=[smem()] + vmem(1) + hbm(5), out_specs=pl...  10.5 us
    all_to_all x1, starting transfers between devices, local(): terms = lax.all_to_all(partial, 'tm', 0, 0, tiled=True)  7.4 us
    ppermute x8, starting transfers between devices, swapped(): lax.ppermute(array, 'tm', [(i, i ^ distance) for i in range(devices)])  6.53 us
    ppermute x8, waiting for transfers between devices, swapped(): lax.ppermute(array, 'tm', [(i, i ^ distance) for i in range(devices)])  6.34 us
    pallas_call x1, Pallas kernels, partial_drive(): pl.pallas_call(kernel, in_specs=[smem()] + hbm(6), out_specs=pl.BlockSpec...  2.15 us
    pallas_call x1, Pallas kernels, finish(): pl.pallas_call(kernel, in_specs=[smem()] + vmem(7), out_specs=vmem(2), ou...  2.07 us
    pallas_call x1, Pallas kernels, prepared(): pl.pallas_call(kernel, in_specs=[smem()] + vmem(1) + hbm(5), out_specs=vm...  1.57 us
  transfers between devices with their start and end apart: 9, of which 6 were waited for; matrix products, arithmetic and copies ran while one was open for 0% of the time, Pallas kernels for 25%

profile of v10, /device:TPU:0, one launch (start us, length us, event | category | flops | bytes accessed | tf_op | source)
XLA Modules:
  0.0 52.2 jit_solution(8764377574071579421)
XLA Ops:
  0.6 0.0 copy-start.4
  0.6 0.0 copy-start.3
  0.7 0.0 copy-start.2
  0.7 0.0 copy-start.1
  0.7 0.0 copy-start.6
  0.7 2.1 %partial_drive.1 = f32[16,4,256]{2,1,0:T(4,128)} custom-call(s32[1]{0:T(128)} %bitcast.index_ref, bf16[64,1024]{1,0:T(8,128)(2,1)} %series_ref.1, bf16[16384,256]{1,0:T(8,128)(2,1)} %load_hbm.5, f32[1,16384]{1,0:T(1,128)} %bitcast.8, s32[1,16384]{1,0:T(1,128)} %bitcast.11, s32[1,16384]{1,0:T(1,128)} %bitcast.14, s32[1,16384]{1,0:T(1,128)} %bitcast.17), custom_call_target="tpu_custom_call" | custom-call | flops 33554432 | bytes 1048576 | tf_op jit(solution)/shard_map/partial_drive/pallas_call | solution.py:106
  2.8 7.4 %all-to-all-start = ((f32[16,4,256]{2,1,0:T(4,128)}), f32[16,4,256]{2,1,0:T(4,128)S(1)}, u32[]{:S(2)}, u32[]{:S(2)}) async-start(f32[16,4,256]{2,1,0:T(4,128)} %partial_drive.1), calls=%async_computation | async-start | bytes 131072 | tf_op jit(solution)/shard_map/all_to_all | solution.py:535
  10.2 0.0 copy-done.4
  10.3 0.0 copy-done.3
  10.3 0.0 copy-done.2
  10.3 0.0 copy-done.1
  10.3 0.0 copy-done.6
  10.3 0.0 copy-start.7
  10.3 0.0 copy-start.5
  10.3 10.5 %damped.1.damped_ref = bf16[4,256,256]{2,1,0:T(8,128)(2,1)S(1)} custom-call(s32[1]{0:T(128)S(6)} %mul.3.day_ref, f32[1,256]{1,0:T(1,128)S(1)} %bitcast.20, bf16[16384,256]{1,0:T(8,128)(2,1)} %load_hbm.5, f32[1,16384]{1,0:T(1,128)S(1)} %bitcast.9, s32[1,16384]{1,0:T(1,128)S(1)} %bitcast.12, s32[1,16384]{1,0:T(1,128)S(1)} %bitcast.15, s32[1,16384]{1,0:T(1,128)S(1)} %bitcast.18), custom_call_target="tpu_custom_call" | custom-call | flops 8589934592 | bytes 10485760 | tf_op jit(solution)/shard_map/damped/pallas_call | solution.py:169
  20.9 0.0 copy-start
  20.9 0.0 all-to-all-done.terms_ref
  20.9 0.0 copy-done.7
  20.9 1.3 %block.1 = (f32[3,256,256]{2,1,0:T(8,128)S(1)}, f32[256,256]{1,0:T(8,128)S(1)}, f32[4,256]{1,0:T(4,128)S(1)}, f32[1,256]{1,0:T(1,128)S(1)}, bf16[272,256]{1,0:T(8,128)(2,1)S(1)}) custom-call(bf16[4,256,256]{2,1,0:T(8,128)(2,1)S(1)} %damped.1.damped_ref, f32[16,4,256]{2,1,0:T(4,128)S(1)} %all-to-all-done.terms_ref, f32[1,256]{1,0:T(1,128)S(1)} %bitcast.21, ...), custom_call_target="tpu_custom_call" | custom-call | flops 838860800 | bytes 3145728 | tf_op jit(solution)/shard_map/block/pallas_call | solution.py:264
  22.3 0.5 collective-permute-start
  22.7 1.0 %collective-permute-done.other_ref.refs_8_ = bf16[272,256]{1,0:T(8,128)(2,1)S(1)} collective-permute-done((bf16[272,256]{1,0:T(8,128)(2,1)S(1)}, bf16[272,256]{1,0:T(8,128)(2,1)S(1)}, u32[]{:S(2)}, u32[]{:S(2)}) %collective-permute-start) | collective-permute-done | bytes 139296 | tf_op jit(solution)/shard_map/ppermute | solution.py:531
  23.7 0.3 combined.1
  24.0 2.8 %collective-permute-start.5 = (bf16[144,256]{1,0:T(8,128)(2,1)S(1)}, bf16[144,256]{1,0:T(8,128)(2,1)S(1)}, u32[]{:S(2)}, u32[]{:S(2)}) collective-permute-start(bf16[144,256]{1,0:T(8,128)(2,1)S(1)} %get-tuple-element.32.refs_0_), channel_id=1, source_target_pairs={{0,6},{1,7},{2,4},{3,5},{4,2},{5,3},{6,0},{7,1},{8,14},{9,15},{10,... | collective-permute-start | bytes 221192 | tf_op jit(solution)/shard_map/ppermute | solution.py:531
  26.9 0.6 %collective-permute-start.3 = (bf16[144,256]{1,0:T(8,128)(2,1)S(1)}, bf16[144,256]{1,0:T(8,128)(2,1)S(1)}, u32[]{:S(2)}, u32[]{:S(2)}) collective-permute-start(bf16[144,256]{1,0:T(8,128)(2,1)S(1)} %get-tuple-element.32.refs_0_), channel_id=1, source_target_pairs={{0,4},{1,5},{2,6},{3,7},{4,0},{5,1},{6,2},{7,3},{8,12},{9,13},{10,... | collective-permute-start | bytes 221192 | tf_op jit(solution)/shard_map/ppermute | solution.py:531
  27.4 0.2 collective-permute-start.1
  27.6 2.3 %collective-permute-done.5.refs_6_ = bf16[144,256]{1,0:T(8,128)(2,1)S(1)} collective-permute-done((bf16[144,256]{1,0:T(8,128)(2,1)S(1)}, bf16[144,256]{1,0:T(8,128)(2,1)S(1)}, u32[]{:S(2)}, u32[]{:S(2)}) %collective-permute-start.5) | collective-permute-done | bytes 73760 | tf_op jit(solution)/shard_map/ppermute | solution.py:531
  29.8 0.0 collective-permute-start.6
  29.8 1.5 %collective-permute-done.3.refs_4_ = bf16[144,256]{1,0:T(8,128)(2,1)S(1)} collective-permute-done((bf16[144,256]{1,0:T(8,128)(2,1)S(1)}, bf16[144,256]{1,0:T(8,128)(2,1)S(1)}, u32[]{:S(2)}, u32[]{:S(2)}) %collective-permute-start.3) | collective-permute-done | bytes 73760 | tf_op jit(solution)/shard_map/ppermute | solution.py:531
  31.4 0.0 collective-permute-start.4
  31.4 0.4 collective-permute-done.1.refs_2_
  31.8 0.1 collective-permute-start.2
  31.9 0.0 collective-permute-done.6.refs_7_
  31.9 0.7 %collective-permute-done.4.refs_5_ = bf16[144,256]{1,0:T(8,128)(2,1)S(1)} collective-permute-done((bf16[144,256]{1,0:T(8,128)(2,1)S(1)}, bf16[144,256]{1,0:T(8,128)(2,1)S(1)}, u32[]{:S(2)}, u32[]{:S(2)}) %collective-permute-start.4) | collective-permute-done | bytes 73760 | tf_op jit(solution)/shard_map/ppermute | solution.py:531
  32.6 0.4 collective-permute-done.2.refs_3_
  33.0 0.5 advanced.1
  33.5 2.4 %collective-permute-start.7 = (f32[1,256]{1,0:T(1,128)S(1)}, f32[1,256]{1,0:T(1,128)S(1)}, u32[]{:S(2)}, u32[]{:S(2)}) collective-permute-start(f32[1,256]{1,0:T(1,128)S(1)} %advanced.1), channel_id=1, source_target_pairs={{0,8},{1,9},{2,10},{3,11},{4,12},{5,13},{6,14},{7,15},{8,0},{9,1},... | collective-permute-start | bytes 3080 | tf_op jit(solution)/shard_map/ppermute | solution.py:531
  35.9 1.1 %prefixed.1 = (bf16[256,1024]{1,0:T(8,128)(2,1)S(1)}, bf16[256,1024]{1,0:T(8,128)(2,1)S(1)}, f32[1,1024]{1,0:T(1,128)S(1)}) custom-call(s32[1]{0:T(128)} %bitcast.1.pair_ref, s32[1]{0:T(128)} %bitcast.2.upper_ref, bf16[144,256]{1,0:T(8,128)(2,1)S(1)} %get-tuple-element.32.refs_0_, bf16[144,256]{1,0:T(8,128)(2,1)S(1)} %get-tuple-element.33.refs_1_, ...), custom_call_target="tpu_custom_call" | custom-call | flops 603979776 | bytes 3145728 | tf_op jit(solution)/shard_map/prefixed/pallas_call | solution.py:374
  37.0 0.0 copy-done.5
  37.0 1.6 %prepared.1 = (bf16[5,256,256]{2,1,0:T(8,128)(2,1)S(1)}, bf16[5,256,256]{2,1,0:T(8,128)(2,1)S(1)}, bf16[1024,256]{1,0:T(8,128)(2,1)S(1)}, f32[64,1024]{1,0:T(8,128)S(1)}) custom-call(s32[1]{0:T(128)} %bitcast.index_ref, f32[256,256]{1,0:T(8,128)S(1)} %copy-done.5, bf16[16384,256]{1,0:T(8,128)(2,1)} %load_hbm.5, f32[1,16384]{1,0:T(1,128)S(1)} %bitcast.10, ...), custom_call_target="tpu_custom_call" | custom-call | flops 402653184 | bytes 3145728 | tf_op jit(solution)/shard_map/prepared/pallas_call | solution.py:445
  38.6 0.0 collective-permute-done.7
  38.6 0.2 filtered.1
  38.9 11.2 %all_to_all.10.gathered_ref = f32[16,4,256]{2,1,0:T(4,128)S(1)} all-to-all(f32[16,4,256]{2,1,0:T(4,128)S(1)} %broadcast_in_dim.24), channel_id=1, replica_groups=mesh['spec'=2,'tm'=16] {'tm'}, dimensions={0} | all-to-all | bytes 131072 | tf_op jit(solution)/shard_map/all_to_all | solution.py:562
  50.1 0.0 copy-done
  50.1 2.1 %finish.1 = (f32[4,256]{1,0:T(4,128)}, bf16[64,1024]{1,0:T(8,128)(2,1)}) custom-call(s32[1]{0:T(128)} %bitcast.index_ref, f32[16,4,256]{2,1,0:T(4,128)S(1)} %all_to_all.10.gathered_ref, bf16[5,256,256]{2,1,0:T(8,128)(2,1)S(1)} %get-tuple-element.48.high_ref, bf16[5,256,256]{2,1,0:T(8,128)(2,1)S(1)} %get-tuple-element.49.low_ref, ...), custom_call_target="tpu_custom_call" | custom-call | flops 33554432 | bytes 2097152 | tf_op jit(solution)/shard_map/finish/pallas_call | solution.py:505
  (3 shorter events, 0.0 us)
Async XLA Ops:
  0.6 9.6 %copy-start.4 = (s32[16384]{0:T(1024)S(1)}, s32[16384]{0:T(1024)}, u32[]{:S(2)}) copy-start(s32[16384]{0:T(1024)} %param.14) | copy-start | bytes 196612
  0.6 9.6 %copy-start.3 = (s32[16384]{0:T(1024)S(1)}, s32[16384]{0:T(1024)}, u32[]{:S(2)}) copy-start(s32[16384]{0:T(1024)} %param.13) | copy-start | bytes 196612
  0.7 9.6 %copy-start.2 = (s32[16384]{0:T(1024)S(1)}, s32[16384]{0:T(1024)}, u32[]{:S(2)}) copy-start(s32[16384]{0:T(1024)} %param.12) | copy-start | bytes 196612
  0.7 9.6 %copy-start.1 = (f32[16384]{0:T(1024)S(1)}, f32[16384]{0:T(1024)}, u32[]{:S(2)}) copy-start(f32[16384]{0:T(1024)} %param.11) | copy-start | bytes 196612
  0.7 9.6 %copy-start.6 = (f32[256]{0:T(256)S(1)}, f32[256]{0:T(256)}, u32[]{:S(2)}) copy-start(f32[256]{0:T(256)} %param.15) | copy-start | bytes 3076
  2.8 18.1 %all-to-all-start = ((f32[16,4,256]{2,1,0:T(4,128)}), f32[16,4,256]{2,1,0:T(4,128)S(1)}, u32[]{:S(2)}, u32[]{:S(2)}) async-start(f32[16,4,256]{2,1,0:T(4,128)} %partial_drive.1), calls=%async_computation | async-start | bytes 131072 | tf_op jit(solution)/shard_map/all_to_all | solution.py:535
  10.3 10.6 %copy-start.7 = (bf16[256,256]{1,0:T(8,128)(2,1)S(1)}, bf16[256,256]{1,0:T(8,128)(2,1)}, u32[]{:S(2)}) copy-start(bf16[256,256]{1,0:T(8,128)(2,1)} %gain_ref.1) | copy-start | bytes 393220
  10.3 26.7 %copy-start.5 = (f32[256,256]{1,0:T(8,128)S(1)}, f32[256,256]{1,0:T(8,128)}, u32[]{:S(2)}) copy-start(f32[256,256]{1,0:T(8,128)} %in_ref) | copy-start | bytes 786436
  20.9 29.2 %copy-start = (bf16[64,1024]{1,0:T(8,128)(2,1)S(1)}, bf16[64,1024]{1,0:T(8,128)(2,1)}, u32[]{:S(2)}) copy-start(bf16[64,1024]{1,0:T(8,128)(2,1)} %series_ref.1) | copy-start | bytes 393220
  22.3 1.5 %collective-permute-start = (bf16[272,256]{1,0:T(8,128)(2,1)S(1)}, bf16[272,256]{1,0:T(8,128)(2,1)S(1)}, u32[]{:S(2)}, u32[]{:S(2)}) collective-permute-start(bf16[272,256]{1,0:T(8,128)(2,1)S(1)} %get-tuple-element.31), channel_id=1, source_target_pairs={{0,1},{1,0},{2,3},{3,2},{4,5},{5,4},{6,7},{7,6},{8,9},{9,8},{10,11... | collective-permute-start | bytes 417800 | tf_op jit(solution)/shard_map/ppermute | solution.py:531
  24.0 5.8 %collective-permute-start.5 = (bf16[144,256]{1,0:T(8,128)(2,1)S(1)}, bf16[144,256]{1,0:T(8,128)(2,1)S(1)}, u32[]{:S(2)}, u32[]{:S(2)}) collective-permute-start(bf16[144,256]{1,0:T(8,128)(2,1)S(1)} %get-tuple-element.32.refs_0_), channel_id=1, source_target_pairs={{0,6},{1,7},{2,4},{3,5},{4,2},{5,3},{6,0},{7,1},{8,14},{9,15},{10,... | collective-permute-start | bytes 221192 | tf_op jit(solution)/shard_map/ppermute | solution.py:531
  26.9 4.5 %collective-permute-start.3 = (bf16[144,256]{1,0:T(8,128)(2,1)S(1)}, bf16[144,256]{1,0:T(8,128)(2,1)S(1)}, u32[]{:S(2)}, u32[]{:S(2)}) collective-permute-start(bf16[144,256]{1,0:T(8,128)(2,1)S(1)} %get-tuple-element.32.refs_0_), channel_id=1, source_target_pairs={{0,4},{1,5},{2,6},{3,7},{4,0},{5,1},{6,2},{7,3},{8,12},{9,13},{10,... | collective-permute-start | bytes 221192 | tf_op jit(solution)/shard_map/ppermute | solution.py:531
  27.4 4.4 %collective-permute-start.1 = (bf16[144,256]{1,0:T(8,128)(2,1)S(1)}, bf16[144,256]{1,0:T(8,128)(2,1)S(1)}, u32[]{:S(2)}, u32[]{:S(2)}) collective-permute-start(bf16[144,256]{1,0:T(8,128)(2,1)S(1)} %get-tuple-element.32.refs_0_), channel_id=1, source_target_pairs={{0,2},{1,3},{2,0},{3,1},{4,6},{5,7},{6,4},{7,5},{8,10},{9,11},{10,... | collective-permute-start | bytes 221192 | tf_op jit(solution)/shard_map/ppermute | solution.py:531
  29.8 2.1 %collective-permute-start.6 = (bf16[144,256]{1,0:T(8,128)(2,1)S(1)}, bf16[144,256]{1,0:T(8,128)(2,1)S(1)}, u32[]{:S(2)}, u32[]{:S(2)}) collective-permute-start(bf16[144,256]{1,0:T(8,128)(2,1)S(1)} %collective-permute-done.5.refs_6_), channel_id=1, source_target_pairs={{0,1},{1,0},{2,3},{3,2},{4,5},{5,4},{6,7},{7,6},{8,9},{9,8},{10,11... | collective-permute-start | bytes 221192 | tf_op jit(solution)/shard_map/ppermute | solution.py:531
  31.4 1.3 %collective-permute-start.4 = (bf16[144,256]{1,0:T(8,128)(2,1)S(1)}, bf16[144,256]{1,0:T(8,128)(2,1)S(1)}, u32[]{:S(2)}, u32[]{:S(2)}) collective-permute-start(bf16[144,256]{1,0:T(8,128)(2,1)S(1)} %collective-permute-done.3.refs_4_), channel_id=1, source_target_pairs={{0,1},{1,0},{2,3},{3,2},{4,5},{5,4},{6,7},{7,6},{8,9},{9,8},{10,11... | collective-permute-start | bytes 221192 | tf_op jit(solution)/shard_map/ppermute | solution.py:531
  31.8 1.3 %collective-permute-start.2 = (bf16[144,256]{1,0:T(8,128)(2,1)S(1)}, bf16[144,256]{1,0:T(8,128)(2,1)S(1)}, u32[]{:S(2)}, u32[]{:S(2)}) collective-permute-start(bf16[144,256]{1,0:T(8,128)(2,1)S(1)} %collective-permute-done.1.refs_2_), channel_id=1, source_target_pairs={{0,1},{1,0},{2,3},{3,2},{4,5},{5,4},{6,7},{7,6},{8,9},{9,8},{10,11... | collective-permute-start | bytes 221192 | tf_op jit(solution)/shard_map/ppermute | solution.py:531
  33.5 5.1 %collective-permute-start.7 = (f32[1,256]{1,0:T(1,128)S(1)}, f32[1,256]{1,0:T(1,128)S(1)}, u32[]{:S(2)}, u32[]{:S(2)}) collective-permute-start(f32[1,256]{1,0:T(1,128)S(1)} %advanced.1), channel_id=1, source_target_pairs={{0,8},{1,9},{2,10},{3,11},{4,12},{5,13},{6,14},{7,15},{8,0},{9,1},... | collective-permute-start | bytes 3080 | tf_op jit(solution)/shard_map/ppermute | solution.py:531
